TPU v7x, 32 devices: a whole 2x2x4 slice. The times are simulated.
32 devices in a mesh: grp: 2 (over y), row: 16 (over z, x, core), col: 1.
Axes of the slice: x: 2, y: 2, z: 4, core: 2. Of those that a mesh axis runs over, the one named last changes fastest.
Arguments:
- alignment_state: bfloat16 [64, 128, 64], P(('grp', 'row'), 'col'), parts along dimension 0, may hold values from -6 to 6
- pair_state: bfloat16 [256, 128, 128], P(('grp', 'row'), 'col'), parts along dimension 0, may hold values from -6 to 6
- cotangent: bfloat16 [256, 128, 128], P(('grp', 'row'), 'col'), parts along dimension 0, may hold values from -0.046875 to 0.046875
- sequence_row_mask: int32 [64], P('grp'), parts along dimension 0, may hold values 0 or 1
- residue_mask: int32 [256], P('grp'), parts along dimension 0, may hold values 0 or 1
- norm_gain_vector: float32 [64], replicated, may hold values from 0.1 to 1.9
- left_matrix_weight: bfloat16 [64, 32], replicated, may hold values from -3 to 3
- right_matrix_weight: bfloat16 [64, 32], replicated, may hold values from -3 to 3
- output_weight: bfloat16 [1024, 128], replicated, may hold values from -0.1875 to 0.1875
- output_bias: float32 [128], replicated, may hold values from -4 to 4
- gate_matrix: bfloat16 [128, 128], replicated, may hold values from -0.5 to 0.5
Outputs:
- pair_update: bfloat16 [256, 128, 128], P(('grp', 'row'), 'col'), parts along dimension 0
- grad_left: float32 [128, 32], P('grp'), parts along dimension 0
- grad_right: float32 [128, 32], P('grp'), parts along dimension 0
- grad_out: float32 [2048, 128], P('grp'), parts along dimension 0
- grad_gate: float32 [256, 128], P('grp'), parts along dimension 0
There are 2 independent parts, one for each index of `grp`. A program takes and returns all parts, laid end to end along the dimension named above; an argument that names none is the same for every part. Nothing has to cross between parts.
All inputs are finite; a program needn't handle non-finite values.
Results may differ from a plain program's by a relative error of at most 0.0076.
Values may be sent and summed in bfloat16 or wider, within the bound.
No kernel may reach another device: no remote copies, remote signals or barrier semaphores. Data moves between devices by JAX's collectives and lax.ppermute only.
A program may use at most 64 MiB of HBM per device.

v0:
```python
import jax
import jax.numpy as jnp
from jax import lax
from jax.sharding import PartitionSpec as P


def layer_normalize(alignment_state, norm_gain_vector):
    value_entries = alignment_state.astype(jnp.float32)
    average = jnp.mean(value_entries, axis=-1, keepdims=True)
    centred = value_entries - average
    variance = jnp.mean(centred * centred, axis=-1, keepdims=True)
    return (centred * lax.rsqrt(variance + 1e-05) * norm_gain_vector).astype(jnp.bfloat16)


def per_device(
    alignment_state,
    pair_state,
    cotangent,
    sequence_row_mask,
    residue_mask,
    norm_gain_vector,
    left_matrix_weight,
    right_matrix_weight,
    output_weight,
    output_bias,
    gate_matrix,
):
    sequence_resident, column_count, alignment_channel_count = alignment_state.shape
    count_of_rows = pair_state.shape[0]
    pair_chans = pair_state.shape[2]
    projection_width = left_matrix_weight.shape[1]
    every_sequence = sequence_row_mask.shape[0]
    row_at = lax.axis_index("row")
    col_at = lax.axis_index("col")
    number_of_rows = lax.axis_size("row")
    contract_first = (((0,), (0,)), ((), ()))
    contract_second = (((1,), (1,)), ((), ()))
    resident_features = layer_normalize(alignment_state, norm_gain_vector)
    seq_flags = sequence_row_mask.astype(jnp.float32)
    res_flags = residue_mask.astype(jnp.float32)
    my_cols = lax.dynamic_slice_in_dim(res_flags, col_at * column_count, column_count, 0)
    my_rows = lax.dynamic_slice_in_dim(res_flags, row_at * count_of_rows, count_of_rows, 0)
    panel_mask = seq_flags[:, None] * my_rows[None, :]
    column_mask = seq_flags[:, None] * my_cols[None, :]
    broadcast_features = lax.all_gather(
        resident_features.reshape(sequence_resident, column_count * alignment_channel_count),
        "col",
        axis=1,
        tiled=True,
    )
    row_portions = broadcast_features.reshape(
        sequence_resident, number_of_rows, count_of_rows * alignment_channel_count
    )
    row_feats = lax.all_to_all(
        row_portions, "row", split_axis=1, concat_axis=0, tiled=True
    ).reshape(every_sequence * count_of_rows, alignment_channel_count)
    left_panel = (
        jnp.dot(row_feats, left_matrix_weight, preferred_element_type=jnp.float32).reshape(
            every_sequence, count_of_rows, projection_width
        )
        * panel_mask[:, :, None]
    ).astype(jnp.bfloat16)
    left_matrix = left_panel.transpose(1, 2, 0).reshape(
        count_of_rows * projection_width, every_sequence
    )
    column_features = lax.all_gather(
        resident_features.reshape(sequence_resident, column_count * alignment_channel_count),
        "row",
        axis=0,
        tiled=True,
    ).reshape(every_sequence, column_count, alignment_channel_count)
    right_panel = (
        jnp.dot(
            column_features.reshape(every_sequence * column_count, alignment_channel_count),
            right_matrix_weight,
            preferred_element_type=jnp.float32,
        ).reshape(every_sequence, column_count, projection_width)
        * column_mask[:, :, None]
    ).astype(jnp.bfloat16)
    surplus_offset = jnp.zeros((alignment_channel_count, projection_width), jnp.float32)

    def absorb(extra, first_col, width_columns, right_part):
        feat_blk = (
            lax.dynamic_slice_in_dim(column_features, first_col, width_columns, 1)
            .reshape(every_sequence * width_columns, alignment_channel_count)
            .astype(jnp.float32)
        )
        mask_blk = lax.dynamic_slice_in_dim(column_mask, first_col, width_columns, 1)
        masked_part = (
            right_part.reshape(every_sequence, width_columns, projection_width)
            * mask_blk[:, :, None]
        ).reshape(every_sequence * width_columns, projection_width)
        return extra + jnp.dot(feat_blk.T, masked_part, precision=lax.Precision.HIGHEST)

    right_flat = right_panel.reshape(every_sequence, column_count * projection_width)
    row_total = jnp.sum(seq_flags)
    col_block = 128
    n_blocks = column_count // col_block

    def one_block(block_idx, carry):
        new_update, grad_out, grad_gate, left_acc, extra = carry
        first_col = block_idx * col_block
        right_blk = lax.dynamic_slice_in_dim(
            right_flat, first_col * projection_width, col_block * projection_width, 1
        )
        outer_prod = jnp.dot(left_matrix, right_blk, preferred_element_type=jnp.float32)
        outer_prod = outer_prod.reshape(
            count_of_rows, projection_width, col_block, projection_width
        ).transpose(0, 2, 1, 3)
        outer_prod = outer_prod.reshape(
            count_of_rows * col_block, projection_width * projection_width
        ).astype(jnp.bfloat16)
        linear = (
            jnp.dot(outer_prod, output_weight, preferred_element_type=jnp.float32) + output_bias
        )
        pair_blk = lax.dynamic_slice_in_dim(pair_state, first_col, col_block, 1).reshape(
            count_of_rows * col_block, pair_chans
        )
        gate_val = jax.nn.sigmoid(
            jnp.dot(pair_blk, gate_matrix, preferred_element_type=jnp.float32)
        )
        blk_flags = lax.dynamic_slice_in_dim(my_cols, first_col, col_block, 0)
        divisor = jnp.maximum(row_total * my_rows[:, None] * blk_flags[None, :], 1.0).reshape(
            count_of_rows * col_block, 1
        )
        cot_blk = (
            lax.dynamic_slice_in_dim(cotangent, first_col, col_block, 1)
            .reshape(count_of_rows * col_block, pair_chans)
            .astype(jnp.float32)
        )
        new_pair = (gate_val * linear / divisor).astype(jnp.bfloat16)
        new_update = lax.dynamic_update_slice_in_dim(
            new_update, new_pair.reshape(count_of_rows, col_block, pair_chans), first_col, 1
        )
        grad_lin = (cot_blk * gate_val / divisor).astype(jnp.bfloat16)
        grad_pre = (cot_blk * linear / divisor * gate_val * (1.0 - gate_val)).astype(jnp.bfloat16)
        grad_out = grad_out + lax.dot_general(
            outer_prod, grad_lin, contract_first, preferred_element_type=jnp.float32
        )
        grad_gate = grad_gate + lax.dot_general(
            pair_blk, grad_pre, contract_first, preferred_element_type=jnp.float32
        )
        grad_outer = lax.dot_general(
            grad_lin, output_weight, contract_second, preferred_element_type=jnp.float32
        ).astype(jnp.bfloat16)
        outer_turned = (
            grad_outer.reshape(count_of_rows, col_block, projection_width, projection_width)
            .transpose(0, 2, 1, 3)
            .reshape(count_of_rows * projection_width, col_block * projection_width)
        )
        left_acc = left_acc + lax.dot_general(
            outer_turned, right_blk, contract_second, preferred_element_type=jnp.float32
        )
        right_part = lax.dot_general(
            left_matrix, outer_turned, contract_first, preferred_element_type=jnp.float32
        )
        extra = absorb(extra, first_col, col_block, right_part)
        return (new_update, grad_out, grad_gate, left_acc, extra)

    start_carry = (
        jnp.zeros((count_of_rows, column_count, pair_chans), jnp.bfloat16),
        jnp.zeros((projection_width * projection_width, pair_chans), jnp.float32),
        jnp.zeros((pair_chans, pair_chans), jnp.float32),
        jnp.zeros((count_of_rows * projection_width, every_sequence), jnp.float32),
        surplus_offset,
    )
    new_update, grad_out, grad_gate, left_acc, extra = lax.fori_loop(
        0, n_blocks, one_block, start_carry
    )
    grad_left_act = (
        left_acc.reshape(count_of_rows, projection_width, every_sequence).transpose(2, 0, 1)
        * panel_mask[:, :, None]
    )
    grad_left = jnp.dot(
        row_feats.astype(jnp.float32).T,
        grad_left_act.reshape(every_sequence * count_of_rows, projection_width),
        precision=lax.Precision.HIGHEST,
    )
    summed_left, summed_right, summed_out, summed_gate = lax.psum(
        (grad_left, extra, grad_out, grad_gate), ("row", "col")
    )
    return (new_update, summed_left, summed_right, summed_out, summed_gate)


def solution(mesh):
    return jax.shard_map(
        per_device,
        mesh=mesh,
        in_specs=(
            P(("grp", "row"), "col", None),
            P(("grp", "row"), "col", None),
            P(("grp", "row"), "col", None),
            P("grp"),
            P("grp"),
            P(),
            P(),
            P(),
            P(),
            P(),
            P(),
        ),
        out_specs=(
            P(("grp", "row"), "col", None),
            P("grp", None),
            P("grp", None),
            P("grp", None),
            P("grp", None),
        ),
        check_vma=False,
    )
```

profile of v0, /device:TPU:0, one launch (start us, length us, event | category | flops | bytes accessed | tf_op | source)
XLA Modules:
  0.0 186.8 jit_solution(15133442757585819444)
XLA Ops:
  7.2 0.8 convert_reduce_fusion
  8.0 0.8 fusion.43
  8.8 0.8 fusion.45
  10.6 7.4 %all-to-all-start = ((bf16[2,16,512]{2,0,1:T(2,128)(2,1)}), bf16[2,16,512]{2,0,1:T(2,128)(2,1)S(1)}, u32[]{:S(2)}, u32[]{:S(2)}) async-start(bf16[2,16,512]{2,0,1:T(2,128)(2,1)} %copy.43), calls=%async_computation | async-start | bytes 65536 | tf_op jit(solution)/shard_map/all_to_all | solution.py:54
  18.0 1.3 convert_reduce_fusion.1
  22.2 23.3 %all-gather = bf16[16,2,8192]{2,1,0:T(2,128)(2,1)S(1)} all-gather(bf16[1,2,8192]{2,1,0:T(2,128)(2,1)S(1)} %reshape.191), channel_id=1, replica_groups=mesh['grp'=2,'row'=16,'col'=1] {'row'}, dimensions={0}, use_global_device_ids=true | all-gather | bytes 557056 | tf_op jit(solution)/shard_map/all_gather | solution.py:66
  47.8 1.1 reshape.181
  49.0 0.8 dot_general.68
  51.5 1.4 copy.50
  53.9 1.3 fusion.34
  55.2 1.5 fusion
  58.1 1.9 %convolution_bitcast_fusion.1 = f32[128,128]{0,1:T(8,128)} fusion(bf16[1024,128]{1,0:T(8,128)(2,1)} %get-tuple-element.83, bf16[1024,128]{1,0:T(8,128)(2,1)} %bitcast.106), kind=kOutput, calls=%fused_computation.24 | convolution fusion | flops 33554432 | bytes 589824 | tf_op jit(solution)/shard_map/while/body/eval_jaxpr/dot_general | solution.py:140
  60.0 2.6 %copy.51 = bf16[1024,1024]{0,1:T(8,128)(2,1)} copy(bf16[1024,1024]{1,0:T(8,128)(2,1)S(1)} %convolution_convert_fusion) | data formatting | bytes 4194304 | tf_op jit(solution)/shard_map/while/body/eval_jaxpr/convert_element_type | solution.py:145
  62.6 2.2 %copy.69 = bf16[128,8,8,128]{3,2,1,0:T(8,128)(2,1)S(1)} copy(bf16[128,8,8,128]{3,1,2,0:T(8,128)(2,1)} %bitcast.100) | data formatting | bytes 4194304
  64.8 6.0 %copy.56 = bf16[8,32,128,32]{3,2,1,0:T(8,128)(2,1)} copy(bf16[8,32,128,32]{2,0,3,1:T(8,128)(2,1)S(1)} %bitcast.96) | data formatting | bytes 4194304 | tf_op jit(solution)/shard_map/while/body/eval_jaxpr/transpose | solution.py:148
  70.8 3.3 %fusion.21 = f32[32,8,32]{2,0,1:T(8,128)} fusion(bf16[8,32,128,32]{2,0,3,1:T(8,128)(2,1)S(1)} %bitcast.97, bf16[32,128,32]{1,2,0:T(8,128)(2,1)} %copy-done.1, f32[32,8]{0,1:T(8,128)S(1)} %copy-done.7), kind=kOutput, calls=%fused_computation.22 | convolution fusion | flops 67117056 | bytes 2393088 | tf_op jit(solution)/shard_map/while/body/eval_jaxpr/dot_general | solution.py:151
  74.2 10.7 %reshape.188 = bf16[256,4096]{1,0:T(8,128)(2,1)S(1)} reshape(bf16[8,32,128,32]{3,2,1,0:T(8,128)(2,1)} %copy.56) | data formatting | bytes 4194304 | tf_op jit(solution)/shard_map/while/body/eval_jaxpr/reshape | solution.py:149
  84.8 2.5 %copy.57 = bf16[4096,256]{1,0:T(8,128)(2,1)} copy(bf16[4096,256]{0,1:T(8,128)(2,1)S(1)} %bitcast.98) | data formatting | bytes 4194304 | tf_op jit(solution)/shard_map/while/body/eval_jaxpr/dot_general | solution.py:154
  87.4 4.0 %fusion.4 = f32[32,128,32]{1,0,2:T(8,128)S(1)} fusion(bf16[256,32,1]{0,1,2:T(8,128)(2,1)S(1)} %copy-done.4, bf16[128,32,256]{2,1,0:T(8,128)(2,1)} %bitcast.99), kind=kOutput, calls=%fused_computation.4 | convolution fusion | flops 67108864 | bytes 2637824 | tf_op jit(solution)/shard_map/while/body/eval_jaxpr/dot_general | solution.py:154
  91.7 0.8 fusion.30
  92.5 58.5 %all-reduce = (f32[64,32]{0,1:T(8,128)}, f32[64,32]{0,1:T(8,128)}) all-reduce(f32[64,32]{0,1:T(8,128)S(1)} %fusion.38, f32[64,32]{0,1:T(8,128)S(1)} %fusion.30), channel_id=1, replica_groups=mesh['grp'=2,'row'=16,'col'=1] {'row','col'}, use_global_device_ids=true, to_apply=%region_3.0 | all-reduce | flops 4096 | bytes 32768 | tf_op jit(solution)/shard_map/psum | solution.py:179
  151.0 25.5 %all-reduce.4.cloned.1.call-done = (f32[1024,128]{1,0:T(8,128)}, f32[128,128]{0,1:T(8,128)}) async-done(((f32[1024,128]{1,0:T(8,128)}, f32[128,128]{0,1:T(8,128)}), (f32[1024,128]{1,0:T(8,128)}, f32[128,128]{0,1:T(8,128)})) %all-reduce.4.cloned.1.call-update) | async-done | bytes 589840 | tf_op jit(solution)/shard_map/psum | solution.py:179
  176.5 1.6 copy.61
  178.1 1.9 copy.109
  (52 shorter events, 10.7 us)
Async XLA Ops:
  7.2 45.7 %copy-start = (bf16[1024,128]{1,0:T(8,128)(2,1)S(1)}, bf16[1024,128]{1,0:T(8,128)(2,1)}, u32[]{:S(2)}) copy-start(bf16[1024,128]{1,0:T(8,128)(2,1)} %param.19) | copy-start | bytes 786436
  7.2 39.0 %copy-start.5 = (bf16[64,32]{0,1:T(8,128)(2,1)S(1)}, bf16[64,32]{0,1:T(8,128)(2,1)}, u32[]{:S(2)}) copy-start(bf16[64,32]{0,1:T(8,128)(2,1)} %param.18) | copy-start | bytes 12292
  10.6 39.8 %all-to-all-start = ((bf16[2,16,512]{2,0,1:T(2,128)(2,1)}), bf16[2,16,512]{2,0,1:T(2,128)(2,1)S(1)}, u32[]{:S(2)}, u32[]{:S(2)}) async-start(bf16[2,16,512]{2,0,1:T(2,128)(2,1)} %copy.43), calls=%async_computation | async-start | bytes 65536 | tf_op jit(solution)/shard_map/all_to_all | solution.py:54
  17.9 158.6 %all-reduce.4.cloned.1.call-start = ((), (), s32[]{:S(2)}) async-start(), calls=%async_computation.1 | async-start | bytes 1179648 | tf_op jit(solution)/shard_map/psum | solution.py:179
  46.6 2.4 %copy-start.1 = (bf16[32,128,32]{1,2,0:T(8,128)(2,1)}, bf16[32,128,32]{1,2,0:T(8,128)(2,1)S(1)}, u32[]{:S(2)}) copy-start(bf16[32,128,32]{1,2,0:T(8,128)(2,1)S(1)} %fusion.16) | copy-start | bytes 786436
  47.8 2.7 %copy-start.6 = (bf16[64,32]{0,1:T(8,128)(2,1)S(1)}, bf16[64,32]{0,1:T(8,128)(2,1)}, u32[]{:S(2)}) copy-start(bf16[64,32]{0,1:T(8,128)(2,1)} %param.17) | copy-start | bytes 12292
  51.5 1.4 copy-start.10
  52.9 1.0 copy-start.2
  52.9 1.0 copy-start.8
  52.9 1.0 copy-start.9
  64.8 6.0 %copy-start.7 = (f32[32,8]{0,1:T(8,128)S(1)}, f32[32,8]{0,1:T(8,128)}, u32[]{:S(2)}) copy-start(f32[32,8]{0,1:T(8,128)} %broadcast_multiply_fusion.1) | copy-start | bytes 3076
  84.8 2.5 %copy-start.4 = (bf16[256,32,1]{0,1,2:T(8,128)(2,1)S(1)}, bf16[256,32,1]{0,1,2:T(8,128)(2,1)}, u32[]{:S(2)}) copy-start(bf16[256,32,1]{0,1,2:T(8,128)(2,1)} %reshape.202) | copy-start | bytes 49156
  87.3 4.0 %copy-start.3 = (f32[32,8,32]{2,0,1:T(8,128)S(1)}, f32[32,8,32]{2,0,1:T(8,128)}, u32[]{:S(2)}) copy-start(f32[32,8,32]{2,0,1:T(8,128)} %fusion.21) | copy-start | bytes 98308
Sparse Core Ops, SparseCore 0:
  87.5 88.9 all-reduce.3
where the time goes:
time: 188 us; the launch traced here: 187 us
  blocking collectives  81.7 us (43%)
  local copies, waits for them, and re-layouts  35.2 us (19%)
  waiting for transfers between devices  25.5 us (14%)
  matrix products  16 us (9%)
  between operations  14.3 us (8%)
  starting transfers between devices  7.4 us (4%)
  other arithmetic  6.65 us (4%)
    psum x1, blocking collectives, per_device(): lax.psum((grad_left, extra, grad_out, grad_gate), ('row', 'col'))  58.5 us
    psum x1, waiting for transfers between devices, per_device(): lax.psum((grad_left, extra, grad_out, grad_gate), ('row', 'col'))  25.5 us
    all_gather x1, blocking collectives, per_device(): lax.all_gather(resident_features.reshape(sequence_resident, column_count...  23.3 us
    reshape x1, local copies, waits for them, and re-layouts, one_block(): outer_turned = grad_outer.reshape(count_of_rows, col_block, projection_wi...  10.7 us
    all_to_all x1, starting transfers between devices, per_device(): lax.all_to_all(row_portions, 'row', split_axis=1, concat_axis=0, tiled=True)  7.36 us
    unnamed x26, local copies, waits for them, and re-layouts  6.04 us
    transpose x1, local copies, waits for them, and re-layouts, one_block(): outer_turned = grad_outer.reshape(count_of_rows, col_block, projection_wi...  6 us
    dot_general x1, matrix products, one_block(): lax.dot_general(left_matrix, outer_turned, contract_first, preferred_elem...  3.98 us
  transfers between devices with their start and end apart: 2, of which 1 were waited for; matrix products, arithmetic and copies ran while one was open for 8% of the time, Pallas kernels for 0%

commit v1 on v0

--- a/solution.py
+++ b/solution.py
@@ -1,7 +1,317 @@
+import functools
+
 import jax
 import jax.numpy as jnp
 from jax import lax
+from jax.experimental import pallas as pl
+from jax.experimental.pallas import tpu as pltpu
 from jax.sharding import PartitionSpec as P
+
+F32 = jnp.float32
+BF16 = jnp.bfloat16
+VMEM = pl.BlockSpec(memory_space=pltpu.VMEM)
+SMEM = pl.BlockSpec(memory_space=pltpu.SMEM)
+LHS_T = (((0,), (0,)), ((), ()))
+RHS_T = (((1,), (1,)), ((), ()))
+QUAD = 4
+CHANS = 32
+GROUP = 16
+
+
+def iota(shape, dim):
+    return lax.broadcasted_iota(jnp.int32, shape, dim)
+
+
+def dot(a, b, dims=(((1,), (0,)), ((), ())), **kw):
+    return lax.dot_general(a, b, dims, preferred_element_type=F32, **kw)
+
+
+def norm_kernel(seq_ref, state_ref, res_ref, gain_ref, out_ref):
+    first = lax.axis_index("row") * 2
+    res = res_ref[...].astype(F32)
+    halves = []
+    for s in range(2):
+        value = state_ref[s].astype(F32)
+        centred = value - jnp.mean(value, axis=0, keepdims=True)
+        variance = jnp.mean(centred * centred, axis=0, keepdims=True)
+        seq = seq_ref[first + s].astype(F32)
+        halves.append(centred * (lax.rsqrt(variance + 1e-05) * (res * seq)))
+    turned = jnp.concatenate(halves, axis=0).T
+    gain = gain_ref[...]
+    out_ref[...] = (turned * jnp.concatenate([gain, gain], axis=1)).astype(BF16)
+
+
+def gate_kernel(
+    res_s_ref, seq_ref, res_ref, pair_ref, cot_ref, gate_ref,
+    scale_ref, slope_ref, full_ref, own_ref, core_ref, across_ref, both_ref,
+):
+    row = lax.axis_index("row")
+    quad_at = lax.rem(row, QUAD)
+    rows = pair_ref.shape[0]
+    n = res_ref.shape[1]
+    total = jnp.sum(seq_ref[...].astype(F32), axis=1, keepdims=True)
+    eye = iota((n, n), 0) == iota((n, n), 1)
+    res_col = jnp.sum(jnp.where(eye, res_ref[...].astype(F32), 0.0), axis=1, keepdims=True)
+    wide = QUAD * n
+    src = iota((wide, wide), 0)
+    dst = iota((wide, wide), 1)
+    slot = dst // n
+    chan = (quad_at ^ slot) * CHANS + dst % CHANS
+    place = jnp.where(
+        (src // n == (dst % n) // CHANS) & (src % n == chan), 1.0, 0.0
+    ).astype(BF16)
+    outs = (own_ref, core_ref, across_ref, both_ref)
+    for half in range(rows // QUAD):
+        for k in range(QUAD):
+            i = half * QUAD + k
+            gate = jax.nn.sigmoid(dot(pair_ref[i], gate_ref[...]))
+            res_row = res_s_ref[row * rows + i].astype(F32)
+            scale = gate / jnp.maximum(total * res_row * res_col, 1.0)
+            lin = cot_ref[i].astype(F32) * scale
+            scale_ref[i] = scale
+            slope_ref[i] = lin * (1.0 - gate)
+            full_ref[:, i * n : (i + 1) * n] = lin.astype(BF16)
+        packed = dot(full_ref[:, half * wide : (half + 1) * wide], place).astype(BF16)
+        for m in range(QUAD):
+            outs[m][:, half * n : (half + 1) * n] = packed[:, m * n : (m + 1) * n]
+
+
+def weight_kernel(
+    right_ref, left_ref, out_w_ref,
+    kron_ref, block_ref, wide_ref, part_ref, wf_ref,
+):
+    quad_at = lax.rem(lax.axis_index("row"), QUAD)
+    width, chans = right_ref.shape
+    n = out_w_ref.shape[1]
+    cols = width * GROUP
+    spread = jnp.where(iota((width, cols), 0) == iota((width, cols), 1) // GROUP, 1.0, 0.0)
+    repeated = dot(right_ref[...], spread.astype(BF16), LHS_T)
+    lane = iota((chans, cols), 1) % GROUP
+    for s in range(GROUP):
+        kron_ref[s * chans : (s + 1) * chans, :] = jnp.where(lane == s, repeated, 0.0).astype(BF16)
+    spread = jnp.where(iota((width, n), 0) == iota((width, n), 1) % width, 1.0, 0.0)
+    repeated = dot(left_ref[...], spread.astype(BF16), LHS_T)
+    lane = iota((chans, n), 1) // width
+    for k in range(QUAD):
+        block_ref[k * chans : (k + 1) * chans, :] = jnp.where(lane == k, repeated, 0.0).astype(BF16)
+    wf_ref[...] = out_w_ref[...].astype(F32)
+    for e in range(width):
+        wide_ref[:, e * n : (e + 1) * n] = wf_ref[pl.ds(e, width, stride=width), :].astype(BF16)
+    pick = jnp.where(
+        iota((n, n), 0) == quad_at * CHANS + iota((n, n), 1) % CHANS, 1.0, 0.0
+    ).astype(BF16)
+    wf_ref[...] = dot(out_w_ref[...], pick)
+    lane = iota((width, n), 1) // CHANS
+    for e in range(width):
+        tile = wf_ref[pl.ds(e, width, stride=width), :]
+        part_ref[:, e * n : (e + 1) * n] = jnp.concatenate(
+            [jnp.where(lane == k, tile, 0.0) for k in range(QUAD)], axis=0
+        ).astype(BF16)
+
+
+def main_kernel(
+    y0_ref, y1_ref, y2_ref, y3_ref, g0_ref, g1_ref, g2_ref, g3_ref,
+    full_ref, scale_ref, slope_ref, pair_ref, bias_ref,
+    kron_ref, block_ref, wide_ref, part_ref,
+    update_ref, sums_ref,
+    r_ref, m_ref, n_ref, turn_ref, own_ref, slope_s_ref,
+):
+    row = lax.axis_index("row")
+    quad_at = lax.rem(row, QUAD)
+    first = (row - quad_at) * 8
+    rows, n, _ = pair_ref.shape
+    chans = 64
+    width = 32
+    cols = width * GROUP
+    seqs = 2 * GROUP
+    ys = (y0_ref, y1_ref, y2_ref, y3_ref)
+    slots = [y[t * n : (t + 1) * n, :] for y in ys for t in range(4)]
+    feats = [jnp.concatenate(slots[g * 8 : (g + 1) * 8], axis=1) for g in range(2)]
+    for g in range(2):
+        r_ref[:, g * cols : (g + 1) * cols] = dot(feats[g], kron_ref[...]).astype(BF16)
+    at = iota((32, n), 0)
+    four = at % 8
+    here = first + (quad_at ^ (four // 2)) * 8 + (four % 2) * QUAD + at // 8
+    pick = jnp.where(iota((32, n), 1) == here, 1.0, 0.0).astype(BF16)
+    for t, slot in enumerate(slots):
+        picked = dot(pick, slot)
+        for s in range(2):
+            at = (2 * t + s) * 8
+            for half in range(2):
+                turn_ref[half, at : at + 8, :] = jnp.concatenate(
+                    [
+                        picked[k * 8 : (k + 1) * 8, s * chans : (s + 1) * chans]
+                        for k in (2 * half, 2 * half + 1)
+                    ],
+                    axis=1,
+                )
+    for f in range(8):
+        for half in range(2):
+            own_ref[f * seqs : (f + 1) * seqs, half * n : (half + 1) * n] = turn_ref[
+                half, pl.ds(f, seqs, stride=8), :
+            ].astype(BF16)
+    left = dot(own_ref[...], block_ref[...])
+    left_b = left.astype(BF16)
+    mine = jnp.concatenate(
+        [
+            left[f * seqs : (f + 1) * seqs, k * width : (k + 1) * width]
+            for f in range(2)
+            for k in range(QUAD)
+        ],
+        axis=0,
+    ).astype(BF16)
+    for e4 in range(width // 4):
+        part = dot(mine, wide_ref[:, e4 * 4 * n : (e4 + 1) * 4 * n]).astype(BF16)
+        for el in range(4):
+            e = e4 * 4 + el
+            for i in range(rows):
+                for g in range(2):
+                    m_ref[g * cols + e * GROUP : g * cols + (e + 1) * GROUP, i * n : (i + 1) * n] = (
+                        part[i * seqs + g * GROUP : i * seqs + (g + 1) * GROUP, el * n : (el + 1) * n]
+                    )
+    for f2, g_ref in enumerate((g0_ref, g1_ref, g2_ref, g3_ref)):
+        part = dot(r_ref[...], g_ref[...], LHS_T).astype(BF16)
+        for fl in range(2):
+            f = f2 * 2 + fl
+            for g in range(2):
+                for e in range(width):
+                    n_ref[f * seqs + g * GROUP : f * seqs + (g + 1) * GROUP, e * n : (e + 1) * n] = (
+                        part[g * cols + e * GROUP : g * cols + (e + 1) * GROUP, fl * n : (fl + 1) * n]
+                    )
+    lane = iota((width, n), 1) // CHANS
+    for h in range(width // 4):
+        whole = dot(left_b, n_ref[:, h * 4 * n : (h + 1) * 4 * n], LHS_T)
+        packed = None
+        for el in range(4):
+            tile = None
+            for k in range(QUAD):
+                block = whole[k * width : (k + 1) * width, el * n : (el + 1) * n]
+                tile = block if tile is None else jnp.where(lane == k, block, tile)
+            tile = tile + pltpu.roll(tile, 2 * CHANS, 1)
+            tile = tile + pltpu.roll(tile, CHANS, 1)
+            packed = tile if packed is None else jnp.where(lane == el, tile, packed)
+        sums_ref[h * width : (h + 1) * width, :] = packed.astype(BF16)
+    linear = dot(r_ref[...], m_ref[...])
+    for i in range(rows):
+        value = linear[:, i * n : (i + 1) * n] + bias_ref[...]
+        update_ref[i] = (scale_ref[i] * value).astype(BF16)
+        slope_s_ref[i * n : (i + 1) * n, :] = (slope_ref[i] * value).astype(BF16)
+    grad_gate = dot(pair_ref[...].reshape(rows * n, n), slope_s_ref[...], LHS_T)
+    sums_ref[256:384, :] = grad_gate.astype(BF16)
+    left_act = dot(n_ref[...], part_ref[...], RHS_T).astype(BF16)
+    whole = dot(left_act, own_ref[...], LHS_T)
+    grad_left = whole[0:width, 0:chans]
+    for k in range(1, QUAD):
+        grad_left = grad_left + whole[k * width : (k + 1) * width, k * chans : (k + 1) * chans]
+    right_act = dot(full_ref[...], m_ref[...], RHS_T).astype(BF16)
+    whole = dot(feats[0], right_act[:, :cols], LHS_T) + dot(feats[1], right_act[:, cols:], LHS_T)
+    lane = iota((chans, cols), 1) % GROUP
+    tile = whole[0:chans, :]
+    for s in range(1, GROUP):
+        tile = jnp.where(lane == s, whole[s * chans : (s + 1) * chans, :], tile)
+    spread = jnp.where(iota((width, cols), 0) == iota((width, cols), 1) // GROUP, 1.0, 0.0)
+    grad_right = dot(spread, tile, RHS_T, precision=lax.Precision.HIGHEST)
+    sums_ref[384:416, :] = jnp.concatenate([grad_left, grad_right], axis=1).astype(BF16)
+
+
+def last_kernel(t0_ref, t1_ref, t2_ref, t3_ref, out_ref, gate_ref, left_ref, right_ref):
+    quad_at = lax.rem(lax.axis_index("row"), QUAD)
+    n = t0_ref.shape[1]
+    ts = (t0_ref, t1_ref, t2_ref, t3_ref)
+    wide = QUAD * n
+    src = iota((wide, wide), 0)
+    dst = iota((wide, wide), 1)
+    chan = (quad_at ^ (src // n)) * CHANS + src % CHANS
+    place = jnp.where(
+        (dst // n == (src % n) // CHANS) & (dst % n == chan), 1.0, 0.0
+    ).astype(BF16)
+    packed = jnp.concatenate([t[0:256, :] for t in ts], axis=1)
+    whole = dot(packed, place)
+    for h in range(8):
+        for el in range(4):
+            out_ref[pl.ds(h * 4 + el, 32, stride=32), :] = whole[
+                h * 32 : (h + 1) * 32, el * n : (el + 1) * n
+            ]
+
+    def total(lo, hi):
+        a, b, c, d = (t[lo:hi, :].astype(F32) for t in ts)
+        return (a + b) + (c + d)
+
+    gate_ref[...] = total(256, 384)
+    both = total(384, 416)
+    left_ref[...] = both[:, 0:64]
+    right_ref[...] = both[:, 64:128]
+
+
+def call(kernel, shapes, scratch=(), smem=0, ins=0, flops=1 << 20):
+    return pl.pallas_call(
+        kernel,
+        out_shape=[jax.ShapeDtypeStruct(s, d) for s, d in shapes],
+        in_specs=[SMEM] * smem + [VMEM] * (ins - smem),
+        out_specs=[VMEM] * len(shapes),
+        scratch_shapes=[pltpu.VMEM(s, d) for s, d in scratch],
+        compiler_params=pltpu.CompilerParams(vmem_limit_bytes=48 << 20),
+        cost_estimate=pl.CostEstimate(flops=flops, bytes_accessed=1 << 20, transcendentals=0),
+    )
+
+
+def swap(x, bit, size):
+    return lax.ppermute(x, "row", [(i, i ^ bit) for i in range(size)])
+
+
+def one_column(
+    alignment_state, pair_state, cotangent, sequence_row_mask, residue_mask, norm_gain_vector,
+    left_matrix_weight, right_matrix_weight, output_weight, output_bias, gate_matrix,
+):
+    size = lax.axis_size("row")
+    rows, n, _ = pair_state.shape
+    res = residue_mask.reshape(1, n)
+    seq = sequence_row_mask.reshape(1, -1)
+    (feat,) = call(norm_kernel, [((n, n), BF16)], smem=1, ins=4)(
+        sequence_row_mask, alignment_state.transpose(0, 2, 1), res, norm_gain_vector.reshape(1, -1)
+    )
+    near = swap(feat, 4, size)
+    scale, slope, full, g0, g1, g2, g3 = call(
+        gate_kernel,
+        [((rows, n, n), F32), ((rows, n, n), F32), ((n, rows * n), BF16)] + [((n, 2 * n), BF16)] * 4,
+        smem=1, ins=6, flops=300 << 20,
+    )(residue_mask, seq, res, pair_state, cotangent, gate_matrix)
+    g1 = swap(g1, 1, size)
+    g2 = swap(g2, 2, size)
+    g3 = swap(g3, 3, size)
+    kron, block, wide, part = call(
+        weight_kernel,
+        [((1024, 512), BF16), ((256, n), BF16), ((32, 32 * n), BF16), ((n, 32 * n), BF16)],
+        scratch=[((1024, n), F32)], ins=3, flops=300 << 20,
+    )(right_matrix_weight.T, left_matrix_weight.T, output_weight)
+    y0 = jnp.concatenate([feat, near], axis=0)
+    y0 = jnp.concatenate([y0, swap(y0, 8, size)], axis=0)
+    y1 = swap(y0, 2, size)
+    y2 = swap(y0, 1, size)
+    y3 = swap(y1, 1, size)
+    update, sums = call(
+        main_kernel,
+        [((rows, n, n), BF16), ((416, n), BF16)],
+        scratch=[
+            ((n, 1024), BF16), ((1024, rows * n), BF16), ((256, 32 * n), BF16),
+            ((2, 256, n), F32), ((256, 256), BF16), ((rows * n, n), BF16),
+        ],
+        ins=17, flops=2000 << 20,
+    )(
+        y0, y1, y2, y3, g0, g1, g2, g3, full, scale, slope, pair_state,
+        output_bias.reshape(1, n), kron, block, wide, part,
+    )
+    sums = sums + swap(sums, 4, size)
+    sums = sums + swap(sums, 8, size)
+    across = swap(sums, 2, size)
+    core = swap(sums, 1, size)
+    both = swap(across, 1, size)
+    grad_out, grad_gate, left, right = call(
+        last_kernel,
+        [((1024, n), F32), ((n, n), F32), ((32, 64), F32), ((32, 64), F32)],
+        ins=4,
+    )(sums, core, across, both)
+    return update, left.T, right.T, grad_out, grad_gate
 
 
 def layer_normalize(alignment_state, norm_gain_vector):
@@ -12,7 +322,7 @@
     return (centred * lax.rsqrt(variance + 1e-05) * norm_gain_vector).astype(jnp.bfloat16)
 
 
-def per_device(
+def any_mesh(
     alignment_state,
     pair_state,
     cotangent,
@@ -182,6 +492,17 @@
     return (new_update, summed_left, summed_right, summed_out, summed_gate)
 
 
+def per_device(*args):
+    alignment_state, pair_state = args[0], args[1]
+    fits = (
+        lax.axis_size("col") == 1
+        and lax.axis_size("row") == 16
+        and alignment_state.shape == (2, 128, 64)
+        and pair_state.shape == (8, 128, 128)
+    )
+    return one_column(*args) if fits else any_mesh(*args)
+
+
 def solution(mesh):
     return jax.shard_map(
         per_device,

time: 188 us -> 55.7 us (0.30)
  blocking collectives: 81.7 us -> 0 us
  local copies, waits for them, and re-layouts: 35.2 us -> 3.04 us
  matrix products: 16 us -> 0 us
  between operations: 14.3 us -> 0.77 us
  Pallas kernels: 0 us -> 11.8 us
  starting transfers between devices: 7.4 us -> 16.6 us
  other arithmetic: 6.65 us -> 0.08 us
  waiting for transfers between devices: 25.5 us -> 23.3 us
    psum x1 -> x0, blocking collectives: 58.5 us -> none  [per_device(): lax.psum((grad_left, extra, grad_out, grad_gate), ('row', 'col'))]
    psum x1 -> x0, waiting for transfers between devices: 25.5 us -> none  [per_device(): lax.psum((grad_left, extra, grad_out, grad_gate), ('row', 'col'))]
    ppermute x0 -> x13, waiting for transfers between devices: none -> 23.3 us  [swap(): return lax.ppermute(x, 'row', [(i, i ^ bit) for i in range(size)])]
    all_gather x1 -> x0, blocking collectives: 23.3 us -> none  [per_device(): lax.all_gather(resident_features.reshape(sequence_resident, column_count...]
    ppermute x0 -> x13, starting transfers between devices: none -> 16.6 us  [swap(): return lax.ppermute(x, 'row', [(i, i ^ bit) for i in range(size)])]
    dot_general x12 -> x0, matrix products: 16 us -> none  [the longest x1 3.98 us: one_block(): lax.dot_general(left_matrix, outer_turned, contract_first, preferred_elem...]
    reshape x7 -> x0, local copies, waits for them, and re-layouts: 14 us -> none  [the longest x1 10.7 us: one_block(): outer_turned = grad_outer.reshape(count_of_rows, col_block, projection_wi...]
    pallas_call x0 -> x5, Pallas kernels: none -> 11.8 us  [the longest x1 7.04 us: one_column(): call(main_kernel, [((rows, n, n), BF16), ((416, n), BF16)], scratch=[((n,...]
  transfers between devices with their start and end apart: 2 -> 13, of which waited for: 1 -> 9; matrix products, arithmetic and copies ran while one was open for 8% -> 0% of each run, Pallas kernels for 0% -> 5%
where the time goes in v1:
time: 55.7 us; the launch traced here: 55.5 us
  waiting for transfers between devices  23.3 us (42%)
  starting transfers between devices  16.6 us (30%)
  Pallas kernels  11.8 us (21%)
  local copies, waits for them, and re-layouts  3.04 us (5%)
  between operations  0.77 us (1%)
    ppermute x13, waiting for transfers between devices, swap(): return lax.ppermute(x, 'row', [(i, i ^ bit) for i in range(size)])  23.3 us
    ppermute x13, starting transfers between devices, swap(): return lax.ppermute(x, 'row', [(i, i ^ bit) for i in range(size)])  16.6 us
    pallas_call x1, Pallas kernels, one_column(): call(main_kernel, [((rows, n, n), BF16), ((416, n), BF16)], scratch=[((n,...  7.04 us
    unnamed x24, local copies, waits for them, and re-layouts  3.04 us
    pallas_call x1, Pallas kernels, one_column(): call(last_kernel, [((1024, n), F32), ((n, n), F32), ((32, 64), F32), ((32...  1.4 us
    pallas_call x1, Pallas kernels, one_column(): call(weight_kernel, [((1024, 512), BF16), ((256, n), BF16), ((32, 32 * n)...  1.33 us
    pallas_call x1, Pallas kernels, one_column(): call(gate_kernel, [((rows, n, n), F32), ((rows, n, n), F32), ((n, rows *...  1.3 us
  transfers between devices with their start and end apart: 13, of which 9 were waited for; matrix products, arithmetic and copies ran while one was open for 0% of the time, Pallas kernels for 5%

profile of v1, /device:TPU:0, one launch (start us, length us, event | category | flops | bytes accessed | tf_op | source)
XLA Modules:
  0.0 55.5 jit_solution(15772305690969631466)
XLA Ops:
  1.3 0.8 %copy-done = bf16[2,128,64]{1,2,0:T(8,128)(2,1)S(1)} copy-done((bf16[2,128,64]{1,2,0:T(8,128)(2,1)S(1)}, bf16[2,128,64]{1,2,0:T(8,128)(2,1)}, u32[]{:S(2)}) %copy-start) | copy-done | bytes 32792
  2.1 0.7 %shard_map.146 = bf16[128,128]{1,0:T(8,128)(2,1)S(1)} custom-call(s32[32]{0:T(128)S(1)} %copy-done.2, bf16[2,64,128]{2,1,0:T(8,128)(2,1)S(1)} %bitcast.9, s32[1,128]{1,0:T(1,128)S(1)} %bitcast.12, f32[1,64]{1,0:T(1,128)S(1)} %bitcast.10), custom_call_target="tpu_custom_call" | custom-call | flops 1048576 | bytes 1048576 | tf_op jit(solution)/shard_map/pallas_call | solution.py:270
  2.8 3.1 %collective-permute-start = (bf16[128,128]{1,0:T(8,128)(2,1)S(1)}, bf16[128,128]{1,0:T(8,128)(2,1)S(1)}, u32[]{:S(2)}, u32[]{:S(2)}) collective-permute-start(bf16[128,128]{1,0:T(8,128)(2,1)S(1)} %shard_map.146), channel_id=1, source_target_pairs={{0,4},{1,5},{2,6},{3,7},{4,0},{5,1},{6,2},{7,3},{8,12},{9,13},{10,... | collective-permute-start | bytes 98312 | tf_op jit(solution)/shard_map/ppermute | solution.py:259
  5.9 1.9 %collective-permute-done = bf16[128,128]{1,0:T(8,128)(2,1)S(1)} collective-permute-done((bf16[128,128]{1,0:T(8,128)(2,1)S(1)}, bf16[128,128]{1,0:T(8,128)(2,1)S(1)}, u32[]{:S(2)}, u32[]{:S(2)}) %collective-permute-start) | collective-permute-done | bytes 32800 | tf_op jit(solution)/shard_map/ppermute | solution.py:259
  7.8 3.1 %collective-permute-start.1 = (bf16[256,128]{1,0:T(8,128)(2,1)S(1)}, bf16[256,128]{1,0:T(8,128)(2,1)S(1)}, u32[]{:S(2)}, u32[]{:S(2)}) collective-permute-start(bf16[256,128]{1,0:T(8,128)(2,1)S(1)} %pad_maximum_fusion.1), channel_id=1, source_target_pairs={{0,8},{1,9},{2,10},{3,11},{4,12},{5,13},{6,14},{7,15},{8,0},{9,1},... | collective-permute-start | bytes 196616 | tf_op jit(solution)/shard_map/ppermute | solution.py:259
  10.9 2.2 %collective-permute-done.1 = bf16[256,128]{1,0:T(8,128)(2,1)S(1)} collective-permute-done((bf16[256,128]{1,0:T(8,128)(2,1)S(1)}, bf16[256,128]{1,0:T(8,128)(2,1)S(1)}, u32[]{:S(2)}, u32[]{:S(2)}) %collective-permute-start.1) | collective-permute-done | bytes 65568 | tf_op jit(solution)/shard_map/ppermute | solution.py:259
  13.1 1.9 %collective-permute-start.2 = (bf16[512,128]{1,0:T(8,128)(2,1)S(1)}, bf16[512,128]{1,0:T(8,128)(2,1)S(1)}, u32[]{:S(2)}, u32[]{:S(2)}) collective-permute-start(bf16[512,128]{1,0:T(8,128)(2,1)S(1)} %pad_maximum_fusion.y0_ref), channel_id=1, source_target_pairs={{0,2},{1,3},{2,0},{3,1},{4,6},{5,7},{6,4},{7,5},{8,10},{9,11},{10,... | collective-permute-start | bytes 393224 | tf_op jit(solution)/shard_map/ppermute | solution.py:259
  15.0 3.1 %collective-permute-done.2.y1_ref = bf16[512,128]{1,0:T(8,128)(2,1)S(1)} collective-permute-done((bf16[512,128]{1,0:T(8,128)(2,1)S(1)}, bf16[512,128]{1,0:T(8,128)(2,1)S(1)}, u32[]{:S(2)}, u32[]{:S(2)}) %collective-permute-start.2) | collective-permute-done | bytes 131104 | tf_op jit(solution)/shard_map/ppermute | solution.py:259
  18.2 0.9 %copy-done.6 = bf16[8,128,128]{2,1,0:T(8,128)(2,1)S(1)} copy-done((bf16[8,128,128]{2,1,0:T(8,128)(2,1)S(1)}, bf16[8,128,128]{2,1,0:T(8,128)(2,1)}, u32[]{:S(2)}) %copy-start.6) | copy-done | bytes 262168
  19.1 1.3 %shard_map.147 = (f32[8,128,128]{2,1,0:T(8,128)S(1)}, f32[8,128,128]{2,1,0:T(8,128)S(1)}, bf16[128,1024]{1,0:T(8,128)(2,1)S(1)}, bf16[128,256]{1,0:T(8,128)(2,1)...) custom-call(s32[128]{0:T(128)S(1)} %copy-done.3, ...), custom_call_target="tpu_custom_call" | custom-call | flops 314572800 | bytes 1048576 | tf_op jit(solution)/shard_map/pallas_call | solution.py:274
  21.0 1.8 %collective-permute-start.6 = (bf16[128,256]{1,0:T(8,128)(2,1)S(1)}, bf16[128,256]{1,0:T(8,128)(2,1)S(1)}, u32[]{:S(2)}, u32[]{:S(2)}) collective-permute-start(bf16[128,256]{1,0:T(8,128)(2,1)S(1)} %get-tuple-element.24), channel_id=1, source_target_pairs={{0,2},{1,3},{2,0},{3,1},{4,6},{5,7},{6,4},{7,5},{8,10},{9,11},{10,... | collective-permute-start | bytes 196616 | tf_op jit(solution)/shard_map/ppermute | solution.py:259
  22.9 1.3 %shard_map.148 = (bf16[1024,512]{1,0:T(8,128)(2,1)S(1)}, bf16[256,128]{1,0:T(8,128)(2,1)S(1)}, bf16[32,4096]{1,0:T(8,128)(2,1)S(1)}, bf16[128,4096]{1,0:T(8,128)(2,1)S(1)}) custom-call(bf16[32,64]{1,0:T(8,128)(2,1)S(1)} %bitcast.14, bf16[32,64]{1,0:T(8,128)(2,1)S(1)} %bitcast.15, bf16[1024,128]{1,0:T(8,128)(2,1)S(1)} %copy-done.5), custom_call_target="tpu_custom_call" | custom-call | flops 314572800 | bytes 1048576 | tf_op jit(solution)/shard_map/pallas_call | solution.py:282
  24.2 1.1 %collective-permute-done.6.g2_ref = bf16[128,256]{1,0:T(8,128)(2,1)S(1)} collective-permute-done((bf16[128,256]{1,0:T(8,128)(2,1)S(1)}, bf16[128,256]{1,0:T(8,128)(2,1)S(1)}, u32[]{:S(2)}, u32[]{:S(2)}) %collective-permute-start.6) | collective-permute-done | bytes 65568 | tf_op jit(solution)/shard_map/ppermute | solution.py:259
  25.3 1.9 %collective-permute-done.7.g3_ref = bf16[128,256]{1,0:T(8,128)(2,1)S(1)} collective-permute-done((bf16[128,256]{1,0:T(8,128)(2,1)S(1)}, bf16[128,256]{1,0:T(8,128)(2,1)S(1)}, u32[]{:S(2)}, u32[]{:S(2)}) %collective-permute-start.7) | collective-permute-done | bytes 65568 | tf_op jit(solution)/shard_map/ppermute | solution.py:259
  27.2 0.6 %copy-done.11 = f32[128]{0:T(128)S(1)} copy-done((f32[128]{0:T(128)S(1)}, f32[128]{0:T(128)}, u32[]{:S(2)}) %copy-start.11) | copy-done | bytes 536
  27.9 7.0 %shard_map.149 = (bf16[8,128,128]{2,1,0:T(8,128)(2,1)}, bf16[416,128]{1,0:T(8,128)(2,1)S(1)}) custom-call(bf16[512,128]{1,0:T(8,128)(2,1)S(1)} %pad_maximum_fusion.y0_ref, bf16[512,128]{1,0:T(8,128)(2,1)S(1)} %collective-permute-done.2.y1_ref, bf16[512,128]{1,0:T(8,128)(2,1)S(1)} %collective-permute-done.3.y2_ref, ...), custom_call_target="tpu_custom_call" | custom-call | flops 2097152000 | bytes 1048576 | tf_op jit(solution)/shard_map/pallas_call | solution.py:292
  34.9 1.6 %collective-permute-start.8 = (bf16[416,128]{1,0:T(8,128)(2,1)S(1)}, bf16[416,128]{1,0:T(8,128)(2,1)S(1)}, u32[]{:S(2)}, u32[]{:S(2)}) collective-permute-start(bf16[416,128]{1,0:T(8,128)(2,1)S(1)} %get-tuple-element.34), channel_id=1, source_target_pairs={{0,4},{1,5},{2,6},{3,7},{4,0},{5,1},{6,2},{7,3},{8,12},{9,13},{10,... | collective-permute-start | bytes 319496 | tf_op jit(solution)/shard_map/ppermute | solution.py:259
  36.5 3.4 %collective-permute-done.8 = bf16[416,128]{1,0:T(8,128)(2,1)S(1)} collective-permute-done((bf16[416,128]{1,0:T(8,128)(2,1)S(1)}, bf16[416,128]{1,0:T(8,128)(2,1)S(1)}, u32[]{:S(2)}, u32[]{:S(2)}) %collective-permute-start.8) | collective-permute-done | bytes 106528 | tf_op jit(solution)/shard_map/ppermute | solution.py:259
  39.9 3.1 %collective-permute-start.9 = (bf16[416,128]{1,0:T(8,128)(2,1)S(1)}, bf16[416,128]{1,0:T(8,128)(2,1)S(1)}, u32[]{:S(2)}, u32[]{:S(2)}) collective-permute-start(bf16[416,128]{1,0:T(8,128)(2,1)S(1)} %add.6), channel_id=1, source_target_pairs={{0,8},{1,9},{2,10},{3,11},{4,12},{5,13},{6,14},{7,15},{8,0},{9,1},... | collective-permute-start | bytes 319496 | tf_op jit(solution)/shard_map/ppermute | solution.py:259
  43.0 5.0 %collective-permute-done.9 = bf16[416,128]{1,0:T(8,128)(2,1)S(1)} collective-permute-done((bf16[416,128]{1,0:T(8,128)(2,1)S(1)}, bf16[416,128]{1,0:T(8,128)(2,1)S(1)}, u32[]{:S(2)}, u32[]{:S(2)}) %collective-permute-start.9) | collective-permute-done | bytes 106528 | tf_op jit(solution)/shard_map/ppermute | solution.py:259
  48.0 1.4 %collective-permute-start.11 = (bf16[416,128]{1,0:T(8,128)(2,1)S(1)}, bf16[416,128]{1,0:T(8,128)(2,1)S(1)}, u32[]{:S(2)}, u32[]{:S(2)}) collective-permute-start(bf16[416,128]{1,0:T(8,128)(2,1)S(1)} %add.7.t0_ref), channel_id=1, source_target_pairs={{0,2},{1,3},{2,0},{3,1},{4,6},{5,7},{6,4},{7,5},{8,10},{9,11},{10,... | collective-permute-start | bytes 319496 | tf_op jit(solution)/shard_map/ppermute | solution.py:259
  49.4 3.3 %collective-permute-done.11.t2_ref = bf16[416,128]{1,0:T(8,128)(2,1)S(1)} collective-permute-done((bf16[416,128]{1,0:T(8,128)(2,1)S(1)}, bf16[416,128]{1,0:T(8,128)(2,1)S(1)}, u32[]{:S(2)}, u32[]{:S(2)}) %collective-permute-start.11) | collective-permute-done | bytes 106528 | tf_op jit(solution)/shard_map/ppermute | solution.py:259
  52.8 1.3 %collective-permute-done.12.t3_ref = bf16[416,128]{1,0:T(8,128)(2,1)S(1)} collective-permute-done((bf16[416,128]{1,0:T(8,128)(2,1)S(1)}, bf16[416,128]{1,0:T(8,128)(2,1)S(1)}, u32[]{:S(2)}, u32[]{:S(2)}) %collective-permute-start.12) | collective-permute-done | bytes 106528 | tf_op jit(solution)/shard_map/ppermute | solution.py:259
  54.1 1.4 %shard_map.150 = (f32[1024,128]{1,0:T(8,128)}, f32[128,128]{1,0:T(8,128)}, f32[32,64]{1,0:T(8,128)}, f32[32,64]{1,0:T(8,128)}) custom-call(bf16[416,128]{1,0:T(8,128)(2,1)S(1)} %add.7.t0_ref, bf16[416,128]{1,0:T(8,128)(2,1)S(1)} %collective-permute-done.10.t1_ref, bf16[416,128]{1,0:T(8,128)(2,1)S(1)} %collective-permute-done.11.t2_ref, ...), custom_call_target="tpu_custom_call" | custom-call | flops 1048576 | bytes 1048576 | tf_op jit(solution)/shard_map/pallas_call | solution.py:309
  (35 shorter events, 1.4 us)
Async XLA Ops:
  0.6 0.7 %copy-start.2 = (s32[32]{0:T(128)S(1)}, s32[32]{0:T(128)}, u32[]{:S(2)}) copy-start(s32[32]{0:T(128)} %seq_ref.1) | copy-start | bytes 388
  0.7 0.7 %copy-start.3 = (s32[128]{0:T(128)S(1)}, s32[128]{0:T(128)}, u32[]{:S(2)}) copy-start(s32[128]{0:T(128)} %res_s_ref.1) | copy-start | bytes 1540
  1.3 0.8 %copy-start = (bf16[2,128,64]{1,2,0:T(8,128)(2,1)S(1)}, bf16[2,128,64]{1,2,0:T(8,128)(2,1)}, u32[]{:S(2)}) copy-start(bf16[2,128,64]{1,2,0:T(8,128)(2,1)} %param.11) | copy-start | bytes 98308
  2.1 16.1 %copy-start.4 = (bf16[8,128,128]{2,1,0:T(8,128)(2,1)S(1)}, bf16[8,128,128]{2,1,0:T(8,128)(2,1)}, u32[]{:S(2)}) copy-start(bf16[8,128,128]{2,1,0:T(8,128)(2,1)} %cot_ref.1) | copy-start | bytes 786436
  2.8 5.0 %collective-permute-start = (bf16[128,128]{1,0:T(8,128)(2,1)S(1)}, bf16[128,128]{1,0:T(8,128)(2,1)S(1)}, u32[]{:S(2)}, u32[]{:S(2)}) collective-permute-start(bf16[128,128]{1,0:T(8,128)(2,1)S(1)} %shard_map.146), channel_id=1, source_target_pairs={{0,4},{1,5},{2,6},{3,7},{4,0},{5,1},{6,2},{7,3},{8,12},{9,13},{10,... | collective-permute-start | bytes 98312 | tf_op jit(solution)/shard_map/ppermute | solution.py:259
  7.8 10.4 %copy-start.8 = (bf16[128,128]{1,0:T(8,128)(2,1)S(1)}, bf16[128,128]{1,0:T(8,128)(2,1)}, u32[]{:S(2)}) copy-start(bf16[128,128]{1,0:T(8,128)(2,1)} %gate_ref.1) | copy-start | bytes 98308
  7.8 5.3 %collective-permute-start.1 = (bf16[256,128]{1,0:T(8,128)(2,1)S(1)}, bf16[256,128]{1,0:T(8,128)(2,1)S(1)}, u32[]{:S(2)}, u32[]{:S(2)}) collective-permute-start(bf16[256,128]{1,0:T(8,128)(2,1)S(1)} %pad_maximum_fusion.1), channel_id=1, source_target_pairs={{0,8},{1,9},{2,10},{3,11},{4,12},{5,13},{6,14},{7,15},{8,0},{9,1},... | collective-permute-start | bytes 196616 | tf_op jit(solution)/shard_map/ppermute | solution.py:259
  13.1 5.0 %collective-permute-start.2 = (bf16[512,128]{1,0:T(8,128)(2,1)S(1)}, bf16[512,128]{1,0:T(8,128)(2,1)S(1)}, u32[]{:S(2)}, u32[]{:S(2)}) collective-permute-start(bf16[512,128]{1,0:T(8,128)(2,1)S(1)} %pad_maximum_fusion.y0_ref), channel_id=1, source_target_pairs={{0,2},{1,3},{2,0},{3,1},{4,6},{5,7},{6,4},{7,5},{8,10},{9,11},{10,... | collective-permute-start | bytes 393224 | tf_op jit(solution)/shard_map/ppermute | solution.py:259
  15.0 12.2 %collective-permute-start.3 = (bf16[512,128]{1,0:T(8,128)(2,1)S(1)}, bf16[512,128]{1,0:T(8,128)(2,1)S(1)}, u32[]{:S(2)}, u32[]{:S(2)}) collective-permute-start(bf16[512,128]{1,0:T(8,128)(2,1)S(1)} %pad_maximum_fusion.y0_ref), channel_id=1, source_target_pairs={{0,1},{1,0},{2,3},{3,2},{4,5},{5,4},{6,7},{7,6},{8,9},{9,8},{10,11... | collective-permute-start | bytes 393224 | tf_op jit(solution)/shard_map/ppermute | solution.py:259
  18.1 9.1 %collective-permute-start.4 = (bf16[512,128]{1,0:T(8,128)(2,1)S(1)}, bf16[512,128]{1,0:T(8,128)(2,1)S(1)}, u32[]{:S(2)}, u32[]{:S(2)}) collective-permute-start(bf16[512,128]{1,0:T(8,128)(2,1)S(1)} %collective-permute-done.2.y1_ref), channel_id=1, source_target_pairs={{0,1},{1,0},{2,3},{3,2},{4,5},{5,4},{6,7},{7,6},{8,9},{9,8},{10,11... | collective-permute-start | bytes 393224 | tf_op jit(solution)/shard_map/ppermute | solution.py:259
  18.2 1.0 %copy-start.6 = (bf16[8,128,128]{2,1,0:T(8,128)(2,1)S(1)}, bf16[8,128,128]{2,1,0:T(8,128)(2,1)}, u32[]{:S(2)}) copy-start(bf16[8,128,128]{2,1,0:T(8,128)(2,1)} %pair_ref.3) | copy-start | bytes 786436
  19.1 3.7 %copy-start.5 = (bf16[1024,128]{1,0:T(8,128)(2,1)S(1)}, bf16[1024,128]{1,0:T(8,128)(2,1)}, u32[]{:S(2)}) copy-start(bf16[1024,128]{1,0:T(8,128)(2,1)} %out_w_ref.1) | copy-start | bytes 786436
  19.1 3.7 %copy-start.10 = (bf16[64,32]{0,1:T(8,128)(2,1)S(1)}, bf16[64,32]{0,1:T(8,128)(2,1)}, u32[]{:S(2)}) copy-start(bf16[64,32]{0,1:T(8,128)(2,1)} %param.17) | copy-start | bytes 12292
  20.4 2.4 %copy-start.9 = (bf16[64,32]{0,1:T(8,128)(2,1)S(1)}, bf16[64,32]{0,1:T(8,128)(2,1)}, u32[]{:S(2)}) copy-start(bf16[64,32]{0,1:T(8,128)(2,1)} %param.18) | copy-start | bytes 12292
  20.4 3.8 %collective-permute-start.5 = (bf16[128,256]{1,0:T(8,128)(2,1)S(1)}, bf16[128,256]{1,0:T(8,128)(2,1)S(1)}, u32[]{:S(2)}, u32[]{:S(2)}) collective-permute-start(bf16[128,256]{1,0:T(8,128)(2,1)S(1)} %get-tuple-element.23), channel_id=1, source_target_pairs={{0,1},{1,0},{2,3},{3,2},{4,5},{5,4},{6,7},{7,6},{8,9},{9,8},{10,11... | collective-permute-start | bytes 196616 | tf_op jit(solution)/shard_map/ppermute | solution.py:259
  21.0 4.3 %collective-permute-start.6 = (bf16[128,256]{1,0:T(8,128)(2,1)S(1)}, bf16[128,256]{1,0:T(8,128)(2,1)S(1)}, u32[]{:S(2)}, u32[]{:S(2)}) collective-permute-start(bf16[128,256]{1,0:T(8,128)(2,1)S(1)} %get-tuple-element.24), channel_id=1, source_target_pairs={{0,2},{1,3},{2,0},{3,1},{4,6},{5,7},{6,4},{7,5},{8,10},{9,11},{10,... | collective-permute-start | bytes 196616 | tf_op jit(solution)/shard_map/ppermute | solution.py:259
  22.8 4.4 %collective-permute-start.7 = (bf16[128,256]{1,0:T(8,128)(2,1)S(1)}, bf16[128,256]{1,0:T(8,128)(2,1)S(1)}, u32[]{:S(2)}, u32[]{:S(2)}) collective-permute-start(bf16[128,256]{1,0:T(8,128)(2,1)S(1)} %get-tuple-element.25), channel_id=1, source_target_pairs={{0,3},{1,2},{2,1},{3,0},{4,7},{5,6},{6,5},{7,4},{8,11},{9,10},{10,... | collective-permute-start | bytes 196616 | tf_op jit(solution)/shard_map/ppermute | solution.py:259
  22.9 4.4 %copy-start.7 = (bf16[8,128,128]{2,1,0:T(8,128)(2,1)S(1)}, bf16[8,128,128]{2,1,0:T(8,128)(2,1)}, u32[]{:S(2)}) copy-start(bf16[8,128,128]{2,1,0:T(8,128)(2,1)} %pair_ref.3) | copy-start | bytes 786436
  27.2 0.7 %copy-start.11 = (f32[128]{0:T(128)S(1)}, f32[128]{0:T(128)}, u32[]{:S(2)}) copy-start(f32[128]{0:T(128)} %param.20) | copy-start | bytes 1540
  34.9 5.0 %collective-permute-start.8 = (bf16[416,128]{1,0:T(8,128)(2,1)S(1)}, bf16[416,128]{1,0:T(8,128)(2,1)S(1)}, u32[]{:S(2)}, u32[]{:S(2)}) collective-permute-start(bf16[416,128]{1,0:T(8,128)(2,1)S(1)} %get-tuple-element.34), channel_id=1, source_target_pairs={{0,4},{1,5},{2,6},{3,7},{4,0},{5,1},{6,2},{7,3},{8,12},{9,13},{10,... | collective-permute-start | bytes 319496 | tf_op jit(solution)/shard_map/ppermute | solution.py:259
  39.9 8.1 %collective-permute-start.9 = (bf16[416,128]{1,0:T(8,128)(2,1)S(1)}, bf16[416,128]{1,0:T(8,128)(2,1)S(1)}, u32[]{:S(2)}, u32[]{:S(2)}) collective-permute-start(bf16[416,128]{1,0:T(8,128)(2,1)S(1)} %add.6), channel_id=1, source_target_pairs={{0,8},{1,9},{2,10},{3,11},{4,12},{5,13},{6,14},{7,15},{8,0},{9,1},... | collective-permute-start | bytes 319496 | tf_op jit(solution)/shard_map/ppermute | solution.py:259
  48.0 4.8 %collective-permute-start.11 = (bf16[416,128]{1,0:T(8,128)(2,1)S(1)}, bf16[416,128]{1,0:T(8,128)(2,1)S(1)}, u32[]{:S(2)}, u32[]{:S(2)}) collective-permute-start(bf16[416,128]{1,0:T(8,128)(2,1)S(1)} %add.7.t0_ref), channel_id=1, source_target_pairs={{0,2},{1,3},{2,0},{3,1},{4,6},{5,7},{6,4},{7,5},{8,10},{9,11},{10,... | collective-permute-start | bytes 319496 | tf_op jit(solution)/shard_map/ppermute | solution.py:259
  49.4 3.3 %collective-permute-start.10 = (bf16[416,128]{1,0:T(8,128)(2,1)S(1)}, bf16[416,128]{1,0:T(8,128)(2,1)S(1)}, u32[]{:S(2)}, u32[]{:S(2)}) collective-permute-start(bf16[416,128]{1,0:T(8,128)(2,1)S(1)} %add.7.t0_ref), channel_id=1, source_target_pairs={{0,1},{1,0},{2,3},{3,2},{4,5},{5,4},{6,7},{7,6},{8,9},{9,8},{10,11... | collective-permute-start | bytes 319496 | tf_op jit(solution)/shard_map/ppermute | solution.py:259
  52.8 1.3 %collective-permute-start.12 = (bf16[416,128]{1,0:T(8,128)(2,1)S(1)}, bf16[416,128]{1,0:T(8,128)(2,1)S(1)}, u32[]{:S(2)}, u32[]{:S(2)}) collective-permute-start(bf16[416,128]{1,0:T(8,128)(2,1)S(1)} %collective-permute-done.11.t2_ref), channel_id=1, source_target_pairs={{0,1},{1,0},{2,3},{3,2},{4,5},{5,4},{6,7},{7,6},{8,9},{9,8},{10,11... | collective-permute-start | bytes 319496 | tf_op jit(solution)/shard_map/ppermute | solution.py:259
  (1 other events, 0.7 us)

commit v2 on v1

--- a/solution.py
+++ b/solution.py
@@ -26,25 +26,35 @@
     return lax.dot_general(a, b, dims, preferred_element_type=F32, **kw)
 
 
-def norm_kernel(seq_ref, state_ref, res_ref, gain_ref, out_ref):
-    first = lax.axis_index("row") * 2
+def first_kernel(out_ref):
+    out_ref[...] = jnp.zeros_like(out_ref)
+
+
+def norm_kernel(seq_ref, res_ref, gain_ref, own_ref, near_ref, out_ref):
+    row = lax.axis_index("row")
+    n = res_ref.shape[1]
     res = res_ref[...].astype(F32)
-    halves = []
-    for s in range(2):
-        value = state_ref[s].astype(F32)
-        centred = value - jnp.mean(value, axis=0, keepdims=True)
-        variance = jnp.mean(centred * centred, axis=0, keepdims=True)
-        seq = seq_ref[first + s].astype(F32)
-        halves.append(centred * (lax.rsqrt(variance + 1e-05) * (res * seq)))
-    turned = jnp.concatenate(halves, axis=0).T
     gain = gain_ref[...]
-    out_ref[...] = (turned * jnp.concatenate([gain, gain], axis=1)).astype(BF16)
+    gain = jnp.concatenate([gain, gain], axis=1)
+    for at, (state_ref, first) in enumerate(((own_ref, row * 2), (near_ref, (row ^ 4) * 2))):
+        halves = []
+        for s in range(2):
+            value = state_ref[s].astype(F32)
+            centred = value - jnp.mean(value, axis=0, keepdims=True)
+            variance = jnp.mean(centred * centred, axis=0, keepdims=True)
+            seq = seq_ref[first + s].astype(F32)
+            halves.append(centred * (lax.rsqrt(variance + 1e-05) * (res * seq)))
+        turned = jnp.concatenate(halves, axis=0).T
+        out_ref[at * n : (at + 1) * n, :] = (turned * gain).astype(BF16)
 
 
 def gate_kernel(
-    res_s_ref, seq_ref, res_ref, pair_ref, cot_ref, gate_ref,
-    scale_ref, slope_ref, full_ref, own_ref, core_ref, across_ref, both_ref,
+    res_s_ref, seq_ref, res_ref, pair_ref, cot_ref, gate_ref, gain_ref, bias_ref, after_ref,
+    scale_ref, slope_ref, turned_ref, own_ref, core_ref, across_ref, both_ref, gain_out_ref, bias_out_ref,
+    full_ref,
 ):
+    gain_out_ref[...] = gain_ref[...]
+    bias_out_ref[...] = bias_ref[...]
     row = lax.axis_index("row")
     quad_at = lax.rem(row, QUAD)
     rows = pair_ref.shape[0]
@@ -71,13 +81,14 @@
             scale_ref[i] = scale
             slope_ref[i] = lin * (1.0 - gate)
             full_ref[:, i * n : (i + 1) * n] = lin.astype(BF16)
+            turned_ref[i * n : (i + 1) * n, :] = lin.T.astype(BF16)
         packed = dot(full_ref[:, half * wide : (half + 1) * wide], place).astype(BF16)
         for m in range(QUAD):
             outs[m][:, half * n : (half + 1) * n] = packed[:, m * n : (m + 1) * n]
 
 
 def weight_kernel(
-    right_ref, left_ref, out_w_ref,
+    right_ref, left_ref, out_w_ref, after_ref,
     kron_ref, block_ref, wide_ref, part_ref, wf_ref,
 ):
     quad_at = lax.rem(lax.axis_index("row"), QUAD)
@@ -102,33 +113,37 @@
     ).astype(BF16)
     wf_ref[...] = dot(out_w_ref[...], pick)
     lane = iota((width, n), 1) // CHANS
-    for e in range(width):
-        tile = wf_ref[pl.ds(e, width, stride=width), :]
-        part_ref[:, e * n : (e + 1) * n] = jnp.concatenate(
-            [jnp.where(lane == k, tile, 0.0) for k in range(QUAD)], axis=0
-        ).astype(BF16)
-
-
-def main_kernel(
-    y0_ref, y1_ref, y2_ref, y3_ref, g0_ref, g1_ref, g2_ref, g3_ref,
-    full_ref, scale_ref, slope_ref, pair_ref, bias_ref,
-    kron_ref, block_ref, wide_ref, part_ref,
-    update_ref, sums_ref,
-    r_ref, m_ref, n_ref, turn_ref, own_ref, slope_s_ref,
-):
+    for h in range(width // QUAD):
+        tile = None
+        for k in range(QUAD):
+            rows = wf_ref[pl.ds(h * QUAD + k, width, stride=width), :]
+            tile = rows if tile is None else jnp.where(lane == k, rows, tile)
+        part_ref[:, h * n : (h + 1) * n] = tile.astype(BF16)
+
+
+def fold(tiles, lane):
+    high, low = lane // 2 == 0, lane % 2 == 0
+    pairs = [
+        jnp.where(high, tiles[k], tiles[k + 2])
+        + pltpu.roll(jnp.where(high, tiles[k + 2], tiles[k]), 2 * CHANS, 1)
+        for k in range(2)
+    ]
+    other = jnp.where(low, pairs[1], pairs[0])
+    size = lane.shape[1]
+    other = jnp.where(low, pltpu.roll(other, size - CHANS, 1), pltpu.roll(other, CHANS, 1))
+    return jnp.where(low, pairs[0], pairs[1]) + other
+
+
+def half_of_rows(ys, gs, turned, kron_ref, block_ref, wide_ref, scratch):
+    m_ref, n_ref, turn_ref, own_ref, right_ref, flat_ref = scratch
     row = lax.axis_index("row")
     quad_at = lax.rem(row, QUAD)
     first = (row - quad_at) * 8
-    rows, n, _ = pair_ref.shape
-    chans = 64
-    width = 32
-    cols = width * GROUP
-    seqs = 2 * GROUP
-    ys = (y0_ref, y1_ref, y2_ref, y3_ref)
+    n = ys[0].shape[1]
+    chans, width = 64, 32
     slots = [y[t * n : (t + 1) * n, :] for y in ys for t in range(4)]
-    feats = [jnp.concatenate(slots[g * 8 : (g + 1) * 8], axis=1) for g in range(2)]
-    for g in range(2):
-        r_ref[:, g * cols : (g + 1) * cols] = dot(feats[g], kron_ref[...]).astype(BF16)
+    right = dot(jnp.concatenate(slots, axis=1), kron_ref[...]).astype(BF16)
+    right_t = right.T
     at = iota((32, n), 0)
     four = at % 8
     here = first + (quad_at ^ (four // 2)) * 8 + (four % 2) * QUAD + at // 8
@@ -147,14 +162,13 @@
                 )
     for f in range(8):
         for half in range(2):
-            own_ref[f * seqs : (f + 1) * seqs, half * n : (half + 1) * n] = turn_ref[
-                half, pl.ds(f, seqs, stride=8), :
+            own_ref[f * GROUP : (f + 1) * GROUP, half * n : (half + 1) * n] = turn_ref[
+                half, pl.ds(f, GROUP, stride=8), :
             ].astype(BF16)
-    left = dot(own_ref[...], block_ref[...])
-    left_b = left.astype(BF16)
+    left = dot(own_ref[0 : 2 * GROUP, :], block_ref[...])
     mine = jnp.concatenate(
         [
-            left[f * seqs : (f + 1) * seqs, k * width : (k + 1) * width]
+            left[f * GROUP : (f + 1) * GROUP, k * width : (k + 1) * width]
             for f in range(2)
             for k in range(QUAD)
         ],
@@ -164,53 +178,83 @@
         part = dot(mine, wide_ref[:, e4 * 4 * n : (e4 + 1) * 4 * n]).astype(BF16)
         for el in range(4):
             e = e4 * 4 + el
-            for i in range(rows):
-                for g in range(2):
-                    m_ref[g * cols + e * GROUP : g * cols + (e + 1) * GROUP, i * n : (i + 1) * n] = (
-                        part[i * seqs + g * GROUP : i * seqs + (g + 1) * GROUP, el * n : (el + 1) * n]
-                    )
-    for f2, g_ref in enumerate((g0_ref, g1_ref, g2_ref, g3_ref)):
-        part = dot(r_ref[...], g_ref[...], LHS_T).astype(BF16)
+            for i in range(8):
+                m_ref[e * GROUP : (e + 1) * GROUP, i * n : (i + 1) * n] = part[
+                    i * GROUP : (i + 1) * GROUP, el * n : (el + 1) * n
+                ]
+    for f2, g_ref in enumerate(gs):
+        part = dot(right_t, g_ref[...]).astype(BF16)
         for fl in range(2):
             f = f2 * 2 + fl
-            for g in range(2):
-                for e in range(width):
-                    n_ref[f * seqs + g * GROUP : f * seqs + (g + 1) * GROUP, e * n : (e + 1) * n] = (
-                        part[g * cols + e * GROUP : g * cols + (e + 1) * GROUP, fl * n : (fl + 1) * n]
-                    )
-    lane = iota((width, n), 1) // CHANS
-    for h in range(width // 4):
-        whole = dot(left_b, n_ref[:, h * 4 * n : (h + 1) * 4 * n], LHS_T)
-        packed = None
-        for el in range(4):
-            tile = None
-            for k in range(QUAD):
-                block = whole[k * width : (k + 1) * width, el * n : (el + 1) * n]
-                tile = block if tile is None else jnp.where(lane == k, block, tile)
-            tile = tile + pltpu.roll(tile, 2 * CHANS, 1)
-            tile = tile + pltpu.roll(tile, CHANS, 1)
-            packed = tile if packed is None else jnp.where(lane == el, tile, packed)
-        sums_ref[h * width : (h + 1) * width, :] = packed.astype(BF16)
-    linear = dot(r_ref[...], m_ref[...])
+            for e in range(width):
+                n_ref[f * GROUP : (f + 1) * GROUP, e * n : (e + 1) * n] = part[
+                    e * GROUP : (e + 1) * GROUP, fl * n : (fl + 1) * n
+                ]
+    linear = dot(right, m_ref[...])
+    right_ref[...] = dot(m_ref[...], turned[...])
+    for t in range(8):
+        for s in range(2):
+            flat_ref[s * width : (s + 1) * width, t * n : (t + 1) * n] = right_ref[
+                pl.ds(2 * t + s, width, stride=GROUP), :
+            ].astype(BF16)
+    half = 4 * n
+    act = dot(flat_ref[:, :half], ys[0][...]) + dot(flat_ref[:, half:], ys[1][...])
+    own_t = own_ref[...].T
+    lane = iota((chans, n), 1) // CHANS
+    packed = []
+    for h in range(width // QUAD):
+        whole = dot(own_t, n_ref[:, h * 4 * n : (h + 1) * 4 * n])
+        tiles = []
+        for el in range(QUAD):
+            tile = whole[0:chans, el * n : (el + 1) * n]
+            for k in range(1, QUAD):
+                tile = jnp.where(
+                    lane == k, whole[k * chans : (k + 1) * chans, el * n : (el + 1) * n], tile
+                )
+            tiles.append(tile)
+        packed.append(fold(tiles, lane))
+    return linear, act, jnp.concatenate(packed, axis=1)
+
+
+def half_kernel(
+    y0_ref, y1_ref, g0_ref, g1_ref, g2_ref, g3_ref, turned_ref, kron_ref, block_ref, wide_ref, bias_ref,
+    linear_ref, act_ref, feat_ref, *scratch
+):
+    linear, act, feat = half_of_rows(
+        (y0_ref, y1_ref), (g0_ref, g1_ref, g2_ref, g3_ref), turned_ref, kron_ref, block_ref, wide_ref, scratch
+    )
+    bias = bias_ref[...]
+    linear_ref[...] = linear + jnp.concatenate([bias] * 8, axis=1)
+    act_ref[...] = act
+    feat_ref[...] = feat
+
+
+def main_kernel(
+    y0_ref, y1_ref, g0_ref, g1_ref, g2_ref, g3_ref, turned_ref, kron_ref, block_ref, wide_ref,
+    linear_ref, act_ref, feat_ref, scale_ref, slope_ref, pair_ref, part_ref, left_ref,
+    update_ref, sums_ref,
+    slope_s_ref, *scratch
+):
+    rows, n, _ = pair_ref.shape
+    chans, width = 64, 32
+    linear, act, feat = half_of_rows(
+        (y0_ref, y1_ref), (g0_ref, g1_ref, g2_ref, g3_ref), turned_ref, kron_ref, block_ref, wide_ref, scratch
+    )
     for i in range(rows):
-        value = linear[:, i * n : (i + 1) * n] + bias_ref[...]
+        value = linear[:, i * n : (i + 1) * n] + linear_ref[:, i * n : (i + 1) * n]
         update_ref[i] = (scale_ref[i] * value).astype(BF16)
         slope_s_ref[i * n : (i + 1) * n, :] = (slope_ref[i] * value).astype(BF16)
     grad_gate = dot(pair_ref[...].reshape(rows * n, n), slope_s_ref[...], LHS_T)
     sums_ref[256:384, :] = grad_gate.astype(BF16)
-    left_act = dot(n_ref[...], part_ref[...], RHS_T).astype(BF16)
-    whole = dot(left_act, own_ref[...], LHS_T)
-    grad_left = whole[0:width, 0:chans]
-    for k in range(1, QUAD):
-        grad_left = grad_left + whole[k * width : (k + 1) * width, k * chans : (k + 1) * chans]
-    right_act = dot(full_ref[...], m_ref[...], RHS_T).astype(BF16)
-    whole = dot(feats[0], right_act[:, :cols], LHS_T) + dot(feats[1], right_act[:, cols:], LHS_T)
-    lane = iota((chans, cols), 1) % GROUP
-    tile = whole[0:chans, :]
-    for s in range(1, GROUP):
-        tile = jnp.where(lane == s, whole[s * chans : (s + 1) * chans, :], tile)
-    spread = jnp.where(iota((width, cols), 0) == iota((width, cols), 1) // GROUP, 1.0, 0.0)
-    grad_right = dot(spread, tile, RHS_T, precision=lax.Precision.HIGHEST)
+    feat = feat + feat_ref[...]
+    coarse = feat.astype(BF16)
+    fine = (feat - coarse.astype(F32)).astype(BF16)
+    grad_out = dot(left_ref[...], coarse) + dot(left_ref[...], fine)
+    for h in range(width // QUAD):
+        sums_ref[h * width : (h + 1) * width, :] = grad_out[:, h * n : (h + 1) * n].astype(BF16)
+    grad_left = dot(part_ref[...], coarse, RHS_T) + dot(part_ref[...], fine, RHS_T)
+    act = act + act_ref[...]
+    grad_right = act[:width, :chans] + act[width:, chans:]
     sums_ref[384:416, :] = jnp.concatenate([grad_left, grad_right], axis=1).astype(BF16)
 
 
@@ -243,14 +287,22 @@
     right_ref[...] = both[:, 64:128]
 
 
-def call(kernel, shapes, scratch=(), smem=0, ins=0, flops=1 << 20):
+def tie_kernel(*refs):
+    out_ref, at = refs[-1], 0
+    for ref in refs:
+        if at < out_ref.shape[0]:
+            out_ref[at : at + ref.shape[0], :] = ref[...]
+            at += ref.shape[0]
+
+
+def call(kernel, shapes, scratch=(), smem=0, ins=0, flops=1 << 20, vmem=4):
     return pl.pallas_call(
         kernel,
         out_shape=[jax.ShapeDtypeStruct(s, d) for s, d in shapes],
         in_specs=[SMEM] * smem + [VMEM] * (ins - smem),
         out_specs=[VMEM] * len(shapes),
         scratch_shapes=[pltpu.VMEM(s, d) for s, d in scratch],
-        compiler_params=pltpu.CompilerParams(vmem_limit_bytes=48 << 20),
+        compiler_params=pltpu.CompilerParams(vmem_limit_bytes=vmem << 20),
         cost_estimate=pl.CostEstimate(flops=flops, bytes_accessed=1 << 20, transcendentals=0),
     )
 
@@ -267,39 +319,51 @@
     rows, n, _ = pair_state.shape
     res = residue_mask.reshape(1, n)
     seq = sequence_row_mask.reshape(1, -1)
-    (feat,) = call(norm_kernel, [((n, n), BF16)], smem=1, ins=4)(
-        sequence_row_mask, alignment_state.transpose(0, 2, 1), res, norm_gain_vector.reshape(1, -1)
-    )
-    near = swap(feat, 4, size)
-    scale, slope, full, g0, g1, g2, g3 = call(
+    state = alignment_state.transpose(0, 2, 1)
+    near = swap(state, 4, size)
+    (token,) = call(first_kernel, [((8, n), F32)], flops=20 << 30)()
+    gain = norm_gain_vector.reshape(1, -1)
+    bias = output_bias.reshape(1, n)
+    scale, slope, turned, g0, g1, g2, g3, gain, bias = call(
         gate_kernel,
-        [((rows, n, n), F32), ((rows, n, n), F32), ((n, rows * n), BF16)] + [((n, 2 * n), BF16)] * 4,
-        smem=1, ins=6, flops=300 << 20,
-    )(residue_mask, seq, res, pair_state, cotangent, gate_matrix)
+        [((rows, n, n), F32), ((rows, n, n), F32), ((rows * n, n), BF16)] + [((n, 2 * n), BF16)] * 4
+        + [(gain.shape, F32), (bias.shape, F32)],
+        scratch=[((n, rows * n), BF16)], smem=1, ins=9, flops=1 << 30, vmem=12,
+    )(residue_mask, seq, res, pair_state, cotangent, gate_matrix, gain, bias, token)
+    (pair,) = call(norm_kernel, [((2 * n, n), BF16)], smem=1, ins=5)(
+        sequence_row_mask, res, gain, state, near
+    )
     g1 = swap(g1, 1, size)
     g2 = swap(g2, 2, size)
     g3 = swap(g3, 3, size)
+    far = swap(pair, 8, size)
+    left_t = left_matrix_weight.T
     kron, block, wide, part = call(
         weight_kernel,
-        [((1024, 512), BF16), ((256, n), BF16), ((32, 32 * n), BF16), ((n, 32 * n), BF16)],
-        scratch=[((1024, n), F32)], ins=3, flops=300 << 20,
-    )(right_matrix_weight.T, left_matrix_weight.T, output_weight)
-    y0 = jnp.concatenate([feat, near], axis=0)
-    y0 = jnp.concatenate([y0, swap(y0, 8, size)], axis=0)
+        [((1024, 512), BF16), ((256, n), BF16), ((32, 32 * n), BF16), ((32, 8 * n), BF16)],
+        scratch=[((1024, n), F32)], ins=4, flops=1 << 30, vmem=12,
+    )(right_matrix_weight.T, left_t, output_weight, pair)
+    (y0,) = call(tie_kernel, [((4 * n, n), BF16)], ins=6)(pair, far, g1, g2, g3, block)
     y1 = swap(y0, 2, size)
     y2 = swap(y0, 1, size)
+    scratch = [
+        ((512, rows * n), BF16), ((n, 32 * n), BF16), ((2, n, n), F32), ((n, 256), BF16),
+        ((512, n), F32), ((64, 8 * n), BF16),
+    ]
+    shared = (turned, kron, block, wide)
+    linear, act, gathered = call(
+        half_kernel,
+        [((n, rows * n), F32), ((64, n), F32), ((64, 8 * n), F32)],
+        scratch=scratch, ins=11, flops=2 << 30, vmem=24,
+    )(y0, y2, g0, g1, g2, g3, *shared, bias)
+    (y1,) = call(tie_kernel, [((4 * n, n), BF16)], ins=2)(y1, act)
     y3 = swap(y1, 1, size)
     update, sums = call(
         main_kernel,
         [((rows, n, n), BF16), ((416, n), BF16)],
-        scratch=[
-            ((n, 1024), BF16), ((1024, rows * n), BF16), ((256, 32 * n), BF16),
-            ((2, 256, n), F32), ((256, 256), BF16), ((rows * n, n), BF16),
-        ],
-        ins=17, flops=2000 << 20,
+        scratch=[((rows * n, n), BF16), *scratch], ins=18, flops=3 << 30, vmem=24,
     )(
-        y0, y1, y2, y3, g0, g1, g2, g3, full, scale, slope, pair_state,
-        output_bias.reshape(1, n), kron, block, wide, part,
+        y1, y3, g0, g1, g2, g3, *shared, linear, act, gathered, scale, slope, pair_state, part, left_t
     )
     sums = sums + swap(sums, 4, size)
     sums = sums + swap(sums, 8, size)

time: 55.7 us -> 46.6 us (0.84)
  starting transfers between devices: 16.6 us -> 12.6 us
  waiting for transfers between devices: 23.3 us -> 20.8 us
  local copies, waits for them, and re-layouts: 3.04 us -> 0.68 us
    ppermute x13, starting transfers between devices: 16.6 us -> 12.6 us  [swap(): return lax.ppermute(x, 'row', [(i, i ^ bit) for i in range(size)])]
    ppermute x13, waiting for transfers between devices: 23.3 us -> 20.8 us  [swap(): return lax.ppermute(x, 'row', [(i, i ^ bit) for i in range(size)])]
    unnamed x24 -> x22, local copies, waits for them, and re-layouts: 3.04 us -> 0.68 us
    pallas_call x3 -> x7, Pallas kernels: 9.02 us -> 8.94 us  [the longest x1 3.95 us: one_column(): call(main_kernel, [((rows, n, n), BF16), ((416, n), BF16)], scratch=[((ro...]
  transfers between devices with their start and end apart: 13 -> 13, of which waited for: 9 -> 7; matrix products, arithmetic and copies ran while one was open for 0% -> 0% of each run, Pallas kernels for 5% -> 13%
where the time goes in v2:
time: 46.6 us; the launch traced here: 46.5 us
  waiting for transfers between devices  20.8 us (45%)
  starting transfers between devices  12.6 us (27%)
  Pallas kernels  11.6 us (25%)
  between operations  0.8 us (2%)
  local copies, waits for them, and re-layouts  0.68 us (1%)
    ppermute x13, waiting for transfers between devices, swap(): return lax.ppermute(x, 'row', [(i, i ^ bit) for i in range(size)])  20.8 us
    ppermute x13, starting transfers between devices, swap(): return lax.ppermute(x, 'row', [(i, i ^ bit) for i in range(size)])  12.6 us
    pallas_call x1, Pallas kernels, one_column(): call(main_kernel, [((rows, n, n), BF16), ((416, n), BF16)], scratch=[((ro...  3.95 us
    pallas_call x1, Pallas kernels, one_column(): call(half_kernel, [((n, rows * n), F32), ((64, n), F32), ((64, 8 * n), F3...  2.97 us
    pallas_call x1, Pallas kernels, one_column(): call(last_kernel, [((1024, n), F32), ((n, n), F32), ((32, 64), F32), ((32...  1.4 us
    pallas_call x1, Pallas kernels, one_column(): call(gate_kernel, [((rows, n, n), F32), ((rows, n, n), F32), ((rows * n,...  1.32 us
    pallas_call x1, Pallas kernels, one_column(): call(weight_kernel, [((1024, 512), BF16), ((256, n), BF16), ((32, 32 * n)...  1.23 us
  transfers between devices with their start and end apart: 13, of which 7 were waited for; matrix products, arithmetic and copies ran while one was open for 0% of the time, Pallas kernels for 13%

profile of v2, /device:TPU:0, one launch (start us, length us, event | category | flops | bytes accessed | tf_op | source)
XLA Modules:
  0.0 46.5 jit_solution(1416564625887257537)
XLA Ops:
  0.7 3.1 %collective-permute-start = (bf16[2,64,128]{2,1,0:T(8,128)(2,1)}, bf16[2,64,128]{2,1,0:T(8,128)(2,1)S(1)}, u32[]{:S(2)}, u32[]{:S(2)}) collective-permute-start(bf16[2,64,128]{2,1,0:T(8,128)(2,1)} %bitcast.9), channel_id=1, source_target_pairs={{0,4},{1,5},{2,6},{3,7},{4,0},{5,1},{6,2},{7,3},{8,12},{9,13},{10,... | collective-permute-start | bytes 98312 | tf_op jit(solution)/shard_map/ppermute | solution.py:311
  3.8 0.6 %copy-done.10 = f32[128]{0:T(128)S(1)} copy-done((f32[128]{0:T(128)S(1)}, f32[128]{0:T(128)}, u32[]{:S(2)}) %copy-start.10) | copy-done | bytes 536
  4.5 1.3 %shard_map.147 = (f32[8,128,128]{2,1,0:T(8,128)S(1)}, f32[8,128,128]{2,1,0:T(8,128)S(1)}, bf16[1024,128]{1,0:T(8,128)(2,1)S(1)}, bf16[128,256]{1,0:T(8,128)(2,1)...) custom-call(s32[128]{0:T(128)S(1)} %copy-done.2, ...), custom_call_target="tpu_custom_call" | custom-call | flops 1073741824 | bytes 1048576 | tf_op jit(solution)/shard_map/pallas_call | solution.py:327
  5.8 0.1 collective-permute-start.2
  5.9 1.6 %collective-permute-start.3 = (bf16[128,256]{1,0:T(8,128)(2,1)S(1)}, bf16[128,256]{1,0:T(8,128)(2,1)S(1)}, u32[]{:S(2)}, u32[]{:S(2)}) collective-permute-start(bf16[128,256]{1,0:T(8,128)(2,1)S(1)} %get-tuple-element.29), channel_id=1, source_target_pairs={{0,2},{1,3},{2,0},{3,1},{4,6},{5,7},{6,4},{7,5},{8,10},{9,11},{10,... | collective-permute-start | bytes 196616 | tf_op jit(solution)/shard_map/ppermute | solution.py:311
  7.4 0.3 collective-permute-start.4
  7.7 0.7 %shard_map.148.after_ref.refs_0_ = bf16[256,128]{1,0:T(8,128)(2,1)S(1)} custom-call(s32[32]{0:T(128)S(1)} %copy-done.1, s32[1,128]{1,0:T(1,128)S(1)} %bitcast.13, f32[1,64]{1,0:T(1,128)S(1)} %get-tuple-element.27.gain_ref, bf16[2,64,128]{2,1,0:T(8,128)(2,1)S(1)} %bitcast.10, bf16[2,64,128]{2,1,0:T(8,128)(2,1)S(1)} %collective-permute-done.near_ref), custom_call_target="tpu_custom_call" | custom-call | flops 1048576 | bytes 1048576 | tf_op jit(solution)/shard_map/pallas_call | solution.py:333
  8.4 2.7 %collective-permute-start.1 = (bf16[256,128]{1,0:T(8,128)(2,1)S(1)}, bf16[256,128]{1,0:T(8,128)(2,1)S(1)}, u32[]{:S(2)}, u32[]{:S(2)}) collective-permute-start(bf16[256,128]{1,0:T(8,128)(2,1)S(1)} %shard_map.148.after_ref.refs_0_), channel_id=1, source_target_pairs={{0,8},{1,9},{2,10},{3,11},{4,12},{5,13},{6,14},{7,15},{8,0},{9,1},... | collective-permute-start | bytes 196616 | tf_op jit(solution)/shard_map/ppermute | solution.py:311
  11.1 1.2 %shard_map.149 = (bf16[1024,512]{1,0:T(8,128)(2,1)S(1)}, bf16[256,128]{1,0:T(8,128)(2,1)S(1)}, bf16[32,4096]{1,0:T(8,128)(2,1)S(1)}, bf16[32,1024]{1,0:T(8,128)(2,1)S(1)}) custom-call(bf16[32,64]{1,0:T(8,128)(2,1)S(1)} %bitcast.14, bf16[32,64]{1,0:T(8,128)(2,1)S(1)} %bitcast.15, bf16[1024,128]{1,0:T(8,128)(2,1)S(1)} %copy-done.4, ...), custom_call_target="tpu_custom_call" | custom-call | flops 1073741824 | bytes 1048576 | tf_op jit(solution)/shard_map/pallas_call | solution.py:341
  12.4 2.7 %collective-permute-done.1.refs_1_ = bf16[256,128]{1,0:T(8,128)(2,1)S(1)} collective-permute-done((bf16[256,128]{1,0:T(8,128)(2,1)S(1)}, bf16[256,128]{1,0:T(8,128)(2,1)S(1)}, u32[]{:S(2)}, u32[]{:S(2)}) %collective-permute-start.1) | collective-permute-done | bytes 65568 | tf_op jit(solution)/shard_map/ppermute | solution.py:311
  15.0 0.1 collective-permute-start.6
  15.2 1.6 %collective-permute-start.5 = (bf16[512,128]{1,0:T(8,128)(2,1)S(1)}, bf16[512,128]{1,0:T(8,128)(2,1)S(1)}, u32[]{:S(2)}, u32[]{:S(2)}) collective-permute-start(bf16[512,128]{1,0:T(8,128)(2,1)S(1)} %shard_map.150.y0_ref), channel_id=1, source_target_pairs={{0,2},{1,3},{2,0},{3,1},{4,6},{5,7},{6,4},{7,5},{8,10},{9,11},{10,... | collective-permute-start | bytes 393224 | tf_op jit(solution)/shard_map/ppermute | solution.py:311
  16.7 3.0 %shard_map.151 = (f32[128,1024]{1,0:T(8,128)S(1)}, f32[64,128]{1,0:T(8,128)S(1)}, f32[64,1024]{1,0:T(8,128)S(1)}) custom-call(bf16[512,128]{1,0:T(8,128)(2,1)S(1)} %shard_map.150.y0_ref, bf16[512,128]{1,0:T(8,128)(2,1)S(1)} %collective-permute-done.6.y1_ref, bf16[128,256]{1,0:T(8,128)(2,1)S(1)} %get-tuple-element.32.g0_ref, ...), custom_call_target="tpu_custom_call" | custom-call | flops 2147483648 | bytes 1048576 | tf_op jit(solution)/shard_map/pallas_call | solution.py:354
  19.7 1.3 %collective-permute-done.5.refs_0_ = bf16[512,128]{1,0:T(8,128)(2,1)S(1)} collective-permute-done((bf16[512,128]{1,0:T(8,128)(2,1)S(1)}, bf16[512,128]{1,0:T(8,128)(2,1)S(1)}, u32[]{:S(2)}, u32[]{:S(2)}) %collective-permute-start.5) | collective-permute-done | bytes 131104 | tf_op jit(solution)/shard_map/ppermute | solution.py:311
  21.0 0.1 collective-permute-start.7
  21.1 1.3 %collective-permute-done.7.y1_ref = bf16[512,128]{1,0:T(8,128)(2,1)S(1)} collective-permute-done((bf16[512,128]{1,0:T(8,128)(2,1)S(1)}, bf16[512,128]{1,0:T(8,128)(2,1)S(1)}, u32[]{:S(2)}, u32[]{:S(2)}) %collective-permute-start.7) | collective-permute-done | bytes 131104 | tf_op jit(solution)/shard_map/ppermute | solution.py:311
  22.5 3.9 %shard_map.153 = (bf16[8,128,128]{2,1,0:T(8,128)(2,1)}, bf16[416,128]{1,0:T(8,128)(2,1)S(1)}) custom-call(bf16[512,128]{1,0:T(8,128)(2,1)S(1)} %shard_map.152.y0_ref, bf16[512,128]{1,0:T(8,128)(2,1)S(1)} %collective-permute-done.7.y1_ref, bf16[128,256]{1,0:T(8,128)(2,1)S(1)} %get-tuple-element.32.g0_ref, ...), custom_call_target="tpu_custom_call" | custom-call | flops 3221225472 | bytes 1048576 | tf_op jit(solution)/shard_map/pallas_call | solution.py:361
  26.4 5.0 %collective-permute-done.8 = bf16[416,128]{1,0:T(8,128)(2,1)S(1)} collective-permute-done((bf16[416,128]{1,0:T(8,128)(2,1)S(1)}, bf16[416,128]{1,0:T(8,128)(2,1)S(1)}, u32[]{:S(2)}, u32[]{:S(2)}) %collective-permute-start.8) | collective-permute-done | bytes 106528 | tf_op jit(solution)/shard_map/ppermute | solution.py:311
  31.5 1.5 %collective-permute-start.9 = (bf16[416,128]{1,0:T(8,128)(2,1)S(1)}, bf16[416,128]{1,0:T(8,128)(2,1)S(1)}, u32[]{:S(2)}, u32[]{:S(2)}) collective-permute-start(bf16[416,128]{1,0:T(8,128)(2,1)S(1)} %add.6), channel_id=1, source_target_pairs={{0,8},{1,9},{2,10},{3,11},{4,12},{5,13},{6,14},{7,15},{8,0},{9,1},... | collective-permute-start | bytes 319496 | tf_op jit(solution)/shard_map/ppermute | solution.py:311
  33.0 5.9 %collective-permute-done.9 = bf16[416,128]{1,0:T(8,128)(2,1)S(1)} collective-permute-done((bf16[416,128]{1,0:T(8,128)(2,1)S(1)}, bf16[416,128]{1,0:T(8,128)(2,1)S(1)}, u32[]{:S(2)}, u32[]{:S(2)}) %collective-permute-start.9) | collective-permute-done | bytes 106528 | tf_op jit(solution)/shard_map/ppermute | solution.py:311
  38.9 1.6 %collective-permute-start.11 = (bf16[416,128]{1,0:T(8,128)(2,1)S(1)}, bf16[416,128]{1,0:T(8,128)(2,1)S(1)}, u32[]{:S(2)}, u32[]{:S(2)}) collective-permute-start(bf16[416,128]{1,0:T(8,128)(2,1)S(1)} %add.7.t0_ref), channel_id=1, source_target_pairs={{0,2},{1,3},{2,0},{3,1},{4,6},{5,7},{6,4},{7,5},{8,10},{9,11},{10,... | collective-permute-start | bytes 319496 | tf_op jit(solution)/shard_map/ppermute | solution.py:311
  40.5 3.2 %collective-permute-done.11.t2_ref = bf16[416,128]{1,0:T(8,128)(2,1)S(1)} collective-permute-done((bf16[416,128]{1,0:T(8,128)(2,1)S(1)}, bf16[416,128]{1,0:T(8,128)(2,1)S(1)}, u32[]{:S(2)}, u32[]{:S(2)}) %collective-permute-start.11) | collective-permute-done | bytes 106528 | tf_op jit(solution)/shard_map/ppermute | solution.py:311
  43.8 1.3 %collective-permute-done.12.t3_ref = bf16[416,128]{1,0:T(8,128)(2,1)S(1)} collective-permute-done((bf16[416,128]{1,0:T(8,128)(2,1)S(1)}, bf16[416,128]{1,0:T(8,128)(2,1)S(1)}, u32[]{:S(2)}, u32[]{:S(2)}) %collective-permute-start.12) | collective-permute-done | bytes 106528 | tf_op jit(solution)/shard_map/ppermute | solution.py:311
  45.1 1.4 %shard_map.154 = (f32[1024,128]{1,0:T(8,128)}, f32[128,128]{1,0:T(8,128)}, f32[32,64]{1,0:T(8,128)}, f32[32,64]{1,0:T(8,128)}) custom-call(bf16[416,128]{1,0:T(8,128)(2,1)S(1)} %add.7.t0_ref, bf16[416,128]{1,0:T(8,128)(2,1)S(1)} %collective-permute-done.10.t1_ref, bf16[416,128]{1,0:T(8,128)(2,1)S(1)} %collective-permute-done.11.t2_ref, ...), custom_call_target="tpu_custom_call" | custom-call | flops 1048576 | bytes 1048576 | tf_op jit(solution)/shard_map/pallas_call | solution.py:373
  (35 shorter events, 0.2 us)
Async XLA Ops:
  0.6 3.1 %copy-start.3 = (bf16[8,128,128]{2,1,0:T(8,128)(2,1)S(1)}, bf16[8,128,128]{2,1,0:T(8,128)(2,1)}, u32[]{:S(2)}) copy-start(bf16[8,128,128]{2,1,0:T(8,128)(2,1)} %cot_ref.1) | copy-start | bytes 786436
  0.6 3.1 %copy-start.5 = (bf16[8,128,128]{2,1,0:T(8,128)(2,1)S(1)}, bf16[8,128,128]{2,1,0:T(8,128)(2,1)}, u32[]{:S(2)}) copy-start(bf16[8,128,128]{2,1,0:T(8,128)(2,1)} %pair_ref.3) | copy-start | bytes 786436
  0.7 3.1 %copy-start.6 = (bf16[128,128]{1,0:T(8,128)(2,1)S(1)}, bf16[128,128]{1,0:T(8,128)(2,1)}, u32[]{:S(2)}) copy-start(bf16[128,128]{1,0:T(8,128)(2,1)} %gate_ref.1) | copy-start | bytes 98308
  0.7 7.1 %collective-permute-start = (bf16[2,64,128]{2,1,0:T(8,128)(2,1)}, bf16[2,64,128]{2,1,0:T(8,128)(2,1)S(1)}, u32[]{:S(2)}, u32[]{:S(2)}) collective-permute-start(bf16[2,64,128]{2,1,0:T(8,128)(2,1)} %bitcast.9), channel_id=1, source_target_pairs={{0,4},{1,5},{2,6},{3,7},{4,0},{5,1},{6,2},{7,3},{8,12},{9,13},{10,... | collective-permute-start | bytes 98312 | tf_op jit(solution)/shard_map/ppermute | solution.py:311
  3.8 0.7 %copy-start.10 = (f32[128]{0:T(128)S(1)}, f32[128]{0:T(128)}, u32[]{:S(2)}) copy-start(f32[128]{0:T(128)} %param.20) | copy-start | bytes 1540
  3.8 0.7 %copy-start.1 = (s32[32]{0:T(128)S(1)}, s32[32]{0:T(128)}, u32[]{:S(2)}) copy-start(s32[32]{0:T(128)} %seq_ref.1) | copy-start | bytes 388
  3.8 0.7 %copy-start.2 = (s32[128]{0:T(128)S(1)}, s32[128]{0:T(128)}, u32[]{:S(2)}) copy-start(s32[128]{0:T(128)} %res_s_ref.1) | copy-start | bytes 1540
  3.8 0.7 %copy-start.9 = (f32[64]{0:T(128)S(1)}, f32[64]{0:T(128)}, u32[]{:S(2)}) copy-start(f32[64]{0:T(128)} %param.16) | copy-start | bytes 772
  4.5 3.3 %copy-start = (bf16[2,128,64]{1,2,0:T(8,128)(2,1)S(1)}, bf16[2,128,64]{1,2,0:T(8,128)(2,1)}, u32[]{:S(2)}) copy-start(bf16[2,128,64]{1,2,0:T(8,128)(2,1)} %param.11) | copy-start | bytes 98308
  4.5 6.6 %copy-start.4 = (bf16[1024,128]{1,0:T(8,128)(2,1)S(1)}, bf16[1024,128]{1,0:T(8,128)(2,1)}, u32[]{:S(2)}) copy-start(bf16[1024,128]{1,0:T(8,128)(2,1)} %out_w_ref.1) | copy-start | bytes 786436
  5.8 6.5 %collective-permute-start.2 = (bf16[128,256]{1,0:T(8,128)(2,1)S(1)}, bf16[128,256]{1,0:T(8,128)(2,1)S(1)}, u32[]{:S(2)}, u32[]{:S(2)}) collective-permute-start(bf16[128,256]{1,0:T(8,128)(2,1)S(1)} %get-tuple-element.28), channel_id=1, source_target_pairs={{0,1},{1,0},{2,3},{3,2},{4,5},{5,4},{6,7},{7,6},{8,9},{9,8},{10,11... | collective-permute-start | bytes 196616 | tf_op jit(solution)/shard_map/ppermute | solution.py:311
  5.9 6.5 %collective-permute-start.3 = (bf16[128,256]{1,0:T(8,128)(2,1)S(1)}, bf16[128,256]{1,0:T(8,128)(2,1)S(1)}, u32[]{:S(2)}, u32[]{:S(2)}) collective-permute-start(bf16[128,256]{1,0:T(8,128)(2,1)S(1)} %get-tuple-element.29), channel_id=1, source_target_pairs={{0,2},{1,3},{2,0},{3,1},{4,6},{5,7},{6,4},{7,5},{8,10},{9,11},{10,... | collective-permute-start | bytes 196616 | tf_op jit(solution)/shard_map/ppermute | solution.py:311
  7.4 4.9 %collective-permute-start.4 = (bf16[128,256]{1,0:T(8,128)(2,1)S(1)}, bf16[128,256]{1,0:T(8,128)(2,1)S(1)}, u32[]{:S(2)}, u32[]{:S(2)}) collective-permute-start(bf16[128,256]{1,0:T(8,128)(2,1)S(1)} %get-tuple-element.30), channel_id=1, source_target_pairs={{0,3},{1,2},{2,1},{3,0},{4,7},{5,6},{6,5},{7,4},{8,11},{9,10},{10,... | collective-permute-start | bytes 196616 | tf_op jit(solution)/shard_map/ppermute | solution.py:311
  7.7 3.4 %copy-start.7 = (bf16[64,32]{0,1:T(8,128)(2,1)S(1)}, bf16[64,32]{0,1:T(8,128)(2,1)}, u32[]{:S(2)}) copy-start(bf16[64,32]{0,1:T(8,128)(2,1)} %param.18) | copy-start | bytes 12292
  7.7 3.4 %copy-start.8 = (bf16[64,32]{0,1:T(8,128)(2,1)S(1)}, bf16[64,32]{0,1:T(8,128)(2,1)}, u32[]{:S(2)}) copy-start(bf16[64,32]{0,1:T(8,128)(2,1)} %param.17) | copy-start | bytes 12292
  8.4 6.6 %collective-permute-start.1 = (bf16[256,128]{1,0:T(8,128)(2,1)S(1)}, bf16[256,128]{1,0:T(8,128)(2,1)S(1)}, u32[]{:S(2)}, u32[]{:S(2)}) collective-permute-start(bf16[256,128]{1,0:T(8,128)(2,1)S(1)} %shard_map.148.after_ref.refs_0_), channel_id=1, source_target_pairs={{0,8},{1,9},{2,10},{3,11},{4,12},{5,13},{6,14},{7,15},{8,0},{9,1},... | collective-permute-start | bytes 196616 | tf_op jit(solution)/shard_map/ppermute | solution.py:311
  15.0 1.7 %collective-permute-start.6 = (bf16[512,128]{1,0:T(8,128)(2,1)S(1)}, bf16[512,128]{1,0:T(8,128)(2,1)S(1)}, u32[]{:S(2)}, u32[]{:S(2)}) collective-permute-start(bf16[512,128]{1,0:T(8,128)(2,1)S(1)} %shard_map.150.y0_ref), channel_id=1, source_target_pairs={{0,1},{1,0},{2,3},{3,2},{4,5},{5,4},{6,7},{7,6},{8,9},{9,8},{10,11... | collective-permute-start | bytes 393224 | tf_op jit(solution)/shard_map/ppermute | solution.py:311
  15.2 5.9 %collective-permute-start.5 = (bf16[512,128]{1,0:T(8,128)(2,1)S(1)}, bf16[512,128]{1,0:T(8,128)(2,1)S(1)}, u32[]{:S(2)}, u32[]{:S(2)}) collective-permute-start(bf16[512,128]{1,0:T(8,128)(2,1)S(1)} %shard_map.150.y0_ref), channel_id=1, source_target_pairs={{0,2},{1,3},{2,0},{3,1},{4,6},{5,7},{6,4},{7,5},{8,10},{9,11},{10,... | collective-permute-start | bytes 393224 | tf_op jit(solution)/shard_map/ppermute | solution.py:311
  21.0 1.4 %collective-permute-start.7 = (bf16[512,128]{1,0:T(8,128)(2,1)S(1)}, bf16[512,128]{1,0:T(8,128)(2,1)S(1)}, u32[]{:S(2)}, u32[]{:S(2)}) collective-permute-start(bf16[512,128]{1,0:T(8,128)(2,1)S(1)} %shard_map.152.y0_ref), channel_id=1, source_target_pairs={{0,1},{1,0},{2,3},{3,2},{4,5},{5,4},{6,7},{7,6},{8,9},{9,8},{10,11... | collective-permute-start | bytes 393224 | tf_op jit(solution)/shard_map/ppermute | solution.py:311
  26.4 5.0 %collective-permute-start.8 = (bf16[416,128]{1,0:T(8,128)(2,1)S(1)}, bf16[416,128]{1,0:T(8,128)(2,1)S(1)}, u32[]{:S(2)}, u32[]{:S(2)}) collective-permute-start(bf16[416,128]{1,0:T(8,128)(2,1)S(1)} %get-tuple-element.44), channel_id=1, source_target_pairs={{0,4},{1,5},{2,6},{3,7},{4,0},{5,1},{6,2},{7,3},{8,12},{9,13},{10,... | collective-permute-start | bytes 319496 | tf_op jit(solution)/shard_map/ppermute | solution.py:311
  31.5 7.4 %collective-permute-start.9 = (bf16[416,128]{1,0:T(8,128)(2,1)S(1)}, bf16[416,128]{1,0:T(8,128)(2,1)S(1)}, u32[]{:S(2)}, u32[]{:S(2)}) collective-permute-start(bf16[416,128]{1,0:T(8,128)(2,1)S(1)} %add.6), channel_id=1, source_target_pairs={{0,8},{1,9},{2,10},{3,11},{4,12},{5,13},{6,14},{7,15},{8,0},{9,1},... | collective-permute-start | bytes 319496 | tf_op jit(solution)/shard_map/ppermute | solution.py:311
  38.9 4.8 %collective-permute-start.11 = (bf16[416,128]{1,0:T(8,128)(2,1)S(1)}, bf16[416,128]{1,0:T(8,128)(2,1)S(1)}, u32[]{:S(2)}, u32[]{:S(2)}) collective-permute-start(bf16[416,128]{1,0:T(8,128)(2,1)S(1)} %add.7.t0_ref), channel_id=1, source_target_pairs={{0,2},{1,3},{2,0},{3,1},{4,6},{5,7},{6,4},{7,5},{8,10},{9,11},{10,... | collective-permute-start | bytes 319496 | tf_op jit(solution)/shard_map/ppermute | solution.py:311
  40.5 3.2 %collective-permute-start.10 = (bf16[416,128]{1,0:T(8,128)(2,1)S(1)}, bf16[416,128]{1,0:T(8,128)(2,1)S(1)}, u32[]{:S(2)}, u32[]{:S(2)}) collective-permute-start(bf16[416,128]{1,0:T(8,128)(2,1)S(1)} %add.7.t0_ref), channel_id=1, source_target_pairs={{0,1},{1,0},{2,3},{3,2},{4,5},{5,4},{6,7},{7,6},{8,9},{9,8},{10,11... | collective-permute-start | bytes 319496 | tf_op jit(solution)/shard_map/ppermute | solution.py:311
  43.8 1.3 %collective-permute-start.12 = (bf16[416,128]{1,0:T(8,128)(2,1)S(1)}, bf16[416,128]{1,0:T(8,128)(2,1)S(1)}, u32[]{:S(2)}, u32[]{:S(2)}) collective-permute-start(bf16[416,128]{1,0:T(8,128)(2,1)S(1)} %collective-permute-done.11.t2_ref), channel_id=1, source_target_pairs={{0,1},{1,0},{2,3},{3,2},{4,5},{5,4},{6,7},{7,6},{8,9},{9,8},{10,11... | collective-permute-start | bytes 319496 | tf_op jit(solution)/shard_map/ppermute | solution.py:311

commit v3 on v2

--- a/solution.py
+++ b/solution.py
@@ -14,6 +14,7 @@
 LHS_T = (((0,), (0,)), ((), ()))
 RHS_T = (((1,), (1,)), ((), ()))
 QUAD = 4
+ACROSS = 4
 CHANS = 32
 GROUP = 16
 
@@ -26,11 +27,15 @@
     return lax.dot_general(a, b, dims, preferred_element_type=F32, **kw)
 
 
+def place_in_quad(row):
+    return row % 2 + row // ACROSS % 2 * 2
+
+
 def first_kernel(out_ref):
     out_ref[...] = jnp.zeros_like(out_ref)
 
 
-def norm_kernel(seq_ref, res_ref, gain_ref, own_ref, near_ref, out_ref):
+def norm_kernel(seq_ref, res_ref, gain_ref, own_ref, near_ref, after_ref, out_ref):
     row = lax.axis_index("row")
     n = res_ref.shape[1]
     res = res_ref[...].astype(F32)
@@ -50,13 +55,13 @@
 
 def gate_kernel(
     res_s_ref, seq_ref, res_ref, pair_ref, cot_ref, gate_ref, gain_ref, bias_ref, after_ref,
-    scale_ref, slope_ref, turned_ref, own_ref, core_ref, across_ref, both_ref, gain_out_ref, bias_out_ref,
+    scale_ref, slope_ref, turned_ref, own_ref, core_ref, across_ref, gain_out_ref, bias_out_ref,
     full_ref,
 ):
     gain_out_ref[...] = gain_ref[...]
     bias_out_ref[...] = bias_ref[...]
     row = lax.axis_index("row")
-    quad_at = lax.rem(row, QUAD)
+    quad_at = place_in_quad(row)
     rows = pair_ref.shape[0]
     n = res_ref.shape[1]
     total = jnp.sum(seq_ref[...].astype(F32), axis=1, keepdims=True)
@@ -70,7 +75,7 @@
     place = jnp.where(
         (src // n == (dst % n) // CHANS) & (src % n == chan), 1.0, 0.0
     ).astype(BF16)
-    outs = (own_ref, core_ref, across_ref, both_ref)
+    outs = ((own_ref, 0), (core_ref, 0), (across_ref, 0), (across_ref, 2 * n))
     for half in range(rows // QUAD):
         for k in range(QUAD):
             i = half * QUAD + k
@@ -84,14 +89,15 @@
             turned_ref[i * n : (i + 1) * n, :] = lin.T.astype(BF16)
         packed = dot(full_ref[:, half * wide : (half + 1) * wide], place).astype(BF16)
         for m in range(QUAD):
-            outs[m][:, half * n : (half + 1) * n] = packed[:, m * n : (m + 1) * n]
+            out_ref, at = outs[m]
+            out_ref[:, at + half * n : at + (half + 1) * n] = packed[:, m * n : (m + 1) * n]
 
 
 def weight_kernel(
     right_ref, left_ref, out_w_ref, after_ref,
     kron_ref, block_ref, wide_ref, part_ref, wf_ref,
 ):
-    quad_at = lax.rem(lax.axis_index("row"), QUAD)
+    quad_at = place_in_quad(lax.axis_index("row"))
     width, chans = right_ref.shape
     n = out_w_ref.shape[1]
     cols = width * GROUP
@@ -134,19 +140,18 @@
     return jnp.where(low, pairs[0], pairs[1]) + other
 
 
-def half_of_rows(ys, gs, turned, kron_ref, block_ref, wide_ref, scratch):
-    m_ref, n_ref, turn_ref, own_ref, right_ref, flat_ref = scratch
+def half_of_rows(ys, turned, kron_ref, block_ref, wide_ref, right_t_ref, own_ref, scratch):
+    m_ref, turn_ref, right_ref, flat_ref = scratch
     row = lax.axis_index("row")
-    quad_at = lax.rem(row, QUAD)
-    first = (row - quad_at) * 8
     n = ys[0].shape[1]
     chans, width = 64, 32
     slots = [y[t * n : (t + 1) * n, :] for y in ys for t in range(4)]
     right = dot(jnp.concatenate(slots, axis=1), kron_ref[...]).astype(BF16)
-    right_t = right.T
+    right_t_ref[...] = right.T
     at = iota((32, n), 0)
     four = at % 8
-    here = first + (quad_at ^ (four // 2)) * 8 + (four % 2) * QUAD + at // 8
+    member = four // 2
+    here = (row ^ (member % 2 + member // 2 * ACROSS)) * 8 + (four % 2) * QUAD + at // 8
     pick = jnp.where(iota((32, n), 1) == here, 1.0, 0.0).astype(BF16)
     for t, slot in enumerate(slots):
         picked = dot(pick, slot)
@@ -182,14 +187,6 @@
                 m_ref[e * GROUP : (e + 1) * GROUP, i * n : (i + 1) * n] = part[
                     i * GROUP : (i + 1) * GROUP, el * n : (el + 1) * n
                 ]
-    for f2, g_ref in enumerate(gs):
-        part = dot(right_t, g_ref[...]).astype(BF16)
-        for fl in range(2):
-            f = f2 * 2 + fl
-            for e in range(width):
-                n_ref[f * GROUP : (f + 1) * GROUP, e * n : (e + 1) * n] = part[
-                    e * GROUP : (e + 1) * GROUP, fl * n : (fl + 1) * n
-                ]
     linear = dot(right, m_ref[...])
     right_ref[...] = dot(m_ref[...], turned[...])
     for t in range(8):
@@ -199,7 +196,66 @@
             ].astype(BF16)
     half = 4 * n
     act = dot(flat_ref[:, :half], ys[0][...]) + dot(flat_ref[:, half:], ys[1][...])
-    own_t = own_ref[...].T
+    return linear, act
+
+
+def half_kernel(
+    y0_ref, y1_ref, turned_ref, kron_ref, block_ref, wide_ref, bias_ref,
+    linear_ref, act_ref, right_t_ref, own_ref, *scratch
+):
+    linear, act = half_of_rows(
+        (y0_ref, y1_ref), turned_ref, kron_ref, block_ref, wide_ref, right_t_ref, own_ref, scratch
+    )
+    linear_ref[...] = linear + jnp.concatenate([bias_ref[...]] * 8, axis=1)
+    act_ref[...] = act
+
+
+def pair_kernel(
+    y0_ref, y1_ref, turned_ref, kron_ref, block_ref, wide_ref,
+    linear_ref, act_ref, slope_ref, pair_ref,
+    value_ref, gate_ref, grad_right_ref, right_t_ref, own_ref, slope_s_ref, *scratch
+):
+    rows, n, _ = pair_ref.shape
+    linear, act = half_of_rows(
+        (y0_ref, y1_ref), turned_ref, kron_ref, block_ref, wide_ref, right_t_ref, own_ref, scratch
+    )
+    for i in range(rows):
+        value = linear[:, i * n : (i + 1) * n] + linear_ref[:, i * n : (i + 1) * n]
+        value_ref[i] = value
+        slope_s_ref[i * n : (i + 1) * n, :] = (slope_ref[i] * value).astype(BF16)
+    gate_ref[...] = dot(pair_ref[...].reshape(rows * n, n), slope_s_ref[...], LHS_T).astype(BF16)
+    act = act + act_ref[...]
+    grad_right_ref[...] = act[:32, :64] + act[32:, 64:]
+
+
+def update_kernel(scale_ref, value_ref, after_ref, update_ref, token_ref):
+    token_ref[...] = jnp.zeros_like(token_ref)
+    update_ref[...] = (scale_ref[...] * value_ref[...]).astype(BF16)
+
+
+def add_kernel(own_ref, other_ref, after_ref, out_ref):
+    out_ref[...] = (own_ref[...].astype(F32) + other_ref[...].astype(F32)).astype(BF16)
+
+
+def out_kernel(
+    right0_ref, right1_ref, own0_ref, own1_ref, own_ref, core_ref, across_ref,
+    part_ref, left_ref, gate_ref, grad_right_ref,
+    sums_ref, n_ref
+):
+    n = gate_ref.shape[0]
+    chans, width = 64, 32
+    half = 8 * GROUP
+    grads = (own_ref[...], core_ref[:, : 2 * n], across_ref[:, : 2 * n], core_ref[:, 2 * n :])
+    for f2, grad in enumerate(grads):
+        for g, right_ref in enumerate((right0_ref, right1_ref)):
+            part = dot(right_ref[...], grad).astype(BF16)
+            for fl in range(2):
+                at = g * half + (f2 * 2 + fl) * GROUP
+                for e in range(width):
+                    n_ref[at : at + GROUP, e * n : (e + 1) * n] = part[
+                        e * GROUP : (e + 1) * GROUP, fl * n : (fl + 1) * n
+                    ]
+    own_t = jnp.concatenate([own0_ref[...], own1_ref[...]], axis=0).T
     lane = iota((chans, n), 1) // CHANS
     packed = []
     for h in range(width // QUAD):
@@ -213,55 +269,31 @@
                 )
             tiles.append(tile)
         packed.append(fold(tiles, lane))
-    return linear, act, jnp.concatenate(packed, axis=1)
-
-
-def half_kernel(
-    y0_ref, y1_ref, g0_ref, g1_ref, g2_ref, g3_ref, turned_ref, kron_ref, block_ref, wide_ref, bias_ref,
-    linear_ref, act_ref, feat_ref, *scratch
-):
-    linear, act, feat = half_of_rows(
-        (y0_ref, y1_ref), (g0_ref, g1_ref, g2_ref, g3_ref), turned_ref, kron_ref, block_ref, wide_ref, scratch
-    )
-    bias = bias_ref[...]
-    linear_ref[...] = linear + jnp.concatenate([bias] * 8, axis=1)
-    act_ref[...] = act
-    feat_ref[...] = feat
-
-
-def main_kernel(
-    y0_ref, y1_ref, g0_ref, g1_ref, g2_ref, g3_ref, turned_ref, kron_ref, block_ref, wide_ref,
-    linear_ref, act_ref, feat_ref, scale_ref, slope_ref, pair_ref, part_ref, left_ref,
-    update_ref, sums_ref,
-    slope_s_ref, *scratch
-):
-    rows, n, _ = pair_ref.shape
-    chans, width = 64, 32
-    linear, act, feat = half_of_rows(
-        (y0_ref, y1_ref), (g0_ref, g1_ref, g2_ref, g3_ref), turned_ref, kron_ref, block_ref, wide_ref, scratch
-    )
-    for i in range(rows):
-        value = linear[:, i * n : (i + 1) * n] + linear_ref[:, i * n : (i + 1) * n]
-        update_ref[i] = (scale_ref[i] * value).astype(BF16)
-        slope_s_ref[i * n : (i + 1) * n, :] = (slope_ref[i] * value).astype(BF16)
-    grad_gate = dot(pair_ref[...].reshape(rows * n, n), slope_s_ref[...], LHS_T)
-    sums_ref[256:384, :] = grad_gate.astype(BF16)
-    feat = feat + feat_ref[...]
+    feat = jnp.concatenate(packed, axis=1)
     coarse = feat.astype(BF16)
     fine = (feat - coarse.astype(F32)).astype(BF16)
     grad_out = dot(left_ref[...], coarse) + dot(left_ref[...], fine)
     for h in range(width // QUAD):
         sums_ref[h * width : (h + 1) * width, :] = grad_out[:, h * n : (h + 1) * n].astype(BF16)
     grad_left = dot(part_ref[...], coarse, RHS_T) + dot(part_ref[...], fine, RHS_T)
-    act = act + act_ref[...]
-    grad_right = act[:width, :chans] + act[width:, chans:]
-    sums_ref[384:416, :] = jnp.concatenate([grad_left, grad_right], axis=1).astype(BF16)
-
-
-def last_kernel(t0_ref, t1_ref, t2_ref, t3_ref, out_ref, gate_ref, left_ref, right_ref):
-    quad_at = lax.rem(lax.axis_index("row"), QUAD)
-    n = t0_ref.shape[1]
-    ts = (t0_ref, t1_ref, t2_ref, t3_ref)
+    sums_ref[256:384, :] = gate_ref[...]
+    sums_ref[384:416, :] = jnp.concatenate([grad_left, grad_right_ref[...]], axis=1).astype(BF16)
+
+
+def join_kernel(own_ref, beside_ref, across_ref, both_ref, out_ref):
+    def pair(a_ref, b_ref, lo, hi):
+        return a_ref[lo:hi, :].astype(F32) + b_ref[lo:hi, :].astype(F32)
+
+    out_ref[0:256, :] = pair(own_ref, beside_ref, 0, 256).astype(BF16)
+    out_ref[256:512, :] = pair(across_ref, both_ref, 0, 256).astype(BF16)
+    out_ref[512:672, :] = (
+        pair(own_ref, beside_ref, 256, 416) + pair(across_ref, both_ref, 256, 416)
+    ).astype(BF16)
+
+
+def last_kernel(local_ref, other_ref, out_ref, gate_ref, left_ref, right_ref):
+    quad_at = place_in_quad(lax.axis_index("row"))
+    n = local_ref.shape[1]
     wide = QUAD * n
     src = iota((wide, wide), 0)
     dst = iota((wide, wide), 1)
@@ -269,20 +301,17 @@
     place = jnp.where(
         (dst // n == (src % n) // CHANS) & (dst % n == chan), 1.0, 0.0
     ).astype(BF16)
-    packed = jnp.concatenate([t[0:256, :] for t in ts], axis=1)
+    packed = jnp.concatenate(
+        [local_ref[0:256, :], other_ref[0:256, :], local_ref[256:512, :], other_ref[256:512, :]], axis=1
+    )
     whole = dot(packed, place)
     for h in range(8):
         for el in range(4):
             out_ref[pl.ds(h * 4 + el, 32, stride=32), :] = whole[
                 h * 32 : (h + 1) * 32, el * n : (el + 1) * n
             ]
-
-    def total(lo, hi):
-        a, b, c, d = (t[lo:hi, :].astype(F32) for t in ts)
-        return (a + b) + (c + d)
-
-    gate_ref[...] = total(256, 384)
-    both = total(384, 416)
+    gate_ref[...] = local_ref[512:640, :].astype(F32) + other_ref[512:640, :].astype(F32)
+    both = local_ref[640:672, :].astype(F32) + other_ref[640:672, :].astype(F32)
     left_ref[...] = both[:, 0:64]
     right_ref[...] = both[:, 64:128]
 
@@ -324,18 +353,15 @@
     (token,) = call(first_kernel, [((8, n), F32)], flops=20 << 30)()
     gain = norm_gain_vector.reshape(1, -1)
     bias = output_bias.reshape(1, n)
-    scale, slope, turned, g0, g1, g2, g3, gain, bias = call(
+    scale, slope, turned, own, core, across, gain, bias = call(
         gate_kernel,
-        [((rows, n, n), F32), ((rows, n, n), F32), ((rows * n, n), BF16)] + [((n, 2 * n), BF16)] * 4
-        + [(gain.shape, F32), (bias.shape, F32)],
+        [((rows, n, n), F32), ((rows, n, n), F32), ((rows * n, n), BF16)] + [((n, 2 * n), BF16)] * 2
+        + [((n, 4 * n), BF16), (gain.shape, F32), (bias.shape, F32)],
         scratch=[((n, rows * n), BF16)], smem=1, ins=9, flops=1 << 30, vmem=12,
     )(residue_mask, seq, res, pair_state, cotangent, gate_matrix, gain, bias, token)
-    (pair,) = call(norm_kernel, [((2 * n, n), BF16)], smem=1, ins=5)(
-        sequence_row_mask, res, gain, state, near
-    )
-    g1 = swap(g1, 1, size)
-    g2 = swap(g2, 2, size)
-    g3 = swap(g3, 3, size)
+    (pair,) = call(norm_kernel, [((2 * n, n), BF16)], smem=1, ins=6)(
+        sequence_row_mask, res, gain, state, near, own
+    )
     far = swap(pair, 8, size)
     left_t = left_matrix_weight.T
     kron, block, wide, part = call(
@@ -343,38 +369,42 @@
         [((1024, 512), BF16), ((256, n), BF16), ((32, 32 * n), BF16), ((32, 8 * n), BF16)],
         scratch=[((1024, n), F32)], ins=4, flops=1 << 30, vmem=12,
     )(right_matrix_weight.T, left_t, output_weight, pair)
-    (y0,) = call(tie_kernel, [((4 * n, n), BF16)], ins=6)(pair, far, g1, g2, g3, block)
+    (y0,) = call(tie_kernel, [((4 * n, n), BF16)], ins=3)(pair, far, block)
     y1 = swap(y0, 2, size)
     y2 = swap(y0, 1, size)
+    (across,) = call(tie_kernel, [((n, 4 * n), BF16)], ins=2)(across, y2)
+    across = swap(across, ACROSS, size)
+    core = swap(jnp.concatenate([core, across[:, 2 * n :]], axis=1), 1, size)
     scratch = [
-        ((512, rows * n), BF16), ((n, 32 * n), BF16), ((2, n, n), F32), ((n, 256), BF16),
-        ((512, n), F32), ((64, 8 * n), BF16),
+        ((512, rows * n), BF16), ((2, n, n), F32), ((512, n), F32), ((64, 8 * n), BF16),
     ]
     shared = (turned, kron, block, wide)
-    linear, act, gathered = call(
+    kept = [((512, n), BF16), ((n, 256), BF16)]
+    linear, act, right0, own0 = call(
         half_kernel,
-        [((n, rows * n), F32), ((64, n), F32), ((64, 8 * n), F32)],
-        scratch=scratch, ins=11, flops=2 << 30, vmem=24,
-    )(y0, y2, g0, g1, g2, g3, *shared, bias)
+        [((n, rows * n), F32), ((64, n), F32), *kept],
+        scratch=scratch, ins=7, flops=2 << 30, vmem=24,
+    )(y0, y2, *shared, bias)
     (y1,) = call(tie_kernel, [((4 * n, n), BF16)], ins=2)(y1, act)
     y3 = swap(y1, 1, size)
-    update, sums = call(
-        main_kernel,
-        [((rows, n, n), BF16), ((416, n), BF16)],
-        scratch=[((rows * n, n), BF16), *scratch], ins=18, flops=3 << 30, vmem=24,
-    )(
-        y1, y3, g0, g1, g2, g3, *shared, linear, act, gathered, scale, slope, pair_state, part, left_t
-    )
-    sums = sums + swap(sums, 4, size)
-    sums = sums + swap(sums, 8, size)
-    across = swap(sums, 2, size)
-    core = swap(sums, 1, size)
-    both = swap(across, 1, size)
+    value, gate_sum, right_sum, right1, own1 = call(
+        pair_kernel,
+        [((rows, n, n), F32), ((n, n), BF16), ((32, 64), F32), *kept],
+        scratch=[((rows * n, n), BF16), *scratch], ins=10, flops=2 << 30, vmem=24,
+    )(y1, y3, *shared, linear, act, slope, pair_state)
+    (sums,) = call(
+        out_kernel, [((416, n), BF16)], scratch=[((256, 32 * n), BF16)], ins=11, flops=1 << 30, vmem=24,
+    )(right0, right1, own0, own1, own, core, across, part, left_t, gate_sum, right_sum)
+    update, token = call(update_kernel, [((rows, n, n), BF16), ((8, n), F32)], ins=3, flops=1 << 30, vmem=8)(scale, value, sums)
+    (sums,) = call(add_kernel, [((416, n), BF16)], ins=3)(sums, swap(sums, 8, size), token)
+    others = [swap(sums, step, size) for step in (2, ACROSS, 2 ^ ACROSS)]
+    (local,) = call(join_kernel, [((672, n), BF16)], ins=4)(sums, *others)
+    other = swap(local, 1, size)
     grad_out, grad_gate, left, right = call(
         last_kernel,
         [((1024, n), F32), ((n, n), F32), ((32, 64), F32), ((32, 64), F32)],
-        ins=4,
-    )(sums, core, across, both)
+        ins=2,
+    )(local, other)
     return update, left.T, right.T, grad_out, grad_gate
 
 

time: 46.6 us -> 43.4 us (0.931)
  waiting for transfers between devices: 20.8 us -> 13.9 us
  starting transfers between devices: 12.6 us -> 16.6 us
    ppermute x13 -> x12, waiting for transfers between devices: 20.8 us -> 13.9 us  [swap(): return lax.ppermute(x, 'row', [(i, i ^ bit) for i in range(size)])]
    ppermute x13 -> x12, starting transfers between devices: 12.6 us -> 16.6 us  [swap(): return lax.ppermute(x, 'row', [(i, i ^ bit) for i in range(size)])]
    pallas_call x4 -> x9, Pallas kernels: 7.61 us -> 7.31 us  [the longest x1 2.07 us: one_column(): call(half_kernel, [((n, rows * n), F32), ((64, n), F32), *kept], scratch=...]
  transfers between devices with their start and end apart: 13 -> 12, of which waited for: 7 -> 9; matrix products, arithmetic and copies ran while one was open for 0% -> 0% of each run, Pallas kernels for 13% -> 17%
where the time goes in v3:
time: 43.4 us; the launch traced here: 43.3 us
  starting transfers between devices  16.6 us (38%)
  waiting for transfers between devices  13.9 us (32%)
  Pallas kernels  11.2 us (26%)
  between operations  0.81 us (2%)
  local copies, waits for them, and re-layouts  0.69 us (2%)
    ppermute x12, starting transfers between devices, swap(): return lax.ppermute(x, 'row', [(i, i ^ bit) for i in range(size)])  16.6 us
    ppermute x12, waiting for transfers between devices, swap(): return lax.ppermute(x, 'row', [(i, i ^ bit) for i in range(size)])  13.9 us
    pallas_call x1, Pallas kernels, one_column(): call(half_kernel, [((n, rows * n), F32), ((64, n), F32), *kept], scratch=...  2.07 us
    pallas_call x1, Pallas kernels, one_column(): call(pair_kernel, [((rows, n, n), F32), ((n, n), BF16), ((32, 64), F32),...  2.05 us
    pallas_call x1, Pallas kernels, one_column(): call(out_kernel, [((416, n), BF16)], scratch=[((256, 32 * n), BF16)], ins...  1.66 us
    pallas_call x1, Pallas kernels, one_column(): call(last_kernel, [((1024, n), F32), ((n, n), F32), ((32, 64), F32), ((32...  1.37 us
    pallas_call x1, Pallas kernels, one_column(): call(gate_kernel, [((rows, n, n), F32), ((rows, n, n), F32), ((rows * n,...  1.32 us
    pallas_call x1, Pallas kernels, one_column(): call(weight_kernel, [((1024, 512), BF16), ((256, n), BF16), ((32, 32 * n)...  1.23 us
  transfers between devices with their start and end apart: 12, of which 9 were waited for; matrix products, arithmetic and copies ran while one was open for 0% of the time, Pallas kernels for 17%

profile of v3, /device:TPU:0, one launch (start us, length us, event | category | flops | bytes accessed | tf_op | source)
XLA Modules:
  0.0 43.3 jit_solution(14886914953612062808)
XLA Ops:
  0.7 3.1 %collective-permute-start = (bf16[2,64,128]{2,1,0:T(8,128)(2,1)}, bf16[2,64,128]{2,1,0:T(8,128)(2,1)S(1)}, u32[]{:S(2)}, u32[]{:S(2)}) collective-permute-start(bf16[2,64,128]{2,1,0:T(8,128)(2,1)} %bitcast.9), channel_id=1, source_target_pairs={{0,4},{1,5},{2,6},{3,7},{4,0},{5,1},{6,2},{7,3},{8,12},{9,13},{10,... | collective-permute-start | bytes 98312 | tf_op jit(solution)/shard_map/ppermute | solution.py:340
  3.8 0.6 %copy-done.10 = f32[128]{0:T(128)S(1)} copy-done((f32[128]{0:T(128)S(1)}, f32[128]{0:T(128)}, u32[]{:S(2)}) %copy-start.10) | copy-done | bytes 536
  4.5 1.3 %shard_map.147 = (f32[8,128,128]{2,1,0:T(8,128)S(1)}, f32[8,128,128]{2,1,0:T(8,128)S(1)}, bf16[1024,128]{1,0:T(8,128)(2,1)S(1)}, bf16[128,256]{1,0:T(8,128)(2,1)...) custom-call(s32[128]{0:T(128)S(1)} %copy-done.1, ...), custom_call_target="tpu_custom_call" | custom-call | flops 1073741824 | bytes 1048576 | tf_op jit(solution)/shard_map/pallas_call | solution.py:356
  5.9 0.7 %shard_map.148.after_ref.refs_0_ = bf16[256,128]{1,0:T(8,128)(2,1)S(1)} custom-call(s32[32]{0:T(128)S(1)} %copy-done.2, s32[1,128]{1,0:T(1,128)S(1)} %bitcast.12, f32[1,64]{1,0:T(1,128)S(1)} %get-tuple-element.33.gain_ref, bf16[2,64,128]{2,1,0:T(8,128)(2,1)S(1)} %bitcast.10, bf16[2,64,128]{2,1,0:T(8,128)(2,1)S(1)} %collective-permute-done.near_ref, ...), custom_call_target="tpu_custom_call" | custom-call | flops 1048576 | bytes 1048576 | tf_op jit(solution)/shard_map/pallas_call | solution.py:362
  6.6 3.1 %collective-permute-start.1 = (bf16[256,128]{1,0:T(8,128)(2,1)S(1)}, bf16[256,128]{1,0:T(8,128)(2,1)S(1)}, u32[]{:S(2)}, u32[]{:S(2)}) collective-permute-start(bf16[256,128]{1,0:T(8,128)(2,1)S(1)} %shard_map.148.after_ref.refs_0_), channel_id=1, source_target_pairs={{0,8},{1,9},{2,10},{3,11},{4,12},{5,13},{6,14},{7,15},{8,0},{9,1},... | collective-permute-start | bytes 196616 | tf_op jit(solution)/shard_map/ppermute | solution.py:340
  9.7 1.2 %shard_map.149 = (bf16[1024,512]{1,0:T(8,128)(2,1)S(1)}, bf16[256,128]{1,0:T(8,128)(2,1)S(1)}, bf16[32,4096]{1,0:T(8,128)(2,1)S(1)}, bf16[32,1024]{1,0:T(8,128)(2,1)S(1)}) custom-call(bf16[32,64]{1,0:T(8,128)(2,1)S(1)} %bitcast.14, bf16[32,64]{1,0:T(8,128)(2,1)S(1)} %bitcast.15, bf16[1024,128]{1,0:T(8,128)(2,1)S(1)} %copy-done.4, ...), custom_call_target="tpu_custom_call" | custom-call | flops 1073741824 | bytes 1048576 | tf_op jit(solution)/shard_map/pallas_call | solution.py:367
  10.9 1.0 %collective-permute-done.1.refs_1_ = bf16[256,128]{1,0:T(8,128)(2,1)S(1)} collective-permute-done((bf16[256,128]{1,0:T(8,128)(2,1)S(1)}, bf16[256,128]{1,0:T(8,128)(2,1)S(1)}, u32[]{:S(2)}, u32[]{:S(2)}) %collective-permute-start.1) | collective-permute-done | bytes 65568 | tf_op jit(solution)/shard_map/ppermute | solution.py:340
  12.0 1.9 %collective-permute-start.2 = (bf16[512,128]{1,0:T(8,128)(2,1)S(1)}, bf16[512,128]{1,0:T(8,128)(2,1)S(1)}, u32[]{:S(2)}, u32[]{:S(2)}) collective-permute-start(bf16[512,128]{1,0:T(8,128)(2,1)S(1)} %shard_map.150.y0_ref), channel_id=1, source_target_pairs={{0,2},{1,3},{2,0},{3,1},{4,6},{5,7},{6,4},{7,5},{8,10},{9,11},{10,... | collective-permute-start | bytes 393224 | tf_op jit(solution)/shard_map/ppermute | solution.py:340
  13.9 1.6 %collective-permute-start.5 = (bf16[128,512]{1,0:T(8,128)(2,1)S(1)}, bf16[128,512]{1,0:T(8,128)(2,1)S(1)}, u32[]{:S(2)}, u32[]{:S(2)}) collective-permute-start(bf16[128,512]{1,0:T(8,128)(2,1)S(1)} %shard_map.154), channel_id=1, source_target_pairs={{0,4},{1,5},{2,6},{3,7},{4,0},{5,1},{6,2},{7,3},{8,12},{9,13},{10,... | collective-permute-start | bytes 393224 | tf_op jit(solution)/shard_map/ppermute | solution.py:340
  15.5 2.1 %shard_map.151 = (f32[128,1024]{1,0:T(8,128)S(1)}, f32[64,128]{1,0:T(8,128)S(1)}, bf16[512,128]{1,0:T(8,128)(2,1)S(1)}, bf16[128,256]{1,0:T(8,128)(2,1)S(1)}) custom-call(bf16[512,128]{1,0:T(8,128)(2,1)S(1)} %shard_map.150.y0_ref, bf16[512,128]{1,0:T(8,128)(2,1)S(1)} %collective-permute-done.3.y1_ref.refs_1_, ...), custom_call_target="tpu_custom_call" | custom-call | flops 2147483648 | bytes 1048576 | tf_op jit(solution)/shard_map/pallas_call | solution.py:383
  17.6 0.4 collective-permute-done.2.refs_0_
  18.1 1.5 %collective-permute-done.5.across_ref = bf16[128,512]{1,0:T(8,128)(2,1)S(1)} collective-permute-done((bf16[128,512]{1,0:T(8,128)(2,1)S(1)}, bf16[128,512]{1,0:T(8,128)(2,1)S(1)}, u32[]{:S(2)}, u32[]{:S(2)}) %collective-permute-start.5) | collective-permute-done | bytes 131104 | tf_op jit(solution)/shard_map/ppermute | solution.py:340
  19.6 2.1 %shard_map.153 = (f32[8,128,128]{2,1,0:T(8,128)S(1)}, bf16[128,128]{1,0:T(8,128)(2,1)S(1)}, f32[32,64]{1,0:T(8,128)S(1)}, bf16[512,128]{1,0:T(8,128)(2,1)S(1)}, bf16[128,256]{1,0:T(8,128)(2,1)S(1)}) custom-call(bf16[512,128]{1,0:T(8,128)(2,1)S(1)} %shard_map.152.y0_ref, bf16[512,128]{1,0:T(8,128)(2,1)S(1)} %collective-permute-done.4.y1_ref, ...), custom_call_target="tpu_custom_call" | custom-call | flops 2147483648 | bytes 1048576 | tf_op jit(solution)/shard_map/pallas_call | solution.py:390
  21.7 1.7 %shard_map.155.after_ref.own_ref = bf16[416,128]{1,0:T(8,128)(2,1)S(1)} custom-call(bf16[512,128]{1,0:T(8,128)(2,1)S(1)} %get-tuple-element.44.right0_ref, bf16[512,128]{1,0:T(8,128)(2,1)S(1)} %get-tuple-element.45.right1_ref, bf16[128,256]{1,0:T(8,128)(2,1)S(1)} %get-tuple-element.46.own0_ref, bf16[128,256]{1,0:T(8,128)(2,1)S(1)} %get-tuple-element.47.own1_ref, ...), custom_call_target="tpu_custom_call" | custom-call | flops 1073741824 | bytes 1048576 | tf_op jit(solution)/shard_map/pallas_call | solution.py:395
  23.4 3.0 %collective-permute-start.7 = (bf16[416,128]{1,0:T(8,128)(2,1)S(1)}, bf16[416,128]{1,0:T(8,128)(2,1)S(1)}, u32[]{:S(2)}, u32[]{:S(2)}) collective-permute-start(bf16[416,128]{1,0:T(8,128)(2,1)S(1)} %shard_map.155.after_ref.own_ref), channel_id=1, source_target_pairs={{0,8},{1,9},{2,10},{3,11},{4,12},{5,13},{6,14},{7,15},{8,0},{9,1},... | collective-permute-start | bytes 319496 | tf_op jit(solution)/shard_map/ppermute | solution.py:340
  26.4 0.8 %shard_map.156 = (bf16[8,128,128]{2,1,0:T(8,128)(2,1)}, f32[8,128]{1,0:T(8,128)S(1)}) custom-call(f32[8,128,128]{2,1,0:T(8,128)S(1)} %get-tuple-element.32.scale_ref, f32[8,128,128]{2,1,0:T(8,128)S(1)} %get-tuple-element.43.value_ref, bf16[416,128]{1,0:T(8,128)(2,1)S(1)} %shard_map.155.after_ref.own_ref), custom_call_target="tpu_custom_call" | custom-call | flops 1073741824 | bytes 1048576 | tf_op jit(solution)/shard_map/pallas_call | solution.py:398
  27.2 5.2 %collective-permute-done.7.other_ref = bf16[416,128]{1,0:T(8,128)(2,1)S(1)} collective-permute-done((bf16[416,128]{1,0:T(8,128)(2,1)S(1)}, bf16[416,128]{1,0:T(8,128)(2,1)S(1)}, u32[]{:S(2)}, u32[]{:S(2)}) %collective-permute-start.7) | collective-permute-done | bytes 106528 | tf_op jit(solution)/shard_map/ppermute | solution.py:340
  32.3 1.5 %collective-permute-start.10 = (bf16[416,128]{1,0:T(8,128)(2,1)S(1)}, bf16[416,128]{1,0:T(8,128)(2,1)S(1)}, u32[]{:S(2)}, u32[]{:S(2)}) collective-permute-start(bf16[416,128]{1,0:T(8,128)(2,1)S(1)} %shard_map.157.own_ref), channel_id=1, source_target_pairs={{0,6},{1,7},{2,4},{3,5},{4,2},{5,3},{6,0},{7,1},{8,14},{9,15},{10,... | collective-permute-start | bytes 319496 | tf_op jit(solution)/shard_map/ppermute | solution.py:340
  33.8 1.3 %collective-permute-start.9 = (bf16[416,128]{1,0:T(8,128)(2,1)S(1)}, bf16[416,128]{1,0:T(8,128)(2,1)S(1)}, u32[]{:S(2)}, u32[]{:S(2)}) collective-permute-start(bf16[416,128]{1,0:T(8,128)(2,1)S(1)} %shard_map.157.own_ref), channel_id=1, source_target_pairs={{0,4},{1,5},{2,6},{3,7},{4,0},{5,1},{6,2},{7,3},{8,12},{9,13},{10,... | collective-permute-start | bytes 319496 | tf_op jit(solution)/shard_map/ppermute | solution.py:340
  35.1 0.8 %collective-permute-start.8 = (bf16[416,128]{1,0:T(8,128)(2,1)S(1)}, bf16[416,128]{1,0:T(8,128)(2,1)S(1)}, u32[]{:S(2)}, u32[]{:S(2)}) collective-permute-start(bf16[416,128]{1,0:T(8,128)(2,1)S(1)} %shard_map.157.own_ref), channel_id=1, source_target_pairs={{0,2},{1,3},{2,0},{3,1},{4,6},{5,7},{6,4},{7,5},{8,10},{9,11},{10,... | collective-permute-start | bytes 319496 | tf_op jit(solution)/shard_map/ppermute | solution.py:340
  35.9 3.3 %collective-permute-done.10.both_ref = bf16[416,128]{1,0:T(8,128)(2,1)S(1)} collective-permute-done((bf16[416,128]{1,0:T(8,128)(2,1)S(1)}, bf16[416,128]{1,0:T(8,128)(2,1)S(1)}, u32[]{:S(2)}, u32[]{:S(2)}) %collective-permute-start.10) | collective-permute-done | bytes 106528 | tf_op jit(solution)/shard_map/ppermute | solution.py:340
  39.2 0.9 %collective-permute-done.9.across_ref = bf16[416,128]{1,0:T(8,128)(2,1)S(1)} collective-permute-done((bf16[416,128]{1,0:T(8,128)(2,1)S(1)}, bf16[416,128]{1,0:T(8,128)(2,1)S(1)}, u32[]{:S(2)}, u32[]{:S(2)}) %collective-permute-start.9) | collective-permute-done | bytes 106528 | tf_op jit(solution)/shard_map/ppermute | solution.py:340
  40.5 1.4 %collective-permute-done.11.other_ref = bf16[672,128]{1,0:T(8,128)(2,1)S(1)} collective-permute-done((bf16[672,128]{1,0:T(8,128)(2,1)S(1)}, bf16[672,128]{1,0:T(8,128)(2,1)S(1)}, u32[]{:S(2)}, u32[]{:S(2)}) %collective-permute-start.11) | collective-permute-done | bytes 172064 | tf_op jit(solution)/shard_map/ppermute | solution.py:340
  41.9 1.4 %shard_map.159 = (f32[1024,128]{1,0:T(8,128)}, f32[128,128]{1,0:T(8,128)}, f32[32,64]{1,0:T(8,128)}, f32[32,64]{1,0:T(8,128)}) custom-call(bf16[672,128]{1,0:T(8,128)(2,1)S(1)} %shard_map.158.local_ref, bf16[672,128]{1,0:T(8,128)(2,1)S(1)} %collective-permute-done.11.other_ref), custom_call_target="tpu_custom_call" | custom-call | flops 1048576 | bytes 1048576 | tf_op jit(solution)/shard_map/pallas_call | solution.py:403
  (38 shorter events, 0.9 us)
Async XLA Ops:
  0.6 3.1 %copy-start.3 = (bf16[8,128,128]{2,1,0:T(8,128)(2,1)S(1)}, bf16[8,128,128]{2,1,0:T(8,128)(2,1)}, u32[]{:S(2)}) copy-start(bf16[8,128,128]{2,1,0:T(8,128)(2,1)} %cot_ref.1) | copy-start | bytes 786436
  0.6 3.1 %copy-start.5 = (bf16[8,128,128]{2,1,0:T(8,128)(2,1)S(1)}, bf16[8,128,128]{2,1,0:T(8,128)(2,1)}, u32[]{:S(2)}) copy-start(bf16[8,128,128]{2,1,0:T(8,128)(2,1)} %pair_ref.3) | copy-start | bytes 786436
  0.7 3.1 %copy-start.6 = (bf16[128,128]{1,0:T(8,128)(2,1)S(1)}, bf16[128,128]{1,0:T(8,128)(2,1)}, u32[]{:S(2)}) copy-start(bf16[128,128]{1,0:T(8,128)(2,1)} %gate_ref.1) | copy-start | bytes 98308
  0.7 5.2 %collective-permute-start = (bf16[2,64,128]{2,1,0:T(8,128)(2,1)}, bf16[2,64,128]{2,1,0:T(8,128)(2,1)S(1)}, u32[]{:S(2)}, u32[]{:S(2)}) collective-permute-start(bf16[2,64,128]{2,1,0:T(8,128)(2,1)} %bitcast.9), channel_id=1, source_target_pairs={{0,4},{1,5},{2,6},{3,7},{4,0},{5,1},{6,2},{7,3},{8,12},{9,13},{10,... | collective-permute-start | bytes 98312 | tf_op jit(solution)/shard_map/ppermute | solution.py:340
  3.8 0.7 %copy-start.10 = (f32[128]{0:T(128)S(1)}, f32[128]{0:T(128)}, u32[]{:S(2)}) copy-start(f32[128]{0:T(128)} %param.20) | copy-start | bytes 1540
  3.8 0.7 %copy-start.1 = (s32[128]{0:T(128)S(1)}, s32[128]{0:T(128)}, u32[]{:S(2)}) copy-start(s32[128]{0:T(128)} %res_s_ref.1) | copy-start | bytes 1540
  3.8 0.7 %copy-start.2 = (s32[32]{0:T(128)S(1)}, s32[32]{0:T(128)}, u32[]{:S(2)}) copy-start(s32[32]{0:T(128)} %seq_ref.1) | copy-start | bytes 388
  3.8 0.7 %copy-start.9 = (f32[64]{0:T(128)S(1)}, f32[64]{0:T(128)}, u32[]{:S(2)}) copy-start(f32[64]{0:T(128)} %param.16) | copy-start | bytes 772
  4.5 1.4 %copy-start = (bf16[2,128,64]{1,2,0:T(8,128)(2,1)S(1)}, bf16[2,128,64]{1,2,0:T(8,128)(2,1)}, u32[]{:S(2)}) copy-start(bf16[2,128,64]{1,2,0:T(8,128)(2,1)} %param.11) | copy-start | bytes 98308
  4.5 5.2 %copy-start.4 = (bf16[1024,128]{1,0:T(8,128)(2,1)S(1)}, bf16[1024,128]{1,0:T(8,128)(2,1)}, u32[]{:S(2)}) copy-start(bf16[1024,128]{1,0:T(8,128)(2,1)} %out_w_ref.1) | copy-start | bytes 786436
  5.9 3.8 %copy-start.7 = (bf16[64,32]{0,1:T(8,128)(2,1)S(1)}, bf16[64,32]{0,1:T(8,128)(2,1)}, u32[]{:S(2)}) copy-start(bf16[64,32]{0,1:T(8,128)(2,1)} %param.18) | copy-start | bytes 12292
  5.9 3.8 %copy-start.8 = (bf16[64,32]{0,1:T(8,128)(2,1)S(1)}, bf16[64,32]{0,1:T(8,128)(2,1)}, u32[]{:S(2)}) copy-start(bf16[64,32]{0,1:T(8,128)(2,1)} %param.17) | copy-start | bytes 12292
  6.6 5.3 %collective-permute-start.1 = (bf16[256,128]{1,0:T(8,128)(2,1)S(1)}, bf16[256,128]{1,0:T(8,128)(2,1)S(1)}, u32[]{:S(2)}, u32[]{:S(2)}) collective-permute-start(bf16[256,128]{1,0:T(8,128)(2,1)S(1)} %shard_map.148.after_ref.refs_0_), channel_id=1, source_target_pairs={{0,8},{1,9},{2,10},{3,11},{4,12},{5,13},{6,14},{7,15},{8,0},{9,1},... | collective-permute-start | bytes 196616 | tf_op jit(solution)/shard_map/ppermute | solution.py:340
  11.9 2.0 %collective-permute-start.3 = (bf16[512,128]{1,0:T(8,128)(2,1)S(1)}, bf16[512,128]{1,0:T(8,128)(2,1)S(1)}, u32[]{:S(2)}, u32[]{:S(2)}) collective-permute-start(bf16[512,128]{1,0:T(8,128)(2,1)S(1)} %shard_map.150.y0_ref), channel_id=1, source_target_pairs={{0,1},{1,0},{2,3},{3,2},{4,5},{5,4},{6,7},{7,6},{8,9},{9,8},{10,11... | collective-permute-start | bytes 393224 | tf_op jit(solution)/shard_map/ppermute | solution.py:340
  12.0 6.0 %collective-permute-start.2 = (bf16[512,128]{1,0:T(8,128)(2,1)S(1)}, bf16[512,128]{1,0:T(8,128)(2,1)S(1)}, u32[]{:S(2)}, u32[]{:S(2)}) collective-permute-start(bf16[512,128]{1,0:T(8,128)(2,1)S(1)} %shard_map.150.y0_ref), channel_id=1, source_target_pairs={{0,2},{1,3},{2,0},{3,1},{4,6},{5,7},{6,4},{7,5},{8,10},{9,11},{10,... | collective-permute-start | bytes 393224 | tf_op jit(solution)/shard_map/ppermute | solution.py:340
  13.9 5.6 %collective-permute-start.5 = (bf16[128,512]{1,0:T(8,128)(2,1)S(1)}, bf16[128,512]{1,0:T(8,128)(2,1)S(1)}, u32[]{:S(2)}, u32[]{:S(2)}) collective-permute-start(bf16[128,512]{1,0:T(8,128)(2,1)S(1)} %shard_map.154), channel_id=1, source_target_pairs={{0,4},{1,5},{2,6},{3,7},{4,0},{5,1},{6,2},{7,3},{8,12},{9,13},{10,... | collective-permute-start | bytes 393224 | tf_op jit(solution)/shard_map/ppermute | solution.py:340
  18.0 1.6 %collective-permute-start.4 = (bf16[512,128]{1,0:T(8,128)(2,1)S(1)}, bf16[512,128]{1,0:T(8,128)(2,1)S(1)}, u32[]{:S(2)}, u32[]{:S(2)}) collective-permute-start(bf16[512,128]{1,0:T(8,128)(2,1)S(1)} %shard_map.152.y0_ref), channel_id=1, source_target_pairs={{0,1},{1,0},{2,3},{3,2},{4,5},{5,4},{6,7},{7,6},{8,9},{9,8},{10,11... | collective-permute-start | bytes 393224 | tf_op jit(solution)/shard_map/ppermute | solution.py:340
  19.5 2.1 %collective-permute-start.6 = (bf16[128,512]{1,0:T(8,128)(2,1)S(1)}, bf16[128,512]{1,0:T(8,128)(2,1)S(1)}, u32[]{:S(2)}, u32[]{:S(2)}) collective-permute-start(bf16[128,512]{1,0:T(8,128)(2,1)S(1)} %pad_maximum_fusion), channel_id=1, source_target_pairs={{0,1},{1,0},{2,3},{3,2},{4,5},{5,4},{6,7},{7,6},{8,9},{9,8},{10,11... | collective-permute-start | bytes 393224 | tf_op jit(solution)/shard_map/ppermute | solution.py:340
  23.4 8.9 %collective-permute-start.7 = (bf16[416,128]{1,0:T(8,128)(2,1)S(1)}, bf16[416,128]{1,0:T(8,128)(2,1)S(1)}, u32[]{:S(2)}, u32[]{:S(2)}) collective-permute-start(bf16[416,128]{1,0:T(8,128)(2,1)S(1)} %shard_map.155.after_ref.own_ref), channel_id=1, source_target_pairs={{0,8},{1,9},{2,10},{3,11},{4,12},{5,13},{6,14},{7,15},{8,0},{9,1},... | collective-permute-start | bytes 319496 | tf_op jit(solution)/shard_map/ppermute | solution.py:340
  32.3 6.8 %collective-permute-start.10 = (bf16[416,128]{1,0:T(8,128)(2,1)S(1)}, bf16[416,128]{1,0:T(8,128)(2,1)S(1)}, u32[]{:S(2)}, u32[]{:S(2)}) collective-permute-start(bf16[416,128]{1,0:T(8,128)(2,1)S(1)} %shard_map.157.own_ref), channel_id=1, source_target_pairs={{0,6},{1,7},{2,4},{3,5},{4,2},{5,3},{6,0},{7,1},{8,14},{9,15},{10,... | collective-permute-start | bytes 319496 | tf_op jit(solution)/shard_map/ppermute | solution.py:340
  33.8 6.3 %collective-permute-start.9 = (bf16[416,128]{1,0:T(8,128)(2,1)S(1)}, bf16[416,128]{1,0:T(8,128)(2,1)S(1)}, u32[]{:S(2)}, u32[]{:S(2)}) collective-permute-start(bf16[416,128]{1,0:T(8,128)(2,1)S(1)} %shard_map.157.own_ref), channel_id=1, source_target_pairs={{0,4},{1,5},{2,6},{3,7},{4,0},{5,1},{6,2},{7,3},{8,12},{9,13},{10,... | collective-permute-start | bytes 319496 | tf_op jit(solution)/shard_map/ppermute | solution.py:340
  35.1 5.3 %collective-permute-start.8 = (bf16[416,128]{1,0:T(8,128)(2,1)S(1)}, bf16[416,128]{1,0:T(8,128)(2,1)S(1)}, u32[]{:S(2)}, u32[]{:S(2)}) collective-permute-start(bf16[416,128]{1,0:T(8,128)(2,1)S(1)} %shard_map.157.own_ref), channel_id=1, source_target_pairs={{0,2},{1,3},{2,0},{3,1},{4,6},{5,7},{6,4},{7,5},{8,10},{9,11},{10,... | collective-permute-start | bytes 319496 | tf_op jit(solution)/shard_map/ppermute | solution.py:340
  40.4 1.5 %collective-permute-start.11 = (bf16[672,128]{1,0:T(8,128)(2,1)S(1)}, bf16[672,128]{1,0:T(8,128)(2,1)S(1)}, u32[]{:S(2)}, u32[]{:S(2)}) collective-permute-start(bf16[672,128]{1,0:T(8,128)(2,1)S(1)} %shard_map.158.local_ref), channel_id=1, source_target_pairs={{0,1},{1,0},{2,3},{3,2},{4,5},{5,4},{6,7},{7,6},{8,9},{9,8},{10,11... | collective-permute-start | bytes 516104 | tf_op jit(solution)/shard_map/ppermute | solution.py:340

commit v4 on v3

--- a/solution.py
+++ b/solution.py
@@ -35,13 +35,15 @@
     out_ref[...] = jnp.zeros_like(out_ref)
 
 
-def norm_kernel(seq_ref, res_ref, gain_ref, own_ref, near_ref, after_ref, out_ref):
+def norm_kernel(
+    seq_ref, res_ref, gain_ref, own_ref, near_ref, core_ref, across_ref, out_ref, to_core_ref, to_across_ref
+):
     row = lax.axis_index("row")
     n = res_ref.shape[1]
     res = res_ref[...].astype(F32)
     gain = gain_ref[...]
     gain = jnp.concatenate([gain, gain], axis=1)
-    for at, (state_ref, first) in enumerate(((own_ref, row * 2), (near_ref, (row ^ 4) * 2))):
+    for at, (state_ref, first) in enumerate(((own_ref, row * 2), (near_ref, (row ^ 8) * 2))):
         halves = []
         for s in range(2):
             value = state_ref[s].astype(F32)
@@ -50,7 +52,11 @@
             seq = seq_ref[first + s].astype(F32)
             halves.append(centred * (lax.rsqrt(variance + 1e-05) * (res * seq)))
         turned = jnp.concatenate(halves, axis=0).T
-        out_ref[at * n : (at + 1) * n, :] = (turned * gain).astype(BF16)
+        value = (turned * gain).astype(BF16)
+        for ref in (out_ref, to_core_ref, to_across_ref):
+            ref[at * n : (at + 1) * n, :] = value
+    to_core_ref[2 * n :, :] = core_ref[...]
+    to_across_ref[2 * n :, :] = across_ref[...]
 
 
 def gate_kernel(
@@ -75,7 +81,7 @@
     place = jnp.where(
         (src // n == (dst % n) // CHANS) & (src % n == chan), 1.0, 0.0
     ).astype(BF16)
-    outs = ((own_ref, 0), (core_ref, 0), (across_ref, 0), (across_ref, 2 * n))
+    outs = ((own_ref, 0), (core_ref, 0), (across_ref, 0), (across_ref, 2))
     for half in range(rows // QUAD):
         for k in range(QUAD):
             i = half * QUAD + k
@@ -90,7 +96,7 @@
         packed = dot(full_ref[:, half * wide : (half + 1) * wide], place).astype(BF16)
         for m in range(QUAD):
             out_ref, at = outs[m]
-            out_ref[:, at + half * n : at + (half + 1) * n] = packed[:, m * n : (m + 1) * n]
+            out_ref[(at + half) * n : (at + half + 1) * n, :] = packed[:, m * n : (m + 1) * n]
 
 
 def weight_kernel(
@@ -145,7 +151,7 @@
     row = lax.axis_index("row")
     n = ys[0].shape[1]
     chans, width = 64, 32
-    slots = [y[t * n : (t + 1) * n, :] for y in ys for t in range(4)]
+    slots = [y[t * n : (t + 1) * n, :] for y in ys for t in range(2)]
     right = dot(jnp.concatenate(slots, axis=1), kron_ref[...]).astype(BF16)
     right_t_ref[...] = right.T
     at = iota((32, n), 0)
@@ -194,30 +200,29 @@
             flat_ref[s * width : (s + 1) * width, t * n : (t + 1) * n] = right_ref[
                 pl.ds(2 * t + s, width, stride=GROUP), :
             ].astype(BF16)
-    half = 4 * n
-    act = dot(flat_ref[:, :half], ys[0][...]) + dot(flat_ref[:, half:], ys[1][...])
+    act = sum(dot(flat_ref[:, k * 2 * n : (k + 1) * 2 * n], y[: 2 * n, :]) for k, y in enumerate(ys))
     return linear, act
 
 
 def half_kernel(
-    y0_ref, y1_ref, turned_ref, kron_ref, block_ref, wide_ref, bias_ref,
+    y0_ref, y1_ref, y2_ref, y3_ref, turned_ref, kron_ref, block_ref, wide_ref, bias_ref,
     linear_ref, act_ref, right_t_ref, own_ref, *scratch
 ):
     linear, act = half_of_rows(
-        (y0_ref, y1_ref), turned_ref, kron_ref, block_ref, wide_ref, right_t_ref, own_ref, scratch
+        (y0_ref, y1_ref, y2_ref, y3_ref), turned_ref, kron_ref, block_ref, wide_ref, right_t_ref, own_ref, scratch
     )
     linear_ref[...] = linear + jnp.concatenate([bias_ref[...]] * 8, axis=1)
     act_ref[...] = act
 
 
 def pair_kernel(
-    y0_ref, y1_ref, turned_ref, kron_ref, block_ref, wide_ref,
+    y0_ref, y1_ref, y2_ref, y3_ref, turned_ref, kron_ref, block_ref, wide_ref,
     linear_ref, act_ref, slope_ref, pair_ref,
     value_ref, gate_ref, grad_right_ref, right_t_ref, own_ref, slope_s_ref, *scratch
 ):
     rows, n, _ = pair_ref.shape
     linear, act = half_of_rows(
-        (y0_ref, y1_ref), turned_ref, kron_ref, block_ref, wide_ref, right_t_ref, own_ref, scratch
+        (y0_ref, y1_ref, y2_ref, y3_ref), turned_ref, kron_ref, block_ref, wide_ref, right_t_ref, own_ref, scratch
     )
     for i in range(rows):
         value = linear[:, i * n : (i + 1) * n] + linear_ref[:, i * n : (i + 1) * n]
@@ -238,15 +243,16 @@
 
 
 def out_kernel(
-    right0_ref, right1_ref, own0_ref, own1_ref, own_ref, core_ref, across_ref,
+    right0_ref, right1_ref, own0_ref, own1_ref, own_ref, core_ref, across_ref, both_ref,
     part_ref, left_ref, gate_ref, grad_right_ref,
     sums_ref, n_ref
 ):
     n = gate_ref.shape[0]
     chans, width = 64, 32
     half = 8 * GROUP
-    grads = (own_ref[...], core_ref[:, : 2 * n], across_ref[:, : 2 * n], core_ref[:, 2 * n :])
-    for f2, grad in enumerate(grads):
+    grads = ((own_ref, 0), (core_ref, 2), (across_ref, 2), (both_ref, 4))
+    for f2, (ref, at) in enumerate(grads):
+        grad = jnp.concatenate([ref[(at + k) * n : (at + k + 1) * n, :] for k in range(2)], axis=1)
         for g, right_ref in enumerate((right0_ref, right1_ref)):
             part = dot(right_ref[...], grad).astype(BF16)
             for fl in range(2):
@@ -349,32 +355,30 @@
     res = residue_mask.reshape(1, n)
     seq = sequence_row_mask.reshape(1, -1)
     state = alignment_state.transpose(0, 2, 1)
-    near = swap(state, 4, size)
+    near = swap(state, 8, size)
     (token,) = call(first_kernel, [((8, n), F32)], flops=20 << 30)()
     gain = norm_gain_vector.reshape(1, -1)
     bias = output_bias.reshape(1, n)
     scale, slope, turned, own, core, across, gain, bias = call(
         gate_kernel,
-        [((rows, n, n), F32), ((rows, n, n), F32), ((rows * n, n), BF16)] + [((n, 2 * n), BF16)] * 2
-        + [((n, 4 * n), BF16), (gain.shape, F32), (bias.shape, F32)],
+        [((rows, n, n), F32), ((rows, n, n), F32), ((rows * n, n), BF16)] + [((2 * n, n), BF16)] * 2
+        + [((4 * n, n), BF16), (gain.shape, F32), (bias.shape, F32)],
         scratch=[((n, rows * n), BF16)], smem=1, ins=9, flops=1 << 30, vmem=12,
     )(residue_mask, seq, res, pair_state, cotangent, gate_matrix, gain, bias, token)
-    (pair,) = call(norm_kernel, [((2 * n, n), BF16)], smem=1, ins=6)(
-        sequence_row_mask, res, gain, state, near, own
-    )
-    far = swap(pair, 8, size)
+    pair, to_core, to_across = call(
+        norm_kernel, [((2 * n, n), BF16), ((4 * n, n), BF16), ((6 * n, n), BF16)], smem=1, ins=7
+    )(sequence_row_mask, res, gain, state, near, core, across)
+    beside, ahead, corner = swap(pair, 2, size), swap(to_across, ACROSS, size), swap(pair, 2 ^ ACROSS, size)
     left_t = left_matrix_weight.T
     kron, block, wide, part = call(
         weight_kernel,
         [((1024, 512), BF16), ((256, n), BF16), ((32, 32 * n), BF16), ((32, 8 * n), BF16)],
         scratch=[((1024, n), F32)], ins=4, flops=1 << 30, vmem=12,
     )(right_matrix_weight.T, left_t, output_weight, pair)
-    (y0,) = call(tie_kernel, [((4 * n, n), BF16)], ins=3)(pair, far, block)
-    y1 = swap(y0, 2, size)
-    y2 = swap(y0, 1, size)
-    (across,) = call(tie_kernel, [((n, 4 * n), BF16)], ins=2)(across, y2)
-    across = swap(across, ACROSS, size)
-    core = swap(jnp.concatenate([core, across[:, 2 * n :]], axis=1), 1, size)
+    (beside,) = call(tie_kernel, [((2 * n, n), BF16)], ins=2)(beside, block)
+    pair_core, beside_core, corner_core, ahead_core = (
+        swap(y, 1, size) for y in (to_core, beside, corner, ahead)
+    )
     scratch = [
         ((512, rows * n), BF16), ((2, n, n), F32), ((512, n), F32), ((64, 8 * n), BF16),
     ]
@@ -383,18 +387,16 @@
     linear, act, right0, own0 = call(
         half_kernel,
         [((n, rows * n), F32), ((64, n), F32), *kept],
-        scratch=scratch, ins=7, flops=2 << 30, vmem=24,
-    )(y0, y2, *shared, bias)
-    (y1,) = call(tie_kernel, [((4 * n, n), BF16)], ins=2)(y1, act)
-    y3 = swap(y1, 1, size)
+        scratch=scratch, ins=9, flops=2 << 30, vmem=24,
+    )(pair, pair_core, beside, beside_core, *shared, bias)
     value, gate_sum, right_sum, right1, own1 = call(
         pair_kernel,
         [((rows, n, n), F32), ((n, n), BF16), ((32, 64), F32), *kept],
-        scratch=[((rows * n, n), BF16), *scratch], ins=10, flops=2 << 30, vmem=24,
-    )(y1, y3, *shared, linear, act, slope, pair_state)
+        scratch=[((rows * n, n), BF16), *scratch], ins=12, flops=2 << 30, vmem=24,
+    )(corner, corner_core, ahead, ahead_core, *shared, linear, act, slope, pair_state)
     (sums,) = call(
-        out_kernel, [((416, n), BF16)], scratch=[((256, 32 * n), BF16)], ins=11, flops=1 << 30, vmem=24,
-    )(right0, right1, own0, own1, own, core, across, part, left_t, gate_sum, right_sum)
+        out_kernel, [((416, n), BF16)], scratch=[((256, 32 * n), BF16)], ins=12, flops=1 << 30, vmem=24,
+    )(right0, right1, own0, own1, own, pair_core, ahead, ahead_core, part, left_t, gate_sum, right_sum)
     update, token = call(update_kernel, [((rows, n, n), BF16), ((8, n), F32)], ins=3, flops=1 << 30, vmem=8)(scale, value, sums)
     (sums,) = call(add_kernel, [((416, n), BF16)], ins=3)(sums, swap(sums, 8, size), token)
     others = [swap(sums, step, size) for step in (2, ACROSS, 2 ^ ACROSS)]

time: 43.4 us -> 41.3 us (0.952)
  starting transfers between devices: 16.6 us -> 14.5 us
    ppermute x12 -> x13, starting transfers between devices: 16.6 us -> 14.5 us  [swap(): return lax.ppermute(x, 'row', [(i, i ^ bit) for i in range(size)])]
    ppermute x12 -> x13, waiting for transfers between devices: 13.9 us -> 13.9 us  [swap(): return lax.ppermute(x, 'row', [(i, i ^ bit) for i in range(size)])]
  transfers between devices with their start and end apart: 12 -> 13, of which waited for: 9 -> 8; matrix products, arithmetic and copies ran while one was open for 0% -> 0% of each run, Pallas kernels for 17% -> 13%
where the time goes in v4:
time: 41.3 us; the launch traced here: 41.2 us
  starting transfers between devices  14.5 us (35%)
  waiting for transfers between devices  13.9 us (34%)
  Pallas kernels  11.2 us (27%)
  between operations  0.81 us (2%)
  local copies, waits for them, and re-layouts  0.69 us (2%)
    ppermute x13, starting transfers between devices, swap(): return lax.ppermute(x, 'row', [(i, i ^ bit) for i in range(size)])  14.5 us
    ppermute x13, waiting for transfers between devices, swap(): return lax.ppermute(x, 'row', [(i, i ^ bit) for i in range(size)])  13.9 us
    pallas_call x1, Pallas kernels, one_column(): call(half_kernel, [((n, rows * n), F32), ((64, n), F32), *kept], scratch=...  2.07 us
    pallas_call x1, Pallas kernels, one_column(): call(pair_kernel, [((rows, n, n), F32), ((n, n), BF16), ((32, 64), F32),...  2.05 us
    pallas_call x1, Pallas kernels, one_column(): call(out_kernel, [((416, n), BF16)], scratch=[((256, 32 * n), BF16)], ins...  1.67 us
    pallas_call x1, Pallas kernels, one_column(): call(last_kernel, [((1024, n), F32), ((n, n), F32), ((32, 64), F32), ((32...  1.38 us
    pallas_call x1, Pallas kernels, one_column(): call(gate_kernel, [((rows, n, n), F32), ((rows, n, n), F32), ((rows * n,...  1.32 us
    pallas_call x1, Pallas kernels, one_column(): call(weight_kernel, [((1024, 512), BF16), ((256, n), BF16), ((32, 32 * n)...  1.22 us
  transfers between devices with their start and end apart: 13, of which 8 were waited for; matrix products, arithmetic and copies ran while one was open for 0% of the time, Pallas kernels for 13%

profile of v4, /device:TPU:0, one launch (start us, length us, event | category | flops | bytes accessed | tf_op | source)
XLA Modules:
  0.0 41.2 jit_solution(13397252076445158550)
XLA Ops:
  0.7 4.1 %collective-permute-start = (bf16[2,64,128]{2,1,0:T(8,128)(2,1)}, bf16[2,64,128]{2,1,0:T(8,128)(2,1)S(1)}, u32[]{:S(2)}, u32[]{:S(2)}) collective-permute-start(bf16[2,64,128]{2,1,0:T(8,128)(2,1)} %bitcast.9), channel_id=1, source_target_pairs={{0,8},{1,9},{2,10},{3,11},{4,12},{5,13},{6,14},{7,15},{8,0},{9,1},... | collective-permute-start | bytes 98312 | tf_op jit(solution)/shard_map/ppermute | solution.py:346
  4.8 0.6 %copy-done.10 = f32[128]{0:T(128)S(1)} copy-done((f32[128]{0:T(128)S(1)}, f32[128]{0:T(128)}, u32[]{:S(2)}) %copy-start.10) | copy-done | bytes 536
  5.5 1.3 %shard_map.147 = (f32[8,128,128]{2,1,0:T(8,128)S(1)}, f32[8,128,128]{2,1,0:T(8,128)S(1)}, bf16[1024,128]{1,0:T(8,128)(2,1)S(1)}, bf16[256,128]{1,0:T(8,128)(2,1)...) custom-call(s32[128]{0:T(128)S(1)} %copy-done.1, ...), custom_call_target="tpu_custom_call" | custom-call | flops 1073741824 | bytes 1048576 | tf_op jit(solution)/shard_map/pallas_call | solution.py:362
  7.2 0.7 %shard_map.148 = (bf16[256,128]{1,0:T(8,128)(2,1)S(1)}, bf16[512,128]{1,0:T(8,128)(2,1)S(1)}, bf16[768,128]{1,0:T(8,128)(2,1)S(1)}) custom-call(s32[32]{0:T(128)S(1)} %copy-done.2, s32[1,128]{1,0:T(1,128)S(1)} %bitcast.12, f32[1,64]{1,0:T(1,128)S(1)} %get-tuple-element.36.gain_ref, bf16[2,64,128]{2,1,0:T(8,128)(2,1)S(1)} %bitcast.10, ...), custom_call_target="tpu_custom_call" | custom-call | flops 1048576 | bytes 1048576 | tf_op jit(solution)/shard_map/pallas_call | solution.py:368
  7.9 1.6 %collective-permute-start.3 = (bf16[768,128]{1,0:T(8,128)(2,1)S(1)}, bf16[768,128]{1,0:T(8,128)(2,1)S(1)}, u32[]{:S(2)}, u32[]{:S(2)}) collective-permute-start(bf16[768,128]{1,0:T(8,128)(2,1)S(1)} %get-tuple-element.40), channel_id=1, source_target_pairs={{0,4},{1,5},{2,6},{3,7},{4,0},{5,1},{6,2},{7,3},{8,12},{9,13},{10,... | collective-permute-start | bytes 589832 | tf_op jit(solution)/shard_map/ppermute | solution.py:346
  9.5 1.5 %collective-permute-start.6 = (bf16[256,128]{1,0:T(8,128)(2,1)S(1)}, bf16[256,128]{1,0:T(8,128)(2,1)S(1)}, u32[]{:S(2)}, u32[]{:S(2)}) collective-permute-start(bf16[256,128]{1,0:T(8,128)(2,1)S(1)} %get-tuple-element.39.after_ref.y0_ref), channel_id=1, source_target_pairs={{0,2},{1,3},{2,0},{3,1},{4,6},{5,7},{6,4},{7,5},{8,10},{9,11},{10,... | collective-permute-start | bytes 196616 | tf_op jit(solution)/shard_map/ppermute | solution.py:346
  11.0 0.4 %collective-permute-start.1 = (bf16[256,128]{1,0:T(8,128)(2,1)S(1)}, bf16[256,128]{1,0:T(8,128)(2,1)S(1)}, u32[]{:S(2)}, u32[]{:S(2)}) collective-permute-start(bf16[256,128]{1,0:T(8,128)(2,1)S(1)} %get-tuple-element.39.after_ref.y0_ref), channel_id=1, source_target_pairs={{0,6},{1,7},{2,4},{3,5},{4,2},{5,3},{6,0},{7,1},{8,14},{9,15},{10,... | collective-permute-start | bytes 196616 | tf_op jit(solution)/shard_map/ppermute | solution.py:346
  11.5 1.2 %shard_map.149 = (bf16[1024,512]{1,0:T(8,128)(2,1)S(1)}, bf16[256,128]{1,0:T(8,128)(2,1)S(1)}, bf16[32,4096]{1,0:T(8,128)(2,1)S(1)}, bf16[32,1024]{1,0:T(8,128)(2,1)S(1)}) custom-call(bf16[32,64]{1,0:T(8,128)(2,1)S(1)} %bitcast.14, bf16[32,64]{1,0:T(8,128)(2,1)S(1)} %bitcast.15, bf16[1024,128]{1,0:T(8,128)(2,1)S(1)} %copy-done.4, ...), custom_call_target="tpu_custom_call" | custom-call | flops 1073741824 | bytes 1048576 | tf_op jit(solution)/shard_map/pallas_call | solution.py:373
  12.7 1.8 %collective-permute-done.6.refs_0_ = bf16[256,128]{1,0:T(8,128)(2,1)S(1)} collective-permute-done((bf16[256,128]{1,0:T(8,128)(2,1)S(1)}, bf16[256,128]{1,0:T(8,128)(2,1)S(1)}, u32[]{:S(2)}, u32[]{:S(2)}) %collective-permute-start.6) | collective-permute-done | bytes 65568 | tf_op jit(solution)/shard_map/ppermute | solution.py:346
  14.5 1.8 %collective-permute-done.1.y0_ref = bf16[256,128]{1,0:T(8,128)(2,1)S(1)} collective-permute-done((bf16[256,128]{1,0:T(8,128)(2,1)S(1)}, bf16[256,128]{1,0:T(8,128)(2,1)S(1)}, u32[]{:S(2)}, u32[]{:S(2)}) %collective-permute-start.1) | collective-permute-done | bytes 65568 | tf_op jit(solution)/shard_map/ppermute | solution.py:346
  16.3 0.5 %collective-permute-start.4 = (bf16[768,128]{1,0:T(8,128)(2,1)S(1)}, bf16[768,128]{1,0:T(8,128)(2,1)S(1)}, u32[]{:S(2)}, u32[]{:S(2)}) collective-permute-start(bf16[768,128]{1,0:T(8,128)(2,1)S(1)} %collective-permute-done.3.y2_ref.across_ref), channel_id=1, source_target_pairs={{0,1},{1,0},{2,3},{3,2},{4,5},{5,4},{6,7},{7,6},{8,9},{9,8},{10,11... | collective-permute-start | bytes 589832 | tf_op jit(solution)/shard_map/ppermute | solution.py:346
  16.8 2.1 %shard_map.151 = (f32[128,1024]{1,0:T(8,128)S(1)}, f32[64,128]{1,0:T(8,128)S(1)}, bf16[512,128]{1,0:T(8,128)(2,1)S(1)}, bf16[128,256]{1,0:T(8,128)(2,1)S(1)}) custom-call(bf16[256,128]{1,0:T(8,128)(2,1)S(1)} %get-tuple-element.39.after_ref.y0_ref, bf16[512,128]{1,0:T(8,128)(2,1)S(1)} %collective-permute-done.5.y1_ref.core_ref, ...), custom_call_target="tpu_custom_call" | custom-call | flops 2147483648 | bytes 1048576 | tf_op jit(solution)/shard_map/pallas_call | solution.py:387
  18.9 2.1 %shard_map.152 = (f32[8,128,128]{2,1,0:T(8,128)S(1)}, bf16[128,128]{1,0:T(8,128)(2,1)S(1)}, f32[32,64]{1,0:T(8,128)S(1)}, bf16[512,128]{1,0:T(8,128)(2,1)S(1)}, bf16[128,256]{1,0:T(8,128)(2,1)S(1)}) custom-call(bf16[256,128]{1,0:T(8,128)(2,1)S(1)} %collective-permute-done.1.y0_ref, bf16[256,128]{1,0:T(8,128)(2,1)S(1)} %collective-permute-done.2.y1_ref, ...), custom_call_target="tpu_custom_call" | custom-call | flops 2147483648 | bytes 1048576 | tf_op jit(solution)/shard_map/pallas_call | solution.py:392
  21.0 1.7 %shard_map.153.after_ref.own_ref = bf16[416,128]{1,0:T(8,128)(2,1)S(1)} custom-call(bf16[512,128]{1,0:T(8,128)(2,1)S(1)} %get-tuple-element.51.right0_ref, bf16[512,128]{1,0:T(8,128)(2,1)S(1)} %get-tuple-element.52.right1_ref, bf16[128,256]{1,0:T(8,128)(2,1)S(1)} %get-tuple-element.53.own0_ref, bf16[128,256]{1,0:T(8,128)(2,1)S(1)} %get-tuple-element.54.own1_ref, ...), custom_call_target="tpu_custom_call" | custom-call | flops 1073741824 | bytes 1048576 | tf_op jit(solution)/shard_map/pallas_call | solution.py:397
  22.6 2.7 %collective-permute-start.8 = (bf16[416,128]{1,0:T(8,128)(2,1)S(1)}, bf16[416,128]{1,0:T(8,128)(2,1)S(1)}, u32[]{:S(2)}, u32[]{:S(2)}) collective-permute-start(bf16[416,128]{1,0:T(8,128)(2,1)S(1)} %shard_map.153.after_ref.own_ref), channel_id=1, source_target_pairs={{0,8},{1,9},{2,10},{3,11},{4,12},{5,13},{6,14},{7,15},{8,0},{9,1},... | collective-permute-start | bytes 319496 | tf_op jit(solution)/shard_map/ppermute | solution.py:346
  25.4 0.8 %shard_map.154 = (bf16[8,128,128]{2,1,0:T(8,128)(2,1)}, f32[8,128]{1,0:T(8,128)S(1)}) custom-call(f32[8,128,128]{2,1,0:T(8,128)S(1)} %get-tuple-element.35.scale_ref, f32[8,128,128]{2,1,0:T(8,128)S(1)} %get-tuple-element.50.value_ref, bf16[416,128]{1,0:T(8,128)(2,1)S(1)} %shard_map.153.after_ref.own_ref), custom_call_target="tpu_custom_call" | custom-call | flops 1073741824 | bytes 1048576 | tf_op jit(solution)/shard_map/pallas_call | solution.py:400
  26.1 4.7 %collective-permute-done.8.other_ref = bf16[416,128]{1,0:T(8,128)(2,1)S(1)} collective-permute-done((bf16[416,128]{1,0:T(8,128)(2,1)S(1)}, bf16[416,128]{1,0:T(8,128)(2,1)S(1)}, u32[]{:S(2)}, u32[]{:S(2)}) %collective-permute-start.8) | collective-permute-done | bytes 106528 | tf_op jit(solution)/shard_map/ppermute | solution.py:346
  30.9 0.5 %collective-permute-start.11 = (bf16[416,128]{1,0:T(8,128)(2,1)S(1)}, bf16[416,128]{1,0:T(8,128)(2,1)S(1)}, u32[]{:S(2)}, u32[]{:S(2)}) collective-permute-start(bf16[416,128]{1,0:T(8,128)(2,1)S(1)} %shard_map.155.own_ref), channel_id=1, source_target_pairs={{0,6},{1,7},{2,4},{3,5},{4,2},{5,3},{6,0},{7,1},{8,14},{9,15},{10,... | collective-permute-start | bytes 319496 | tf_op jit(solution)/shard_map/ppermute | solution.py:346
  31.3 1.6 %collective-permute-start.10 = (bf16[416,128]{1,0:T(8,128)(2,1)S(1)}, bf16[416,128]{1,0:T(8,128)(2,1)S(1)}, u32[]{:S(2)}, u32[]{:S(2)}) collective-permute-start(bf16[416,128]{1,0:T(8,128)(2,1)S(1)} %shard_map.155.own_ref), channel_id=1, source_target_pairs={{0,4},{1,5},{2,6},{3,7},{4,0},{5,1},{6,2},{7,3},{8,12},{9,13},{10,... | collective-permute-start | bytes 319496 | tf_op jit(solution)/shard_map/ppermute | solution.py:346
  32.9 1.5 %collective-permute-start.9 = (bf16[416,128]{1,0:T(8,128)(2,1)S(1)}, bf16[416,128]{1,0:T(8,128)(2,1)S(1)}, u32[]{:S(2)}, u32[]{:S(2)}) collective-permute-start(bf16[416,128]{1,0:T(8,128)(2,1)S(1)} %shard_map.155.own_ref), channel_id=1, source_target_pairs={{0,2},{1,3},{2,0},{3,1},{4,6},{5,7},{6,4},{7,5},{8,10},{9,11},{10,... | collective-permute-start | bytes 319496 | tf_op jit(solution)/shard_map/ppermute | solution.py:346
  34.4 2.8 %collective-permute-done.11.both_ref = bf16[416,128]{1,0:T(8,128)(2,1)S(1)} collective-permute-done((bf16[416,128]{1,0:T(8,128)(2,1)S(1)}, bf16[416,128]{1,0:T(8,128)(2,1)S(1)}, u32[]{:S(2)}, u32[]{:S(2)}) %collective-permute-start.11) | collective-permute-done | bytes 106528 | tf_op jit(solution)/shard_map/ppermute | solution.py:346
  37.4 0.9 %collective-permute-done.9.beside_ref = bf16[416,128]{1,0:T(8,128)(2,1)S(1)} collective-permute-done((bf16[416,128]{1,0:T(8,128)(2,1)S(1)}, bf16[416,128]{1,0:T(8,128)(2,1)S(1)}, u32[]{:S(2)}, u32[]{:S(2)}) %collective-permute-start.9) | collective-permute-done | bytes 106528 | tf_op jit(solution)/shard_map/ppermute | solution.py:346
  38.4 1.4 %collective-permute-done.12.other_ref = bf16[672,128]{1,0:T(8,128)(2,1)S(1)} collective-permute-done((bf16[672,128]{1,0:T(8,128)(2,1)S(1)}, bf16[672,128]{1,0:T(8,128)(2,1)S(1)}, u32[]{:S(2)}, u32[]{:S(2)}) %collective-permute-start.12) | collective-permute-done | bytes 172064 | tf_op jit(solution)/shard_map/ppermute | solution.py:346
  39.8 1.4 %shard_map.157 = (f32[1024,128]{1,0:T(8,128)}, f32[128,128]{1,0:T(8,128)}, f32[32,64]{1,0:T(8,128)}, f32[32,64]{1,0:T(8,128)}) custom-call(bf16[672,128]{1,0:T(8,128)(2,1)S(1)} %shard_map.156.local_ref, bf16[672,128]{1,0:T(8,128)(2,1)S(1)} %collective-permute-done.12.other_ref), custom_call_target="tpu_custom_call" | custom-call | flops 1048576 | bytes 1048576 | tf_op jit(solution)/shard_map/pallas_call | solution.py:405
  (36 shorter events, 0.9 us)
Async XLA Ops:
  0.6 4.2 %copy-start.3 = (bf16[8,128,128]{2,1,0:T(8,128)(2,1)S(1)}, bf16[8,128,128]{2,1,0:T(8,128)(2,1)}, u32[]{:S(2)}) copy-start(bf16[8,128,128]{2,1,0:T(8,128)(2,1)} %cot_ref.1) | copy-start | bytes 786436
  0.6 4.2 %copy-start.5 = (bf16[8,128,128]{2,1,0:T(8,128)(2,1)S(1)}, bf16[8,128,128]{2,1,0:T(8,128)(2,1)}, u32[]{:S(2)}) copy-start(bf16[8,128,128]{2,1,0:T(8,128)(2,1)} %pair_ref.3) | copy-start | bytes 786436
  0.7 4.2 %copy-start.6 = (bf16[128,128]{1,0:T(8,128)(2,1)S(1)}, bf16[128,128]{1,0:T(8,128)(2,1)}, u32[]{:S(2)}) copy-start(bf16[128,128]{1,0:T(8,128)(2,1)} %gate_ref.1) | copy-start | bytes 98308
  0.7 6.6 %collective-permute-start = (bf16[2,64,128]{2,1,0:T(8,128)(2,1)}, bf16[2,64,128]{2,1,0:T(8,128)(2,1)S(1)}, u32[]{:S(2)}, u32[]{:S(2)}) collective-permute-start(bf16[2,64,128]{2,1,0:T(8,128)(2,1)} %bitcast.9), channel_id=1, source_target_pairs={{0,8},{1,9},{2,10},{3,11},{4,12},{5,13},{6,14},{7,15},{8,0},{9,1},... | collective-permute-start | bytes 98312 | tf_op jit(solution)/shard_map/ppermute | solution.py:346
  4.8 0.7 %copy-start.10 = (f32[128]{0:T(128)S(1)}, f32[128]{0:T(128)}, u32[]{:S(2)}) copy-start(f32[128]{0:T(128)} %param.20) | copy-start | bytes 1540
  4.8 0.7 %copy-start.1 = (s32[128]{0:T(128)S(1)}, s32[128]{0:T(128)}, u32[]{:S(2)}) copy-start(s32[128]{0:T(128)} %res_s_ref.1) | copy-start | bytes 1540
  4.8 0.7 %copy-start.2 = (s32[32]{0:T(128)S(1)}, s32[32]{0:T(128)}, u32[]{:S(2)}) copy-start(s32[32]{0:T(128)} %seq_ref.1) | copy-start | bytes 388
  4.8 0.7 %copy-start.9 = (f32[64]{0:T(128)S(1)}, f32[64]{0:T(128)}, u32[]{:S(2)}) copy-start(f32[64]{0:T(128)} %param.16) | copy-start | bytes 772
  5.5 1.8 %copy-start = (bf16[2,128,64]{1,2,0:T(8,128)(2,1)S(1)}, bf16[2,128,64]{1,2,0:T(8,128)(2,1)}, u32[]{:S(2)}) copy-start(bf16[2,128,64]{1,2,0:T(8,128)(2,1)} %param.11) | copy-start | bytes 98308
  5.5 6.0 %copy-start.8 = (bf16[64,32]{0,1:T(8,128)(2,1)S(1)}, bf16[64,32]{0,1:T(8,128)(2,1)}, u32[]{:S(2)}) copy-start(bf16[64,32]{0,1:T(8,128)(2,1)} %param.17) | copy-start | bytes 12292
  6.8 4.7 %copy-start.4 = (bf16[1024,128]{1,0:T(8,128)(2,1)S(1)}, bf16[1024,128]{1,0:T(8,128)(2,1)}, u32[]{:S(2)}) copy-start(bf16[1024,128]{1,0:T(8,128)(2,1)} %out_w_ref.1) | copy-start | bytes 786436
  7.9 3.6 %copy-start.7 = (bf16[64,32]{0,1:T(8,128)(2,1)S(1)}, bf16[64,32]{0,1:T(8,128)(2,1)}, u32[]{:S(2)}) copy-start(bf16[64,32]{0,1:T(8,128)(2,1)} %param.18) | copy-start | bytes 12292
  7.9 8.4 %collective-permute-start.3 = (bf16[768,128]{1,0:T(8,128)(2,1)S(1)}, bf16[768,128]{1,0:T(8,128)(2,1)S(1)}, u32[]{:S(2)}, u32[]{:S(2)}) collective-permute-start(bf16[768,128]{1,0:T(8,128)(2,1)S(1)} %get-tuple-element.40), channel_id=1, source_target_pairs={{0,4},{1,5},{2,6},{3,7},{4,0},{5,1},{6,2},{7,3},{8,12},{9,13},{10,... | collective-permute-start | bytes 589832 | tf_op jit(solution)/shard_map/ppermute | solution.py:346
  9.5 5.0 %collective-permute-start.6 = (bf16[256,128]{1,0:T(8,128)(2,1)S(1)}, bf16[256,128]{1,0:T(8,128)(2,1)S(1)}, u32[]{:S(2)}, u32[]{:S(2)}) collective-permute-start(bf16[256,128]{1,0:T(8,128)(2,1)S(1)} %get-tuple-element.39.after_ref.y0_ref), channel_id=1, source_target_pairs={{0,2},{1,3},{2,0},{3,1},{4,6},{5,7},{6,4},{7,5},{8,10},{9,11},{10,... | collective-permute-start | bytes 196616 | tf_op jit(solution)/shard_map/ppermute | solution.py:346
  11.0 5.3 %collective-permute-start.1 = (bf16[256,128]{1,0:T(8,128)(2,1)S(1)}, bf16[256,128]{1,0:T(8,128)(2,1)S(1)}, u32[]{:S(2)}, u32[]{:S(2)}) collective-permute-start(bf16[256,128]{1,0:T(8,128)(2,1)S(1)} %get-tuple-element.39.after_ref.y0_ref), channel_id=1, source_target_pairs={{0,6},{1,7},{2,4},{3,5},{4,2},{5,3},{6,0},{7,1},{8,14},{9,15},{10,... | collective-permute-start | bytes 196616 | tf_op jit(solution)/shard_map/ppermute | solution.py:346
  11.5 5.3 %collective-permute-start.5 = (bf16[512,128]{1,0:T(8,128)(2,1)S(1)}, bf16[512,128]{1,0:T(8,128)(2,1)S(1)}, u32[]{:S(2)}, u32[]{:S(2)}) collective-permute-start(bf16[512,128]{1,0:T(8,128)(2,1)S(1)} %get-tuple-element.45), channel_id=1, source_target_pairs={{0,1},{1,0},{2,3},{3,2},{4,5},{5,4},{6,7},{7,6},{8,9},{9,8},{10,11... | collective-permute-start | bytes 393224 | tf_op jit(solution)/shard_map/ppermute | solution.py:346
  14.5 2.3 %collective-permute-start.7 = (bf16[256,128]{1,0:T(8,128)(2,1)S(1)}, bf16[256,128]{1,0:T(8,128)(2,1)S(1)}, u32[]{:S(2)}, u32[]{:S(2)}) collective-permute-start(bf16[256,128]{1,0:T(8,128)(2,1)S(1)} %shard_map.150.y2_ref), channel_id=1, source_target_pairs={{0,1},{1,0},{2,3},{3,2},{4,5},{5,4},{6,7},{7,6},{8,9},{9,8},{10,11... | collective-permute-start | bytes 196616 | tf_op jit(solution)/shard_map/ppermute | solution.py:346
  16.3 2.6 %collective-permute-start.2 = (bf16[256,128]{1,0:T(8,128)(2,1)S(1)}, bf16[256,128]{1,0:T(8,128)(2,1)S(1)}, u32[]{:S(2)}, u32[]{:S(2)}) collective-permute-start(bf16[256,128]{1,0:T(8,128)(2,1)S(1)} %collective-permute-done.1.y0_ref), channel_id=1, source_target_pairs={{0,1},{1,0},{2,3},{3,2},{4,5},{5,4},{6,7},{7,6},{8,9},{9,8},{10,11... | collective-permute-start | bytes 196616 | tf_op jit(solution)/shard_map/ppermute | solution.py:346
  16.3 2.6 %collective-permute-start.4 = (bf16[768,128]{1,0:T(8,128)(2,1)S(1)}, bf16[768,128]{1,0:T(8,128)(2,1)S(1)}, u32[]{:S(2)}, u32[]{:S(2)}) collective-permute-start(bf16[768,128]{1,0:T(8,128)(2,1)S(1)} %collective-permute-done.3.y2_ref.across_ref), channel_id=1, source_target_pairs={{0,1},{1,0},{2,3},{3,2},{4,5},{5,4},{6,7},{7,6},{8,9},{9,8},{10,11... | collective-permute-start | bytes 589832 | tf_op jit(solution)/shard_map/ppermute | solution.py:346
  22.6 8.2 %collective-permute-start.8 = (bf16[416,128]{1,0:T(8,128)(2,1)S(1)}, bf16[416,128]{1,0:T(8,128)(2,1)S(1)}, u32[]{:S(2)}, u32[]{:S(2)}) collective-permute-start(bf16[416,128]{1,0:T(8,128)(2,1)S(1)} %shard_map.153.after_ref.own_ref), channel_id=1, source_target_pairs={{0,8},{1,9},{2,10},{3,11},{4,12},{5,13},{6,14},{7,15},{8,0},{9,1},... | collective-permute-start | bytes 319496 | tf_op jit(solution)/shard_map/ppermute | solution.py:346
  30.9 6.3 %collective-permute-start.11 = (bf16[416,128]{1,0:T(8,128)(2,1)S(1)}, bf16[416,128]{1,0:T(8,128)(2,1)S(1)}, u32[]{:S(2)}, u32[]{:S(2)}) collective-permute-start(bf16[416,128]{1,0:T(8,128)(2,1)S(1)} %shard_map.155.own_ref), channel_id=1, source_target_pairs={{0,6},{1,7},{2,4},{3,5},{4,2},{5,3},{6,0},{7,1},{8,14},{9,15},{10,... | collective-permute-start | bytes 319496 | tf_op jit(solution)/shard_map/ppermute | solution.py:346
  31.3 6.0 %collective-permute-start.10 = (bf16[416,128]{1,0:T(8,128)(2,1)S(1)}, bf16[416,128]{1,0:T(8,128)(2,1)S(1)}, u32[]{:S(2)}, u32[]{:S(2)}) collective-permute-start(bf16[416,128]{1,0:T(8,128)(2,1)S(1)} %shard_map.155.own_ref), channel_id=1, source_target_pairs={{0,4},{1,5},{2,6},{3,7},{4,0},{5,1},{6,2},{7,3},{8,12},{9,13},{10,... | collective-permute-start | bytes 319496 | tf_op jit(solution)/shard_map/ppermute | solution.py:346
  32.9 5.3 %collective-permute-start.9 = (bf16[416,128]{1,0:T(8,128)(2,1)S(1)}, bf16[416,128]{1,0:T(8,128)(2,1)S(1)}, u32[]{:S(2)}, u32[]{:S(2)}) collective-permute-start(bf16[416,128]{1,0:T(8,128)(2,1)S(1)} %shard_map.155.own_ref), channel_id=1, source_target_pairs={{0,2},{1,3},{2,0},{3,1},{4,6},{5,7},{6,4},{7,5},{8,10},{9,11},{10,... | collective-permute-start | bytes 319496 | tf_op jit(solution)/shard_map/ppermute | solution.py:346
  38.3 1.5 %collective-permute-start.12 = (bf16[672,128]{1,0:T(8,128)(2,1)S(1)}, bf16[672,128]{1,0:T(8,128)(2,1)S(1)}, u32[]{:S(2)}, u32[]{:S(2)}) collective-permute-start(bf16[672,128]{1,0:T(8,128)(2,1)S(1)} %shard_map.156.local_ref), channel_id=1, source_target_pairs={{0,1},{1,0},{2,3},{3,2},{4,5},{5,4},{6,7},{7,6},{8,9},{9,8},{10,11... | collective-permute-start | bytes 516104 | tf_op jit(solution)/shard_map/ppermute | solution.py:346

commit v5 on v4

--- a/solution.py
+++ b/solution.py
@@ -218,7 +218,7 @@
 def pair_kernel(
     y0_ref, y1_ref, y2_ref, y3_ref, turned_ref, kron_ref, block_ref, wide_ref,
     linear_ref, act_ref, slope_ref, pair_ref,
-    value_ref, gate_ref, grad_right_ref, right_t_ref, own_ref, slope_s_ref, *scratch
+    value_ref, keep_ref, send_ref, grad_right_ref, right_t_ref, own_ref, slope_s_ref, *scratch
 ):
     rows, n, _ = pair_ref.shape
     linear, act = half_of_rows(
@@ -228,7 +228,11 @@
         value = linear[:, i * n : (i + 1) * n] + linear_ref[:, i * n : (i + 1) * n]
         value_ref[i] = value
         slope_s_ref[i * n : (i + 1) * n, :] = (slope_ref[i] * value).astype(BF16)
-    gate_ref[...] = dot(pair_ref[...].reshape(rows * n, n), slope_s_ref[...], LHS_T).astype(BF16)
+    grad_gate = dot(pair_ref[...].reshape(rows * n, n), slope_s_ref[...], LHS_T)
+    halves = grad_gate[: n // 2, :], grad_gate[n // 2 :, :]
+    first_core = lax.axis_index("row") % 2 == 0
+    keep_ref[...] = jnp.where(first_core, halves[0], halves[1]).astype(BF16)
+    send_ref[...] = jnp.where(first_core, halves[1], halves[0]).astype(BF16)
     act = act + act_ref[...]
     grad_right_ref[...] = act[:32, :64] + act[32:, 64:]
 
@@ -238,16 +242,21 @@
     update_ref[...] = (scale_ref[...] * value_ref[...]).astype(BF16)
 
 
+def chip_kernel(sums_ref, keep_ref, other_ref, out_ref):
+    out_ref[0:288, :] = sums_ref[...]
+    out_ref[288:352, :] = (keep_ref[...].astype(F32) + other_ref[...].astype(F32)).astype(BF16)
+
+
 def add_kernel(own_ref, other_ref, after_ref, out_ref):
     out_ref[...] = (own_ref[...].astype(F32) + other_ref[...].astype(F32)).astype(BF16)
 
 
 def out_kernel(
     right0_ref, right1_ref, own0_ref, own1_ref, own_ref, core_ref, across_ref, both_ref,
-    part_ref, left_ref, gate_ref, grad_right_ref,
+    part_ref, left_ref, grad_right_ref,
     sums_ref, n_ref
 ):
-    n = gate_ref.shape[0]
+    n = sums_ref.shape[1]
     chans, width = 64, 32
     half = 8 * GROUP
     grads = ((own_ref, 0), (core_ref, 2), (across_ref, 2), (both_ref, 4))
@@ -282,8 +291,7 @@
     for h in range(width // QUAD):
         sums_ref[h * width : (h + 1) * width, :] = grad_out[:, h * n : (h + 1) * n].astype(BF16)
     grad_left = dot(part_ref[...], coarse, RHS_T) + dot(part_ref[...], fine, RHS_T)
-    sums_ref[256:384, :] = gate_ref[...]
-    sums_ref[384:416, :] = jnp.concatenate([grad_left, grad_right_ref[...]], axis=1).astype(BF16)
+    sums_ref[256:288, :] = jnp.concatenate([grad_left, grad_right_ref[...]], axis=1).astype(BF16)
 
 
 def join_kernel(own_ref, beside_ref, across_ref, both_ref, out_ref):
@@ -292,13 +300,14 @@
 
     out_ref[0:256, :] = pair(own_ref, beside_ref, 0, 256).astype(BF16)
     out_ref[256:512, :] = pair(across_ref, both_ref, 0, 256).astype(BF16)
-    out_ref[512:672, :] = (
-        pair(own_ref, beside_ref, 256, 416) + pair(across_ref, both_ref, 256, 416)
+    out_ref[512:608, :] = (
+        pair(own_ref, beside_ref, 256, 352) + pair(across_ref, both_ref, 256, 352)
     ).astype(BF16)
 
 
 def last_kernel(local_ref, other_ref, out_ref, gate_ref, left_ref, right_ref):
-    quad_at = place_in_quad(lax.axis_index("row"))
+    row = lax.axis_index("row")
+    quad_at = place_in_quad(row)
     n = local_ref.shape[1]
     wide = QUAD * n
     src = iota((wide, wide), 0)
@@ -316,10 +325,12 @@
             out_ref[pl.ds(h * 4 + el, 32, stride=32), :] = whole[
                 h * 32 : (h + 1) * 32, el * n : (el + 1) * n
             ]
-    gate_ref[...] = local_ref[512:640, :].astype(F32) + other_ref[512:640, :].astype(F32)
-    both = local_ref[640:672, :].astype(F32) + other_ref[640:672, :].astype(F32)
+    both = local_ref[512:544, :].astype(F32) + other_ref[512:544, :].astype(F32)
     left_ref[...] = both[:, 0:64]
     right_ref[...] = both[:, 64:128]
+    halves = local_ref[544:608, :].astype(F32), other_ref[544:608, :].astype(F32)
+    gate_ref[: n // 2, :] = jnp.where(row % 2 == 0, halves[0], halves[1])
+    gate_ref[n // 2 :, :] = jnp.where(row % 2 == 0, halves[1], halves[0])
 
 
 def tie_kernel(*refs):
@@ -389,18 +400,19 @@
         [((n, rows * n), F32), ((64, n), F32), *kept],
         scratch=scratch, ins=9, flops=2 << 30, vmem=24,
     )(pair, pair_core, beside, beside_core, *shared, bias)
-    value, gate_sum, right_sum, right1, own1 = call(
+    value, keep, send, right_sum, right1, own1 = call(
         pair_kernel,
-        [((rows, n, n), F32), ((n, n), BF16), ((32, 64), F32), *kept],
+        [((rows, n, n), F32), ((n // 2, n), BF16), ((n // 2, n), BF16), ((32, 64), F32), *kept],
         scratch=[((rows * n, n), BF16), *scratch], ins=12, flops=2 << 30, vmem=24,
     )(corner, corner_core, ahead, ahead_core, *shared, linear, act, slope, pair_state)
     (sums,) = call(
-        out_kernel, [((416, n), BF16)], scratch=[((256, 32 * n), BF16)], ins=12, flops=1 << 30, vmem=24,
-    )(right0, right1, own0, own1, own, pair_core, ahead, ahead_core, part, left_t, gate_sum, right_sum)
+        out_kernel, [((288, n), BF16)], scratch=[((256, 32 * n), BF16)], ins=11, flops=1 << 30, vmem=24,
+    )(right0, right1, own0, own1, own, pair_core, ahead, ahead_core, part, left_t, right_sum)
+    (sums,) = call(chip_kernel, [((352, n), BF16)], ins=3)(sums, keep, swap(send, 1, size))
     update, token = call(update_kernel, [((rows, n, n), BF16), ((8, n), F32)], ins=3, flops=1 << 30, vmem=8)(scale, value, sums)
-    (sums,) = call(add_kernel, [((416, n), BF16)], ins=3)(sums, swap(sums, 8, size), token)
+    (sums,) = call(add_kernel, [((352, n), BF16)], ins=3)(sums, swap(sums, 8, size), token)
     others = [swap(sums, step, size) for step in (2, ACROSS, 2 ^ ACROSS)]
-    (local,) = call(join_kernel, [((672, n), BF16)], ins=4)(sums, *others)
+    (local,) = call(join_kernel, [((608, n), BF16)], ins=4)(sums, *others)
     other = swap(local, 1, size)
     grad_out, grad_gate, left, right = call(
         last_kernel,

time: 41.3 us -> 41 us (level)
    ppermute x13 -> x14, waiting for transfers between devices: 13.9 us -> 13.5 us  [swap(): return lax.ppermute(x, 'row', [(i, i ^ bit) for i in range(size)])]
    ppermute x13 -> x14, starting transfers between devices: 14.5 us -> 14.7 us  [swap(): return lax.ppermute(x, 'row', [(i, i ^ bit) for i in range(size)])]
    pallas_call x4 -> x5, Pallas kernels: 3.8 us -> 3.81 us  [the longest x1 2.06 us: one_column(): call(pair_kernel, [((rows, n, n), F32), ((n // 2, n), BF16), ((n // 2, n)...]
  transfers between devices with their start and end apart: 13 -> 14, of which waited for: 8 -> 7; matrix products, arithmetic and copies ran while one was open for 0% -> 0% of each run, Pallas kernels for 13% -> 17%
where the time goes in v5:
time: 41 us; the launch traced here: 40.9 us
  starting transfers between devices  14.7 us (36%)
  waiting for transfers between devices  13.5 us (33%)
  Pallas kernels  11.2 us (27%)
  between operations  0.82 us (2%)
  local copies, waits for them, and re-layouts  0.69 us (2%)
    ppermute x14, starting transfers between devices, swap(): return lax.ppermute(x, 'row', [(i, i ^ bit) for i in range(size)])  14.7 us
    ppermute x14, waiting for transfers between devices, swap(): return lax.ppermute(x, 'row', [(i, i ^ bit) for i in range(size)])  13.5 us
    pallas_call x1, Pallas kernels, one_column(): call(half_kernel, [((n, rows * n), F32), ((64, n), F32), *kept], scratch=...  2.07 us
    pallas_call x1, Pallas kernels, one_column(): call(pair_kernel, [((rows, n, n), F32), ((n // 2, n), BF16), ((n // 2, n)...  2.06 us
    pallas_call x1, Pallas kernels, one_column(): call(out_kernel, [((288, n), BF16)], scratch=[((256, 32 * n), BF16)], ins...  1.67 us
    pallas_call x1, Pallas kernels, one_column(): call(last_kernel, [((1024, n), F32), ((n, n), F32), ((32, 64), F32), ((32...  1.38 us
    pallas_call x1, Pallas kernels, one_column(): call(gate_kernel, [((rows, n, n), F32), ((rows, n, n), F32), ((rows * n,...  1.32 us
    pallas_call x1, Pallas kernels, one_column(): call(weight_kernel, [((1024, 512), BF16), ((256, n), BF16), ((32, 32 * n)...  1.22 us
  transfers between devices with their start and end apart: 14, of which 7 were waited for; matrix products, arithmetic and copies ran while one was open for 0% of the time, Pallas kernels for 17%

profile of v5, /device:TPU:0, one launch (start us, length us, event | category | flops | bytes accessed | tf_op | source)
XLA Modules:
  0.0 40.9 jit_solution(8719008453683331302)
XLA Ops:
  0.7 4.1 %collective-permute-start = (bf16[2,64,128]{2,1,0:T(8,128)(2,1)}, bf16[2,64,128]{2,1,0:T(8,128)(2,1)S(1)}, u32[]{:S(2)}, u32[]{:S(2)}) collective-permute-start(bf16[2,64,128]{2,1,0:T(8,128)(2,1)} %bitcast.9), channel_id=1, source_target_pairs={{0,8},{1,9},{2,10},{3,11},{4,12},{5,13},{6,14},{7,15},{8,0},{9,1},... | collective-permute-start | bytes 98312 | tf_op jit(solution)/shard_map/ppermute | solution.py:357
  4.8 0.6 %copy-done.10 = f32[128]{0:T(128)S(1)} copy-done((f32[128]{0:T(128)S(1)}, f32[128]{0:T(128)}, u32[]{:S(2)}) %copy-start.10) | copy-done | bytes 536
  5.5 1.3 %shard_map.147 = (f32[8,128,128]{2,1,0:T(8,128)S(1)}, f32[8,128,128]{2,1,0:T(8,128)S(1)}, bf16[1024,128]{1,0:T(8,128)(2,1)S(1)}, bf16[256,128]{1,0:T(8,128)(2,1)...) custom-call(s32[128]{0:T(128)S(1)} %copy-done.1, ...), custom_call_target="tpu_custom_call" | custom-call | flops 1073741824 | bytes 1048576 | tf_op jit(solution)/shard_map/pallas_call | solution.py:373
  7.2 0.7 %shard_map.148 = (bf16[256,128]{1,0:T(8,128)(2,1)S(1)}, bf16[512,128]{1,0:T(8,128)(2,1)S(1)}, bf16[768,128]{1,0:T(8,128)(2,1)S(1)}) custom-call(s32[32]{0:T(128)S(1)} %copy-done.2, s32[1,128]{1,0:T(1,128)S(1)} %bitcast.12, f32[1,64]{1,0:T(1,128)S(1)} %get-tuple-element.37.gain_ref, bf16[2,64,128]{2,1,0:T(8,128)(2,1)S(1)} %bitcast.10, ...), custom_call_target="tpu_custom_call" | custom-call | flops 1048576 | bytes 1048576 | tf_op jit(solution)/shard_map/pallas_call | solution.py:379
  7.9 1.6 %collective-permute-start.3 = (bf16[768,128]{1,0:T(8,128)(2,1)S(1)}, bf16[768,128]{1,0:T(8,128)(2,1)S(1)}, u32[]{:S(2)}, u32[]{:S(2)}) collective-permute-start(bf16[768,128]{1,0:T(8,128)(2,1)S(1)} %get-tuple-element.41), channel_id=1, source_target_pairs={{0,4},{1,5},{2,6},{3,7},{4,0},{5,1},{6,2},{7,3},{8,12},{9,13},{10,... | collective-permute-start | bytes 589832 | tf_op jit(solution)/shard_map/ppermute | solution.py:357
  9.5 1.5 %collective-permute-start.6 = (bf16[256,128]{1,0:T(8,128)(2,1)S(1)}, bf16[256,128]{1,0:T(8,128)(2,1)S(1)}, u32[]{:S(2)}, u32[]{:S(2)}) collective-permute-start(bf16[256,128]{1,0:T(8,128)(2,1)S(1)} %get-tuple-element.40.after_ref.y0_ref), channel_id=1, source_target_pairs={{0,2},{1,3},{2,0},{3,1},{4,6},{5,7},{6,4},{7,5},{8,10},{9,11},{10,... | collective-permute-start | bytes 196616 | tf_op jit(solution)/shard_map/ppermute | solution.py:357
  11.0 0.4 %collective-permute-start.1 = (bf16[256,128]{1,0:T(8,128)(2,1)S(1)}, bf16[256,128]{1,0:T(8,128)(2,1)S(1)}, u32[]{:S(2)}, u32[]{:S(2)}) collective-permute-start(bf16[256,128]{1,0:T(8,128)(2,1)S(1)} %get-tuple-element.40.after_ref.y0_ref), channel_id=1, source_target_pairs={{0,6},{1,7},{2,4},{3,5},{4,2},{5,3},{6,0},{7,1},{8,14},{9,15},{10,... | collective-permute-start | bytes 196616 | tf_op jit(solution)/shard_map/ppermute | solution.py:357
  11.5 1.2 %shard_map.149 = (bf16[1024,512]{1,0:T(8,128)(2,1)S(1)}, bf16[256,128]{1,0:T(8,128)(2,1)S(1)}, bf16[32,4096]{1,0:T(8,128)(2,1)S(1)}, bf16[32,1024]{1,0:T(8,128)(2,1)S(1)}) custom-call(bf16[32,64]{1,0:T(8,128)(2,1)S(1)} %bitcast.14, bf16[32,64]{1,0:T(8,128)(2,1)S(1)} %bitcast.15, bf16[1024,128]{1,0:T(8,128)(2,1)S(1)} %copy-done.4, ...), custom_call_target="tpu_custom_call" | custom-call | flops 1073741824 | bytes 1048576 | tf_op jit(solution)/shard_map/pallas_call | solution.py:384
  12.7 1.8 %collective-permute-done.6.refs_0_ = bf16[256,128]{1,0:T(8,128)(2,1)S(1)} collective-permute-done((bf16[256,128]{1,0:T(8,128)(2,1)S(1)}, bf16[256,128]{1,0:T(8,128)(2,1)S(1)}, u32[]{:S(2)}, u32[]{:S(2)}) %collective-permute-start.6) | collective-permute-done | bytes 65568 | tf_op jit(solution)/shard_map/ppermute | solution.py:357
  14.5 1.8 %collective-permute-done.1.y0_ref = bf16[256,128]{1,0:T(8,128)(2,1)S(1)} collective-permute-done((bf16[256,128]{1,0:T(8,128)(2,1)S(1)}, bf16[256,128]{1,0:T(8,128)(2,1)S(1)}, u32[]{:S(2)}, u32[]{:S(2)}) %collective-permute-start.1) | collective-permute-done | bytes 65568 | tf_op jit(solution)/shard_map/ppermute | solution.py:357
  16.3 0.5 %collective-permute-start.4 = (bf16[768,128]{1,0:T(8,128)(2,1)S(1)}, bf16[768,128]{1,0:T(8,128)(2,1)S(1)}, u32[]{:S(2)}, u32[]{:S(2)}) collective-permute-start(bf16[768,128]{1,0:T(8,128)(2,1)S(1)} %collective-permute-done.3.y2_ref.across_ref), channel_id=1, source_target_pairs={{0,1},{1,0},{2,3},{3,2},{4,5},{5,4},{6,7},{7,6},{8,9},{9,8},{10,11... | collective-permute-start | bytes 589832 | tf_op jit(solution)/shard_map/ppermute | solution.py:357
  16.8 2.1 %shard_map.151 = (f32[128,1024]{1,0:T(8,128)S(1)}, f32[64,128]{1,0:T(8,128)S(1)}, bf16[512,128]{1,0:T(8,128)(2,1)S(1)}, bf16[128,256]{1,0:T(8,128)(2,1)S(1)}) custom-call(bf16[256,128]{1,0:T(8,128)(2,1)S(1)} %get-tuple-element.40.after_ref.y0_ref, bf16[512,128]{1,0:T(8,128)(2,1)S(1)} %collective-permute-done.5.y1_ref.core_ref, ...), custom_call_target="tpu_custom_call" | custom-call | flops 2147483648 | bytes 1048576 | tf_op jit(solution)/shard_map/pallas_call | solution.py:398
  18.9 2.1 %shard_map.152 = (f32[8,128,128]{2,1,0:T(8,128)S(1)}, bf16[64,128]{1,0:T(8,128)(2,1)S(1)}, bf16[64,128]{1,0:T(8,128)(2,1)S(1)}, f32[32,64]{1,0:T(8,128)S(1)}, bf...) custom-call(bf16[256,128]{1,0:T(8,128)(2,1)S(1)} %collective-permute-done.1.y0_ref, ...), custom_call_target="tpu_custom_call" | custom-call | flops 2147483648 | bytes 1048576 | tf_op jit(solution)/shard_map/pallas_call | solution.py:403
  21.1 1.7 %shard_map.153.sums_ref = bf16[288,128]{1,0:T(8,128)(2,1)S(1)} custom-call(bf16[512,128]{1,0:T(8,128)(2,1)S(1)} %get-tuple-element.52.right0_ref, bf16[512,128]{1,0:T(8,128)(2,1)S(1)} %get-tuple-element.53.right1_ref, bf16[128,256]{1,0:T(8,128)(2,1)S(1)} %get-tuple-element.54.own0_ref, bf16[128,256]{1,0:T(8,128)(2,1)S(1)} %get-tuple-element.55.own1_ref, ...), custom_call_target="tpu_custom_call" | custom-call | flops 1073741824 | bytes 1048576 | tf_op jit(solution)/shard_map/pallas_call | solution.py:408
  22.8 2.8 %collective-permute-start.9 = (bf16[352,128]{1,0:T(8,128)(2,1)S(1)}, bf16[352,128]{1,0:T(8,128)(2,1)S(1)}, u32[]{:S(2)}, u32[]{:S(2)}) collective-permute-start(bf16[352,128]{1,0:T(8,128)(2,1)S(1)} %shard_map.154.after_ref.own_ref), channel_id=1, source_target_pairs={{0,8},{1,9},{2,10},{3,11},{4,12},{5,13},{6,14},{7,15},{8,0},{9,1},... | collective-permute-start | bytes 270344 | tf_op jit(solution)/shard_map/ppermute | solution.py:357
  25.5 0.8 %shard_map.155 = (bf16[8,128,128]{2,1,0:T(8,128)(2,1)}, f32[8,128]{1,0:T(8,128)S(1)}) custom-call(f32[8,128,128]{2,1,0:T(8,128)S(1)} %get-tuple-element.36.scale_ref, f32[8,128,128]{2,1,0:T(8,128)S(1)} %get-tuple-element.51.value_ref, bf16[352,128]{1,0:T(8,128)(2,1)S(1)} %shard_map.154.after_ref.own_ref), custom_call_target="tpu_custom_call" | custom-call | flops 1073741824 | bytes 1048576 | tf_op jit(solution)/shard_map/pallas_call | solution.py:412
  26.3 4.4 %collective-permute-done.9.other_ref = bf16[352,128]{1,0:T(8,128)(2,1)S(1)} collective-permute-done((bf16[352,128]{1,0:T(8,128)(2,1)S(1)}, bf16[352,128]{1,0:T(8,128)(2,1)S(1)}, u32[]{:S(2)}, u32[]{:S(2)}) %collective-permute-start.9) | collective-permute-done | bytes 90144 | tf_op jit(solution)/shard_map/ppermute | solution.py:357
  30.8 0.5 %collective-permute-start.12 = (bf16[352,128]{1,0:T(8,128)(2,1)S(1)}, bf16[352,128]{1,0:T(8,128)(2,1)S(1)}, u32[]{:S(2)}, u32[]{:S(2)}) collective-permute-start(bf16[352,128]{1,0:T(8,128)(2,1)S(1)} %shard_map.156.own_ref), channel_id=1, source_target_pairs={{0,6},{1,7},{2,4},{3,5},{4,2},{5,3},{6,0},{7,1},{8,14},{9,15},{10,... | collective-permute-start | bytes 270344 | tf_op jit(solution)/shard_map/ppermute | solution.py:357
  31.2 1.6 %collective-permute-start.11 = (bf16[352,128]{1,0:T(8,128)(2,1)S(1)}, bf16[352,128]{1,0:T(8,128)(2,1)S(1)}, u32[]{:S(2)}, u32[]{:S(2)}) collective-permute-start(bf16[352,128]{1,0:T(8,128)(2,1)S(1)} %shard_map.156.own_ref), channel_id=1, source_target_pairs={{0,4},{1,5},{2,6},{3,7},{4,0},{5,1},{6,2},{7,3},{8,12},{9,13},{10,... | collective-permute-start | bytes 270344 | tf_op jit(solution)/shard_map/ppermute | solution.py:357
  32.8 1.5 %collective-permute-start.10 = (bf16[352,128]{1,0:T(8,128)(2,1)S(1)}, bf16[352,128]{1,0:T(8,128)(2,1)S(1)}, u32[]{:S(2)}, u32[]{:S(2)}) collective-permute-start(bf16[352,128]{1,0:T(8,128)(2,1)S(1)} %shard_map.156.own_ref), channel_id=1, source_target_pairs={{0,2},{1,3},{2,0},{3,1},{4,6},{5,7},{6,4},{7,5},{8,10},{9,11},{10,... | collective-permute-start | bytes 270344 | tf_op jit(solution)/shard_map/ppermute | solution.py:357
  34.3 2.7 %collective-permute-done.12.both_ref = bf16[352,128]{1,0:T(8,128)(2,1)S(1)} collective-permute-done((bf16[352,128]{1,0:T(8,128)(2,1)S(1)}, bf16[352,128]{1,0:T(8,128)(2,1)S(1)}, u32[]{:S(2)}, u32[]{:S(2)}) %collective-permute-start.12) | collective-permute-done | bytes 90144 | tf_op jit(solution)/shard_map/ppermute | solution.py:357
  37.1 0.9 %collective-permute-done.10.beside_ref = bf16[352,128]{1,0:T(8,128)(2,1)S(1)} collective-permute-done((bf16[352,128]{1,0:T(8,128)(2,1)S(1)}, bf16[352,128]{1,0:T(8,128)(2,1)S(1)}, u32[]{:S(2)}, u32[]{:S(2)}) %collective-permute-start.10) | collective-permute-done | bytes 90144 | tf_op jit(solution)/shard_map/ppermute | solution.py:357
  38.1 1.4 %collective-permute-done.13.other_ref = bf16[608,128]{1,0:T(8,128)(2,1)S(1)} collective-permute-done((bf16[608,128]{1,0:T(8,128)(2,1)S(1)}, bf16[608,128]{1,0:T(8,128)(2,1)S(1)}, u32[]{:S(2)}, u32[]{:S(2)}) %collective-permute-start.13) | collective-permute-done | bytes 155680 | tf_op jit(solution)/shard_map/ppermute | solution.py:357
  39.5 1.4 %shard_map.158 = (f32[1024,128]{1,0:T(8,128)}, f32[128,128]{1,0:T(8,128)}, f32[32,64]{1,0:T(8,128)}, f32[32,64]{1,0:T(8,128)}) custom-call(bf16[608,128]{1,0:T(8,128)(2,1)S(1)} %shard_map.157.local_ref, bf16[608,128]{1,0:T(8,128)(2,1)S(1)} %collective-permute-done.13.other_ref), custom_call_target="tpu_custom_call" | custom-call | flops 1048576 | bytes 1048576 | tf_op jit(solution)/shard_map/pallas_call | solution.py:417
  (39 shorter events, 0.8 us)
Async XLA Ops:
  0.6 4.2 %copy-start.3 = (bf16[8,128,128]{2,1,0:T(8,128)(2,1)S(1)}, bf16[8,128,128]{2,1,0:T(8,128)(2,1)}, u32[]{:S(2)}) copy-start(bf16[8,128,128]{2,1,0:T(8,128)(2,1)} %cot_ref.1) | copy-start | bytes 786436
  0.6 4.2 %copy-start.5 = (bf16[8,128,128]{2,1,0:T(8,128)(2,1)S(1)}, bf16[8,128,128]{2,1,0:T(8,128)(2,1)}, u32[]{:S(2)}) copy-start(bf16[8,128,128]{2,1,0:T(8,128)(2,1)} %pair_ref.3) | copy-start | bytes 786436
  0.7 4.2 %copy-start.6 = (bf16[128,128]{1,0:T(8,128)(2,1)S(1)}, bf16[128,128]{1,0:T(8,128)(2,1)}, u32[]{:S(2)}) copy-start(bf16[128,128]{1,0:T(8,128)(2,1)} %gate_ref.1) | copy-start | bytes 98308
  0.7 6.6 %collective-permute-start = (bf16[2,64,128]{2,1,0:T(8,128)(2,1)}, bf16[2,64,128]{2,1,0:T(8,128)(2,1)S(1)}, u32[]{:S(2)}, u32[]{:S(2)}) collective-permute-start(bf16[2,64,128]{2,1,0:T(8,128)(2,1)} %bitcast.9), channel_id=1, source_target_pairs={{0,8},{1,9},{2,10},{3,11},{4,12},{5,13},{6,14},{7,15},{8,0},{9,1},... | collective-permute-start | bytes 98312 | tf_op jit(solution)/shard_map/ppermute | solution.py:357
  4.8 0.7 %copy-start.1 = (s32[128]{0:T(128)S(1)}, s32[128]{0:T(128)}, u32[]{:S(2)}) copy-start(s32[128]{0:T(128)} %res_s_ref.1) | copy-start | bytes 1540
  4.8 0.7 %copy-start.2 = (s32[32]{0:T(128)S(1)}, s32[32]{0:T(128)}, u32[]{:S(2)}) copy-start(s32[32]{0:T(128)} %seq_ref.1) | copy-start | bytes 388
  4.8 0.7 %copy-start.9 = (f32[64]{0:T(128)S(1)}, f32[64]{0:T(128)}, u32[]{:S(2)}) copy-start(f32[64]{0:T(128)} %param.16) | copy-start | bytes 772
  5.5 1.8 %copy-start = (bf16[2,128,64]{1,2,0:T(8,128)(2,1)S(1)}, bf16[2,128,64]{1,2,0:T(8,128)(2,1)}, u32[]{:S(2)}) copy-start(bf16[2,128,64]{1,2,0:T(8,128)(2,1)} %param.11) | copy-start | bytes 98308
  5.5 6.0 %copy-start.8 = (bf16[64,32]{0,1:T(8,128)(2,1)S(1)}, bf16[64,32]{0,1:T(8,128)(2,1)}, u32[]{:S(2)}) copy-start(bf16[64,32]{0,1:T(8,128)(2,1)} %param.17) | copy-start | bytes 12292
  6.8 4.7 %copy-start.4 = (bf16[1024,128]{1,0:T(8,128)(2,1)S(1)}, bf16[1024,128]{1,0:T(8,128)(2,1)}, u32[]{:S(2)}) copy-start(bf16[1024,128]{1,0:T(8,128)(2,1)} %out_w_ref.1) | copy-start | bytes 786436
  7.9 3.6 %copy-start.7 = (bf16[64,32]{0,1:T(8,128)(2,1)S(1)}, bf16[64,32]{0,1:T(8,128)(2,1)}, u32[]{:S(2)}) copy-start(bf16[64,32]{0,1:T(8,128)(2,1)} %param.18) | copy-start | bytes 12292
  7.9 8.4 %collective-permute-start.3 = (bf16[768,128]{1,0:T(8,128)(2,1)S(1)}, bf16[768,128]{1,0:T(8,128)(2,1)S(1)}, u32[]{:S(2)}, u32[]{:S(2)}) collective-permute-start(bf16[768,128]{1,0:T(8,128)(2,1)S(1)} %get-tuple-element.41), channel_id=1, source_target_pairs={{0,4},{1,5},{2,6},{3,7},{4,0},{5,1},{6,2},{7,3},{8,12},{9,13},{10,... | collective-permute-start | bytes 589832 | tf_op jit(solution)/shard_map/ppermute | solution.py:357
  9.5 5.0 %collective-permute-start.6 = (bf16[256,128]{1,0:T(8,128)(2,1)S(1)}, bf16[256,128]{1,0:T(8,128)(2,1)S(1)}, u32[]{:S(2)}, u32[]{:S(2)}) collective-permute-start(bf16[256,128]{1,0:T(8,128)(2,1)S(1)} %get-tuple-element.40.after_ref.y0_ref), channel_id=1, source_target_pairs={{0,2},{1,3},{2,0},{3,1},{4,6},{5,7},{6,4},{7,5},{8,10},{9,11},{10,... | collective-permute-start | bytes 196616 | tf_op jit(solution)/shard_map/ppermute | solution.py:357
  11.0 5.3 %collective-permute-start.1 = (bf16[256,128]{1,0:T(8,128)(2,1)S(1)}, bf16[256,128]{1,0:T(8,128)(2,1)S(1)}, u32[]{:S(2)}, u32[]{:S(2)}) collective-permute-start(bf16[256,128]{1,0:T(8,128)(2,1)S(1)} %get-tuple-element.40.after_ref.y0_ref), channel_id=1, source_target_pairs={{0,6},{1,7},{2,4},{3,5},{4,2},{5,3},{6,0},{7,1},{8,14},{9,15},{10,... | collective-permute-start | bytes 196616 | tf_op jit(solution)/shard_map/ppermute | solution.py:357
  11.5 5.3 %collective-permute-start.5 = (bf16[512,128]{1,0:T(8,128)(2,1)S(1)}, bf16[512,128]{1,0:T(8,128)(2,1)S(1)}, u32[]{:S(2)}, u32[]{:S(2)}) collective-permute-start(bf16[512,128]{1,0:T(8,128)(2,1)S(1)} %get-tuple-element.46), channel_id=1, source_target_pairs={{0,1},{1,0},{2,3},{3,2},{4,5},{5,4},{6,7},{7,6},{8,9},{9,8},{10,11... | collective-permute-start | bytes 393224 | tf_op jit(solution)/shard_map/ppermute | solution.py:357
  14.5 2.3 %collective-permute-start.7 = (bf16[256,128]{1,0:T(8,128)(2,1)S(1)}, bf16[256,128]{1,0:T(8,128)(2,1)S(1)}, u32[]{:S(2)}, u32[]{:S(2)}) collective-permute-start(bf16[256,128]{1,0:T(8,128)(2,1)S(1)} %shard_map.150.y2_ref), channel_id=1, source_target_pairs={{0,1},{1,0},{2,3},{3,2},{4,5},{5,4},{6,7},{7,6},{8,9},{9,8},{10,11... | collective-permute-start | bytes 196616 | tf_op jit(solution)/shard_map/ppermute | solution.py:357
  16.3 2.6 %collective-permute-start.2 = (bf16[256,128]{1,0:T(8,128)(2,1)S(1)}, bf16[256,128]{1,0:T(8,128)(2,1)S(1)}, u32[]{:S(2)}, u32[]{:S(2)}) collective-permute-start(bf16[256,128]{1,0:T(8,128)(2,1)S(1)} %collective-permute-done.1.y0_ref), channel_id=1, source_target_pairs={{0,1},{1,0},{2,3},{3,2},{4,5},{5,4},{6,7},{7,6},{8,9},{9,8},{10,11... | collective-permute-start | bytes 196616 | tf_op jit(solution)/shard_map/ppermute | solution.py:357
  16.3 2.6 %collective-permute-start.4 = (bf16[768,128]{1,0:T(8,128)(2,1)S(1)}, bf16[768,128]{1,0:T(8,128)(2,1)S(1)}, u32[]{:S(2)}, u32[]{:S(2)}) collective-permute-start(bf16[768,128]{1,0:T(8,128)(2,1)S(1)} %collective-permute-done.3.y2_ref.across_ref), channel_id=1, source_target_pairs={{0,1},{1,0},{2,3},{3,2},{4,5},{5,4},{6,7},{7,6},{8,9},{9,8},{10,11... | collective-permute-start | bytes 589832 | tf_op jit(solution)/shard_map/ppermute | solution.py:357
  21.0 1.8 %collective-permute-start.8 = (bf16[64,128]{1,0:T(8,128)(2,1)S(1)}, bf16[64,128]{1,0:T(8,128)(2,1)S(1)}, u32[]{:S(2)}, u32[]{:S(2)}) collective-permute-start(bf16[64,128]{1,0:T(8,128)(2,1)S(1)} %get-tuple-element.60), channel_id=1, source_target_pairs={{0,1},{1,0},{2,3},{3,2},{4,5},{5,4},{6,7},{7,6},{8,9},{9,8},{10,11... | collective-permute-start | bytes 49160 | tf_op jit(solution)/shard_map/ppermute | solution.py:357
  22.8 8.0 %collective-permute-start.9 = (bf16[352,128]{1,0:T(8,128)(2,1)S(1)}, bf16[352,128]{1,0:T(8,128)(2,1)S(1)}, u32[]{:S(2)}, u32[]{:S(2)}) collective-permute-start(bf16[352,128]{1,0:T(8,128)(2,1)S(1)} %shard_map.154.after_ref.own_ref), channel_id=1, source_target_pairs={{0,8},{1,9},{2,10},{3,11},{4,12},{5,13},{6,14},{7,15},{8,0},{9,1},... | collective-permute-start | bytes 270344 | tf_op jit(solution)/shard_map/ppermute | solution.py:357
  30.8 6.3 %collective-permute-start.12 = (bf16[352,128]{1,0:T(8,128)(2,1)S(1)}, bf16[352,128]{1,0:T(8,128)(2,1)S(1)}, u32[]{:S(2)}, u32[]{:S(2)}) collective-permute-start(bf16[352,128]{1,0:T(8,128)(2,1)S(1)} %shard_map.156.own_ref), channel_id=1, source_target_pairs={{0,6},{1,7},{2,4},{3,5},{4,2},{5,3},{6,0},{7,1},{8,14},{9,15},{10,... | collective-permute-start | bytes 270344 | tf_op jit(solution)/shard_map/ppermute | solution.py:357
  31.2 5.9 %collective-permute-start.11 = (bf16[352,128]{1,0:T(8,128)(2,1)S(1)}, bf16[352,128]{1,0:T(8,128)(2,1)S(1)}, u32[]{:S(2)}, u32[]{:S(2)}) collective-permute-start(bf16[352,128]{1,0:T(8,128)(2,1)S(1)} %shard_map.156.own_ref), channel_id=1, source_target_pairs={{0,4},{1,5},{2,6},{3,7},{4,0},{5,1},{6,2},{7,3},{8,12},{9,13},{10,... | collective-permute-start | bytes 270344 | tf_op jit(solution)/shard_map/ppermute | solution.py:357
  32.8 5.1 %collective-permute-start.10 = (bf16[352,128]{1,0:T(8,128)(2,1)S(1)}, bf16[352,128]{1,0:T(8,128)(2,1)S(1)}, u32[]{:S(2)}, u32[]{:S(2)}) collective-permute-start(bf16[352,128]{1,0:T(8,128)(2,1)S(1)} %shard_map.156.own_ref), channel_id=1, source_target_pairs={{0,2},{1,3},{2,0},{3,1},{4,6},{5,7},{6,4},{7,5},{8,10},{9,11},{10,... | collective-permute-start | bytes 270344 | tf_op jit(solution)/shard_map/ppermute | solution.py:357
  38.0 1.4 %collective-permute-start.13 = (bf16[608,128]{1,0:T(8,128)(2,1)S(1)}, bf16[608,128]{1,0:T(8,128)(2,1)S(1)}, u32[]{:S(2)}, u32[]{:S(2)}) collective-permute-start(bf16[608,128]{1,0:T(8,128)(2,1)S(1)} %shard_map.157.local_ref), channel_id=1, source_target_pairs={{0,1},{1,0},{2,3},{3,2},{4,5},{5,4},{6,7},{7,6},{8,9},{9,8},{10,11... | collective-permute-start | bytes 466952 | tf_op jit(solution)/shard_map/ppermute | solution.py:357
  (1 other events, 0.7 us)

commit v6 on v5

--- a/solution.py
+++ b/solution.py
@@ -185,16 +185,18 @@
         ],
         axis=0,
     ).astype(BF16)
-    for e4 in range(width // 4):
-        part = dot(mine, wide_ref[:, e4 * 4 * n : (e4 + 1) * 4 * n]).astype(BF16)
-        for el in range(4):
-            e = e4 * 4 + el
+    for e8 in range(width // 8):
+        part = dot(mine, wide_ref[:, e8 * 8 * n : (e8 + 1) * 8 * n]).astype(BF16)
+        for el in range(8):
+            e = e8 * 8 + el
             for i in range(8):
                 m_ref[e * GROUP : (e + 1) * GROUP, i * n : (i + 1) * n] = part[
                     i * GROUP : (i + 1) * GROUP, el * n : (el + 1) * n
                 ]
     linear = dot(right, m_ref[...])
-    right_ref[...] = dot(m_ref[...], turned[...])
+    for k in range(4):
+        at = slice(k * 128, (k + 1) * 128)
+        right_ref[at, :] = dot(m_ref[at, :], turned[...])
     for t in range(8):
         for s in range(2):
             flat_ref[s * width : (s + 1) * width, t * n : (t + 1) * n] = right_ref[

time: 41 us -> 40.5 us (0.988)
  Pallas kernels: 11.2 us -> 10.7 us
where the time goes in v6:
time: 40.5 us; the launch traced here: 40.3 us
  starting transfers between devices  14.7 us (36%)
  waiting for transfers between devices  13.4 us (33%)
  Pallas kernels  10.7 us (26%)
  between operations  0.82 us (2%)
  local copies, waits for them, and re-layouts  0.69 us (2%)
    ppermute x14, starting transfers between devices, swap(): return lax.ppermute(x, 'row', [(i, i ^ bit) for i in range(size)])  14.7 us
    ppermute x14, waiting for transfers between devices, swap(): return lax.ppermute(x, 'row', [(i, i ^ bit) for i in range(size)])  13.4 us
    pallas_call x1, Pallas kernels, one_column(): call(pair_kernel, [((rows, n, n), F32), ((n // 2, n), BF16), ((n // 2, n)...  1.88 us
    pallas_call x1, Pallas kernels, one_column(): call(half_kernel, [((n, rows * n), F32), ((64, n), F32), *kept], scratch=...  1.7 us
    pallas_call x1, Pallas kernels, one_column(): call(out_kernel, [((288, n), BF16)], scratch=[((256, 32 * n), BF16)], ins...  1.67 us
    pallas_call x1, Pallas kernels, one_column(): call(last_kernel, [((1024, n), F32), ((n, n), F32), ((32, 64), F32), ((32...  1.38 us
    pallas_call x1, Pallas kernels, one_column(): call(gate_kernel, [((rows, n, n), F32), ((rows, n, n), F32), ((rows * n,...  1.32 us
    pallas_call x1, Pallas kernels, one_column(): call(weight_kernel, [((1024, 512), BF16), ((256, n), BF16), ((32, 32 * n)...  1.22 us
  transfers between devices with their start and end apart: 14, of which 7 were waited for; matrix products, arithmetic and copies ran while one was open for 0% of the time, Pallas kernels for 17%

profile of v6, /device:TPU:0, one launch (start us, length us, event | category | flops | bytes accessed | tf_op | source)
XLA Modules:
  0.0 40.3 jit_solution(16330493353784386354)
XLA Ops:
  0.7 4.1 %collective-permute-start = (bf16[2,64,128]{2,1,0:T(8,128)(2,1)}, bf16[2,64,128]{2,1,0:T(8,128)(2,1)S(1)}, u32[]{:S(2)}, u32[]{:S(2)}) collective-permute-start(bf16[2,64,128]{2,1,0:T(8,128)(2,1)} %bitcast.9), channel_id=1, source_target_pairs={{0,8},{1,9},{2,10},{3,11},{4,12},{5,13},{6,14},{7,15},{8,0},{9,1},... | collective-permute-start | bytes 98312 | tf_op jit(solution)/shard_map/ppermute | solution.py:359
  4.8 0.6 %copy-done.10 = f32[128]{0:T(128)S(1)} copy-done((f32[128]{0:T(128)S(1)}, f32[128]{0:T(128)}, u32[]{:S(2)}) %copy-start.10) | copy-done | bytes 536
  5.5 1.3 %shard_map.147 = (f32[8,128,128]{2,1,0:T(8,128)S(1)}, f32[8,128,128]{2,1,0:T(8,128)S(1)}, bf16[1024,128]{1,0:T(8,128)(2,1)S(1)}, bf16[256,128]{1,0:T(8,128)(2,1)...) custom-call(s32[128]{0:T(128)S(1)} %copy-done.1, ...), custom_call_target="tpu_custom_call" | custom-call | flops 1073741824 | bytes 1048576 | tf_op jit(solution)/shard_map/pallas_call | solution.py:375
  7.2 0.7 %shard_map.148 = (bf16[256,128]{1,0:T(8,128)(2,1)S(1)}, bf16[512,128]{1,0:T(8,128)(2,1)S(1)}, bf16[768,128]{1,0:T(8,128)(2,1)S(1)}) custom-call(s32[32]{0:T(128)S(1)} %copy-done.2, s32[1,128]{1,0:T(1,128)S(1)} %bitcast.12, f32[1,64]{1,0:T(1,128)S(1)} %get-tuple-element.37.gain_ref, bf16[2,64,128]{2,1,0:T(8,128)(2,1)S(1)} %bitcast.10, ...), custom_call_target="tpu_custom_call" | custom-call | flops 1048576 | bytes 1048576 | tf_op jit(solution)/shard_map/pallas_call | solution.py:381
  7.9 1.6 %collective-permute-start.3 = (bf16[768,128]{1,0:T(8,128)(2,1)S(1)}, bf16[768,128]{1,0:T(8,128)(2,1)S(1)}, u32[]{:S(2)}, u32[]{:S(2)}) collective-permute-start(bf16[768,128]{1,0:T(8,128)(2,1)S(1)} %get-tuple-element.41), channel_id=1, source_target_pairs={{0,4},{1,5},{2,6},{3,7},{4,0},{5,1},{6,2},{7,3},{8,12},{9,13},{10,... | collective-permute-start | bytes 589832 | tf_op jit(solution)/shard_map/ppermute | solution.py:359
  9.5 1.5 %collective-permute-start.6 = (bf16[256,128]{1,0:T(8,128)(2,1)S(1)}, bf16[256,128]{1,0:T(8,128)(2,1)S(1)}, u32[]{:S(2)}, u32[]{:S(2)}) collective-permute-start(bf16[256,128]{1,0:T(8,128)(2,1)S(1)} %get-tuple-element.40.after_ref.y0_ref), channel_id=1, source_target_pairs={{0,2},{1,3},{2,0},{3,1},{4,6},{5,7},{6,4},{7,5},{8,10},{9,11},{10,... | collective-permute-start | bytes 196616 | tf_op jit(solution)/shard_map/ppermute | solution.py:359
  11.0 0.4 %collective-permute-start.1 = (bf16[256,128]{1,0:T(8,128)(2,1)S(1)}, bf16[256,128]{1,0:T(8,128)(2,1)S(1)}, u32[]{:S(2)}, u32[]{:S(2)}) collective-permute-start(bf16[256,128]{1,0:T(8,128)(2,1)S(1)} %get-tuple-element.40.after_ref.y0_ref), channel_id=1, source_target_pairs={{0,6},{1,7},{2,4},{3,5},{4,2},{5,3},{6,0},{7,1},{8,14},{9,15},{10,... | collective-permute-start | bytes 196616 | tf_op jit(solution)/shard_map/ppermute | solution.py:359
  11.5 1.2 %shard_map.149 = (bf16[1024,512]{1,0:T(8,128)(2,1)S(1)}, bf16[256,128]{1,0:T(8,128)(2,1)S(1)}, bf16[32,4096]{1,0:T(8,128)(2,1)S(1)}, bf16[32,1024]{1,0:T(8,128)(2,1)S(1)}) custom-call(bf16[32,64]{1,0:T(8,128)(2,1)S(1)} %bitcast.14, bf16[32,64]{1,0:T(8,128)(2,1)S(1)} %bitcast.15, bf16[1024,128]{1,0:T(8,128)(2,1)S(1)} %copy-done.4, ...), custom_call_target="tpu_custom_call" | custom-call | flops 1073741824 | bytes 1048576 | tf_op jit(solution)/shard_map/pallas_call | solution.py:386
  12.7 1.8 %collective-permute-done.6.refs_0_ = bf16[256,128]{1,0:T(8,128)(2,1)S(1)} collective-permute-done((bf16[256,128]{1,0:T(8,128)(2,1)S(1)}, bf16[256,128]{1,0:T(8,128)(2,1)S(1)}, u32[]{:S(2)}, u32[]{:S(2)}) %collective-permute-start.6) | collective-permute-done | bytes 65568 | tf_op jit(solution)/shard_map/ppermute | solution.py:359
  14.5 1.8 %collective-permute-done.1.y0_ref = bf16[256,128]{1,0:T(8,128)(2,1)S(1)} collective-permute-done((bf16[256,128]{1,0:T(8,128)(2,1)S(1)}, bf16[256,128]{1,0:T(8,128)(2,1)S(1)}, u32[]{:S(2)}, u32[]{:S(2)}) %collective-permute-start.1) | collective-permute-done | bytes 65568 | tf_op jit(solution)/shard_map/ppermute | solution.py:359
  16.3 0.5 %collective-permute-start.4 = (bf16[768,128]{1,0:T(8,128)(2,1)S(1)}, bf16[768,128]{1,0:T(8,128)(2,1)S(1)}, u32[]{:S(2)}, u32[]{:S(2)}) collective-permute-start(bf16[768,128]{1,0:T(8,128)(2,1)S(1)} %collective-permute-done.3.y2_ref.across_ref), channel_id=1, source_target_pairs={{0,1},{1,0},{2,3},{3,2},{4,5},{5,4},{6,7},{7,6},{8,9},{9,8},{10,11... | collective-permute-start | bytes 589832 | tf_op jit(solution)/shard_map/ppermute | solution.py:359
  16.8 1.7 %shard_map.151 = (f32[128,1024]{1,0:T(8,128)S(1)}, f32[64,128]{1,0:T(8,128)S(1)}, bf16[512,128]{1,0:T(8,128)(2,1)S(1)}, bf16[128,256]{1,0:T(8,128)(2,1)S(1)}) custom-call(bf16[256,128]{1,0:T(8,128)(2,1)S(1)} %get-tuple-element.40.after_ref.y0_ref, bf16[512,128]{1,0:T(8,128)(2,1)S(1)} %collective-permute-done.5.y1_ref.core_ref, ...), custom_call_target="tpu_custom_call" | custom-call | flops 2147483648 | bytes 1048576 | tf_op jit(solution)/shard_map/pallas_call | solution.py:400
  18.5 1.9 %shard_map.152 = (f32[8,128,128]{2,1,0:T(8,128)S(1)}, bf16[64,128]{1,0:T(8,128)(2,1)S(1)}, bf16[64,128]{1,0:T(8,128)(2,1)S(1)}, f32[32,64]{1,0:T(8,128)S(1)}, bf...) custom-call(bf16[256,128]{1,0:T(8,128)(2,1)S(1)} %collective-permute-done.1.y0_ref, ...), custom_call_target="tpu_custom_call" | custom-call | flops 2147483648 | bytes 1048576 | tf_op jit(solution)/shard_map/pallas_call | solution.py:405
  20.5 1.7 %shard_map.153.sums_ref = bf16[288,128]{1,0:T(8,128)(2,1)S(1)} custom-call(bf16[512,128]{1,0:T(8,128)(2,1)S(1)} %get-tuple-element.52.right0_ref, bf16[512,128]{1,0:T(8,128)(2,1)S(1)} %get-tuple-element.53.right1_ref, bf16[128,256]{1,0:T(8,128)(2,1)S(1)} %get-tuple-element.54.own0_ref, bf16[128,256]{1,0:T(8,128)(2,1)S(1)} %get-tuple-element.55.own1_ref, ...), custom_call_target="tpu_custom_call" | custom-call | flops 1073741824 | bytes 1048576 | tf_op jit(solution)/shard_map/pallas_call | solution.py:410
  22.2 2.8 %collective-permute-start.9 = (bf16[352,128]{1,0:T(8,128)(2,1)S(1)}, bf16[352,128]{1,0:T(8,128)(2,1)S(1)}, u32[]{:S(2)}, u32[]{:S(2)}) collective-permute-start(bf16[352,128]{1,0:T(8,128)(2,1)S(1)} %shard_map.154.after_ref.own_ref), channel_id=1, source_target_pairs={{0,8},{1,9},{2,10},{3,11},{4,12},{5,13},{6,14},{7,15},{8,0},{9,1},... | collective-permute-start | bytes 270344 | tf_op jit(solution)/shard_map/ppermute | solution.py:359
  25.0 0.8 %shard_map.155 = (bf16[8,128,128]{2,1,0:T(8,128)(2,1)}, f32[8,128]{1,0:T(8,128)S(1)}) custom-call(f32[8,128,128]{2,1,0:T(8,128)S(1)} %get-tuple-element.36.scale_ref, f32[8,128,128]{2,1,0:T(8,128)S(1)} %get-tuple-element.51.value_ref, bf16[352,128]{1,0:T(8,128)(2,1)S(1)} %shard_map.154.after_ref.own_ref), custom_call_target="tpu_custom_call" | custom-call | flops 1073741824 | bytes 1048576 | tf_op jit(solution)/shard_map/pallas_call | solution.py:414
  25.8 4.4 %collective-permute-done.9.other_ref = bf16[352,128]{1,0:T(8,128)(2,1)S(1)} collective-permute-done((bf16[352,128]{1,0:T(8,128)(2,1)S(1)}, bf16[352,128]{1,0:T(8,128)(2,1)S(1)}, u32[]{:S(2)}, u32[]{:S(2)}) %collective-permute-start.9) | collective-permute-done | bytes 90144 | tf_op jit(solution)/shard_map/ppermute | solution.py:359
  30.2 0.5 %collective-permute-start.12 = (bf16[352,128]{1,0:T(8,128)(2,1)S(1)}, bf16[352,128]{1,0:T(8,128)(2,1)S(1)}, u32[]{:S(2)}, u32[]{:S(2)}) collective-permute-start(bf16[352,128]{1,0:T(8,128)(2,1)S(1)} %shard_map.156.own_ref), channel_id=1, source_target_pairs={{0,6},{1,7},{2,4},{3,5},{4,2},{5,3},{6,0},{7,1},{8,14},{9,15},{10,... | collective-permute-start | bytes 270344 | tf_op jit(solution)/shard_map/ppermute | solution.py:359
  30.7 1.6 %collective-permute-start.11 = (bf16[352,128]{1,0:T(8,128)(2,1)S(1)}, bf16[352,128]{1,0:T(8,128)(2,1)S(1)}, u32[]{:S(2)}, u32[]{:S(2)}) collective-permute-start(bf16[352,128]{1,0:T(8,128)(2,1)S(1)} %shard_map.156.own_ref), channel_id=1, source_target_pairs={{0,4},{1,5},{2,6},{3,7},{4,0},{5,1},{6,2},{7,3},{8,12},{9,13},{10,... | collective-permute-start | bytes 270344 | tf_op jit(solution)/shard_map/ppermute | solution.py:359
  32.3 1.5 %collective-permute-start.10 = (bf16[352,128]{1,0:T(8,128)(2,1)S(1)}, bf16[352,128]{1,0:T(8,128)(2,1)S(1)}, u32[]{:S(2)}, u32[]{:S(2)}) collective-permute-start(bf16[352,128]{1,0:T(8,128)(2,1)S(1)} %shard_map.156.own_ref), channel_id=1, source_target_pairs={{0,2},{1,3},{2,0},{3,1},{4,6},{5,7},{6,4},{7,5},{8,10},{9,11},{10,... | collective-permute-start | bytes 270344 | tf_op jit(solution)/shard_map/ppermute | solution.py:359
  33.8 2.7 %collective-permute-done.12.both_ref = bf16[352,128]{1,0:T(8,128)(2,1)S(1)} collective-permute-done((bf16[352,128]{1,0:T(8,128)(2,1)S(1)}, bf16[352,128]{1,0:T(8,128)(2,1)S(1)}, u32[]{:S(2)}, u32[]{:S(2)}) %collective-permute-start.12) | collective-permute-done | bytes 90144 | tf_op jit(solution)/shard_map/ppermute | solution.py:359
  36.5 0.9 %collective-permute-done.10.beside_ref = bf16[352,128]{1,0:T(8,128)(2,1)S(1)} collective-permute-done((bf16[352,128]{1,0:T(8,128)(2,1)S(1)}, bf16[352,128]{1,0:T(8,128)(2,1)S(1)}, u32[]{:S(2)}, u32[]{:S(2)}) %collective-permute-start.10) | collective-permute-done | bytes 90144 | tf_op jit(solution)/shard_map/ppermute | solution.py:359
  37.6 1.4 %collective-permute-done.13.other_ref = bf16[608,128]{1,0:T(8,128)(2,1)S(1)} collective-permute-done((bf16[608,128]{1,0:T(8,128)(2,1)S(1)}, bf16[608,128]{1,0:T(8,128)(2,1)S(1)}, u32[]{:S(2)}, u32[]{:S(2)}) %collective-permute-start.13) | collective-permute-done | bytes 155680 | tf_op jit(solution)/shard_map/ppermute | solution.py:359
  38.9 1.4 %shard_map.158 = (f32[1024,128]{1,0:T(8,128)}, f32[128,128]{1,0:T(8,128)}, f32[32,64]{1,0:T(8,128)}, f32[32,64]{1,0:T(8,128)}) custom-call(bf16[608,128]{1,0:T(8,128)(2,1)S(1)} %shard_map.157.local_ref, bf16[608,128]{1,0:T(8,128)(2,1)S(1)} %collective-permute-done.13.other_ref), custom_call_target="tpu_custom_call" | custom-call | flops 1048576 | bytes 1048576 | tf_op jit(solution)/shard_map/pallas_call | solution.py:419
  (39 shorter events, 0.8 us)
Async XLA Ops:
  0.6 4.2 %copy-start.3 = (bf16[8,128,128]{2,1,0:T(8,128)(2,1)S(1)}, bf16[8,128,128]{2,1,0:T(8,128)(2,1)}, u32[]{:S(2)}) copy-start(bf16[8,128,128]{2,1,0:T(8,128)(2,1)} %cot_ref.1) | copy-start | bytes 786436
  0.6 4.2 %copy-start.5 = (bf16[8,128,128]{2,1,0:T(8,128)(2,1)S(1)}, bf16[8,128,128]{2,1,0:T(8,128)(2,1)}, u32[]{:S(2)}) copy-start(bf16[8,128,128]{2,1,0:T(8,128)(2,1)} %pair_ref.3) | copy-start | bytes 786436
  0.7 4.2 %copy-start.6 = (bf16[128,128]{1,0:T(8,128)(2,1)S(1)}, bf16[128,128]{1,0:T(8,128)(2,1)}, u32[]{:S(2)}) copy-start(bf16[128,128]{1,0:T(8,128)(2,1)} %gate_ref.1) | copy-start | bytes 98308
  0.7 6.6 %collective-permute-start = (bf16[2,64,128]{2,1,0:T(8,128)(2,1)}, bf16[2,64,128]{2,1,0:T(8,128)(2,1)S(1)}, u32[]{:S(2)}, u32[]{:S(2)}) collective-permute-start(bf16[2,64,128]{2,1,0:T(8,128)(2,1)} %bitcast.9), channel_id=1, source_target_pairs={{0,8},{1,9},{2,10},{3,11},{4,12},{5,13},{6,14},{7,15},{8,0},{9,1},... | collective-permute-start | bytes 98312 | tf_op jit(solution)/shard_map/ppermute | solution.py:359
  4.8 0.7 %copy-start.1 = (s32[128]{0:T(128)S(1)}, s32[128]{0:T(128)}, u32[]{:S(2)}) copy-start(s32[128]{0:T(128)} %res_s_ref.1) | copy-start | bytes 1540
  4.8 0.7 %copy-start.2 = (s32[32]{0:T(128)S(1)}, s32[32]{0:T(128)}, u32[]{:S(2)}) copy-start(s32[32]{0:T(128)} %seq_ref.1) | copy-start | bytes 388
  4.8 0.7 %copy-start.9 = (f32[64]{0:T(128)S(1)}, f32[64]{0:T(128)}, u32[]{:S(2)}) copy-start(f32[64]{0:T(128)} %param.16) | copy-start | bytes 772
  5.5 1.8 %copy-start = (bf16[2,128,64]{1,2,0:T(8,128)(2,1)S(1)}, bf16[2,128,64]{1,2,0:T(8,128)(2,1)}, u32[]{:S(2)}) copy-start(bf16[2,128,64]{1,2,0:T(8,128)(2,1)} %param.11) | copy-start | bytes 98308
  5.5 6.0 %copy-start.8 = (bf16[64,32]{0,1:T(8,128)(2,1)S(1)}, bf16[64,32]{0,1:T(8,128)(2,1)}, u32[]{:S(2)}) copy-start(bf16[64,32]{0,1:T(8,128)(2,1)} %param.17) | copy-start | bytes 12292
  6.8 4.7 %copy-start.4 = (bf16[1024,128]{1,0:T(8,128)(2,1)S(1)}, bf16[1024,128]{1,0:T(8,128)(2,1)}, u32[]{:S(2)}) copy-start(bf16[1024,128]{1,0:T(8,128)(2,1)} %out_w_ref.1) | copy-start | bytes 786436
  7.9 3.6 %copy-start.7 = (bf16[64,32]{0,1:T(8,128)(2,1)S(1)}, bf16[64,32]{0,1:T(8,128)(2,1)}, u32[]{:S(2)}) copy-start(bf16[64,32]{0,1:T(8,128)(2,1)} %param.18) | copy-start | bytes 12292
  7.9 8.4 %collective-permute-start.3 = (bf16[768,128]{1,0:T(8,128)(2,1)S(1)}, bf16[768,128]{1,0:T(8,128)(2,1)S(1)}, u32[]{:S(2)}, u32[]{:S(2)}) collective-permute-start(bf16[768,128]{1,0:T(8,128)(2,1)S(1)} %get-tuple-element.41), channel_id=1, source_target_pairs={{0,4},{1,5},{2,6},{3,7},{4,0},{5,1},{6,2},{7,3},{8,12},{9,13},{10,... | collective-permute-start | bytes 589832 | tf_op jit(solution)/shard_map/ppermute | solution.py:359
  9.5 5.0 %collective-permute-start.6 = (bf16[256,128]{1,0:T(8,128)(2,1)S(1)}, bf16[256,128]{1,0:T(8,128)(2,1)S(1)}, u32[]{:S(2)}, u32[]{:S(2)}) collective-permute-start(bf16[256,128]{1,0:T(8,128)(2,1)S(1)} %get-tuple-element.40.after_ref.y0_ref), channel_id=1, source_target_pairs={{0,2},{1,3},{2,0},{3,1},{4,6},{5,7},{6,4},{7,5},{8,10},{9,11},{10,... | collective-permute-start | bytes 196616 | tf_op jit(solution)/shard_map/ppermute | solution.py:359
  11.0 5.3 %collective-permute-start.1 = (bf16[256,128]{1,0:T(8,128)(2,1)S(1)}, bf16[256,128]{1,0:T(8,128)(2,1)S(1)}, u32[]{:S(2)}, u32[]{:S(2)}) collective-permute-start(bf16[256,128]{1,0:T(8,128)(2,1)S(1)} %get-tuple-element.40.after_ref.y0_ref), channel_id=1, source_target_pairs={{0,6},{1,7},{2,4},{3,5},{4,2},{5,3},{6,0},{7,1},{8,14},{9,15},{10,... | collective-permute-start | bytes 196616 | tf_op jit(solution)/shard_map/ppermute | solution.py:359
  11.5 5.3 %collective-permute-start.5 = (bf16[512,128]{1,0:T(8,128)(2,1)S(1)}, bf16[512,128]{1,0:T(8,128)(2,1)S(1)}, u32[]{:S(2)}, u32[]{:S(2)}) collective-permute-start(bf16[512,128]{1,0:T(8,128)(2,1)S(1)} %get-tuple-element.46), channel_id=1, source_target_pairs={{0,1},{1,0},{2,3},{3,2},{4,5},{5,4},{6,7},{7,6},{8,9},{9,8},{10,11... | collective-permute-start | bytes 393224 | tf_op jit(solution)/shard_map/ppermute | solution.py:359
  14.5 2.3 %collective-permute-start.7 = (bf16[256,128]{1,0:T(8,128)(2,1)S(1)}, bf16[256,128]{1,0:T(8,128)(2,1)S(1)}, u32[]{:S(2)}, u32[]{:S(2)}) collective-permute-start(bf16[256,128]{1,0:T(8,128)(2,1)S(1)} %shard_map.150.y2_ref), channel_id=1, source_target_pairs={{0,1},{1,0},{2,3},{3,2},{4,5},{5,4},{6,7},{7,6},{8,9},{9,8},{10,11... | collective-permute-start | bytes 196616 | tf_op jit(solution)/shard_map/ppermute | solution.py:359
  16.3 2.2 %collective-permute-start.2 = (bf16[256,128]{1,0:T(8,128)(2,1)S(1)}, bf16[256,128]{1,0:T(8,128)(2,1)S(1)}, u32[]{:S(2)}, u32[]{:S(2)}) collective-permute-start(bf16[256,128]{1,0:T(8,128)(2,1)S(1)} %collective-permute-done.1.y0_ref), channel_id=1, source_target_pairs={{0,1},{1,0},{2,3},{3,2},{4,5},{5,4},{6,7},{7,6},{8,9},{9,8},{10,11... | collective-permute-start | bytes 196616 | tf_op jit(solution)/shard_map/ppermute | solution.py:359
  16.3 2.2 %collective-permute-start.4 = (bf16[768,128]{1,0:T(8,128)(2,1)S(1)}, bf16[768,128]{1,0:T(8,128)(2,1)S(1)}, u32[]{:S(2)}, u32[]{:S(2)}) collective-permute-start(bf16[768,128]{1,0:T(8,128)(2,1)S(1)} %collective-permute-done.3.y2_ref.across_ref), channel_id=1, source_target_pairs={{0,1},{1,0},{2,3},{3,2},{4,5},{5,4},{6,7},{7,6},{8,9},{9,8},{10,11... | collective-permute-start | bytes 589832 | tf_op jit(solution)/shard_map/ppermute | solution.py:359
  20.4 1.8 %collective-permute-start.8 = (bf16[64,128]{1,0:T(8,128)(2,1)S(1)}, bf16[64,128]{1,0:T(8,128)(2,1)S(1)}, u32[]{:S(2)}, u32[]{:S(2)}) collective-permute-start(bf16[64,128]{1,0:T(8,128)(2,1)S(1)} %get-tuple-element.60), channel_id=1, source_target_pairs={{0,1},{1,0},{2,3},{3,2},{4,5},{5,4},{6,7},{7,6},{8,9},{9,8},{10,11... | collective-permute-start | bytes 49160 | tf_op jit(solution)/shard_map/ppermute | solution.py:359
  22.2 8.0 %collective-permute-start.9 = (bf16[352,128]{1,0:T(8,128)(2,1)S(1)}, bf16[352,128]{1,0:T(8,128)(2,1)S(1)}, u32[]{:S(2)}, u32[]{:S(2)}) collective-permute-start(bf16[352,128]{1,0:T(8,128)(2,1)S(1)} %shard_map.154.after_ref.own_ref), channel_id=1, source_target_pairs={{0,8},{1,9},{2,10},{3,11},{4,12},{5,13},{6,14},{7,15},{8,0},{9,1},... | collective-permute-start | bytes 270344 | tf_op jit(solution)/shard_map/ppermute | solution.py:359
  30.2 6.3 %collective-permute-start.12 = (bf16[352,128]{1,0:T(8,128)(2,1)S(1)}, bf16[352,128]{1,0:T(8,128)(2,1)S(1)}, u32[]{:S(2)}, u32[]{:S(2)}) collective-permute-start(bf16[352,128]{1,0:T(8,128)(2,1)S(1)} %shard_map.156.own_ref), channel_id=1, source_target_pairs={{0,6},{1,7},{2,4},{3,5},{4,2},{5,3},{6,0},{7,1},{8,14},{9,15},{10,... | collective-permute-start | bytes 270344 | tf_op jit(solution)/shard_map/ppermute | solution.py:359
  30.7 5.8 %collective-permute-start.11 = (bf16[352,128]{1,0:T(8,128)(2,1)S(1)}, bf16[352,128]{1,0:T(8,128)(2,1)S(1)}, u32[]{:S(2)}, u32[]{:S(2)}) collective-permute-start(bf16[352,128]{1,0:T(8,128)(2,1)S(1)} %shard_map.156.own_ref), channel_id=1, source_target_pairs={{0,4},{1,5},{2,6},{3,7},{4,0},{5,1},{6,2},{7,3},{8,12},{9,13},{10,... | collective-permute-start | bytes 270344 | tf_op jit(solution)/shard_map/ppermute | solution.py:359
  32.3 5.1 %collective-permute-start.10 = (bf16[352,128]{1,0:T(8,128)(2,1)S(1)}, bf16[352,128]{1,0:T(8,128)(2,1)S(1)}, u32[]{:S(2)}, u32[]{:S(2)}) collective-permute-start(bf16[352,128]{1,0:T(8,128)(2,1)S(1)} %shard_map.156.own_ref), channel_id=1, source_target_pairs={{0,2},{1,3},{2,0},{3,1},{4,6},{5,7},{6,4},{7,5},{8,10},{9,11},{10,... | collective-permute-start | bytes 270344 | tf_op jit(solution)/shard_map/ppermute | solution.py:359
  37.5 1.4 %collective-permute-start.13 = (bf16[608,128]{1,0:T(8,128)(2,1)S(1)}, bf16[608,128]{1,0:T(8,128)(2,1)S(1)}, u32[]{:S(2)}, u32[]{:S(2)}) collective-permute-start(bf16[608,128]{1,0:T(8,128)(2,1)S(1)} %shard_map.157.local_ref), channel_id=1, source_target_pairs={{0,1},{1,0},{2,3},{3,2},{4,5},{5,4},{6,7},{7,6},{8,9},{9,8},{10,11... | collective-permute-start | bytes 466952 | tf_op jit(solution)/shard_map/ppermute | solution.py:359
  (1 other events, 0.7 us)

commit v7 on v6

--- a/solution.py
+++ b/solution.py
@@ -193,10 +193,9 @@
                 m_ref[e * GROUP : (e + 1) * GROUP, i * n : (i + 1) * n] = part[
                     i * GROUP : (i + 1) * GROUP, el * n : (el + 1) * n
                 ]
+        at = slice(e8 * 8 * GROUP, (e8 + 1) * 8 * GROUP)
+        right_ref[at, :] = dot(m_ref[at, :], turned[...])
     linear = dot(right, m_ref[...])
-    for k in range(4):
-        at = slice(k * 128, (k + 1) * 128)
-        right_ref[at, :] = dot(m_ref[at, :], turned[...])
     for t in range(8):
         for s in range(2):
             flat_ref[s * width : (s + 1) * width, t * n : (t + 1) * n] = right_ref[

time: 40.5 us -> 41 us (1.012)
  Pallas kernels: 10.7 us -> 11.2 us
where the time goes in v7:
time: 41 us; the launch traced here: 40.8 us
  starting transfers between devices  14.7 us (36%)
  waiting for transfers between devices  13.5 us (33%)
  Pallas kernels  11.2 us (27%)
  between operations  0.82 us (2%)
  local copies, waits for them, and re-layouts  0.69 us (2%)
    ppermute x14, starting transfers between devices, swap(): return lax.ppermute(x, 'row', [(i, i ^ bit) for i in range(size)])  14.7 us
    ppermute x14, waiting for transfers between devices, swap(): return lax.ppermute(x, 'row', [(i, i ^ bit) for i in range(size)])  13.5 us
    pallas_call x1, Pallas kernels, one_column(): call(pair_kernel, [((rows, n, n), F32), ((n // 2, n), BF16), ((n // 2, n)...  2.05 us
    pallas_call x1, Pallas kernels, one_column(): call(half_kernel, [((n, rows * n), F32), ((64, n), F32), *kept], scratch=...  2.03 us
    pallas_call x1, Pallas kernels, one_column(): call(out_kernel, [((288, n), BF16)], scratch=[((256, 32 * n), BF16)], ins...  1.67 us
    pallas_call x1, Pallas kernels, one_column(): call(last_kernel, [((1024, n), F32), ((n, n), F32), ((32, 64), F32), ((32...  1.38 us
    pallas_call x1, Pallas kernels, one_column(): call(gate_kernel, [((rows, n, n), F32), ((rows, n, n), F32), ((rows * n,...  1.32 us
    pallas_call x1, Pallas kernels, one_column(): call(weight_kernel, [((1024, 512), BF16), ((256, n), BF16), ((32, 32 * n)...  1.22 us
  transfers between devices with their start and end apart: 14, of which 7 were waited for; matrix products, arithmetic and copies ran while one was open for 0% of the time, Pallas kernels for 17%

profile of v7, /device:TPU:0, one launch (start us, length us, event | category | flops | bytes accessed | tf_op | source)
XLA Modules:
  0.0 40.8 jit_solution(1103497579769586089)
XLA Ops:
  0.7 4.1 %collective-permute-start = (bf16[2,64,128]{2,1,0:T(8,128)(2,1)}, bf16[2,64,128]{2,1,0:T(8,128)(2,1)S(1)}, u32[]{:S(2)}, u32[]{:S(2)}) collective-permute-start(bf16[2,64,128]{2,1,0:T(8,128)(2,1)} %bitcast.9), channel_id=1, source_target_pairs={{0,8},{1,9},{2,10},{3,11},{4,12},{5,13},{6,14},{7,15},{8,0},{9,1},... | collective-permute-start | bytes 98312 | tf_op jit(solution)/shard_map/ppermute | solution.py:358
  4.8 0.6 %copy-done.10 = f32[128]{0:T(128)S(1)} copy-done((f32[128]{0:T(128)S(1)}, f32[128]{0:T(128)}, u32[]{:S(2)}) %copy-start.10) | copy-done | bytes 536
  5.5 1.3 %shard_map.147 = (f32[8,128,128]{2,1,0:T(8,128)S(1)}, f32[8,128,128]{2,1,0:T(8,128)S(1)}, bf16[1024,128]{1,0:T(8,128)(2,1)S(1)}, bf16[256,128]{1,0:T(8,128)(2,1)...) custom-call(s32[128]{0:T(128)S(1)} %copy-done.1, ...), custom_call_target="tpu_custom_call" | custom-call | flops 1073741824 | bytes 1048576 | tf_op jit(solution)/shard_map/pallas_call | solution.py:374
  7.2 0.7 %shard_map.148 = (bf16[256,128]{1,0:T(8,128)(2,1)S(1)}, bf16[512,128]{1,0:T(8,128)(2,1)S(1)}, bf16[768,128]{1,0:T(8,128)(2,1)S(1)}) custom-call(s32[32]{0:T(128)S(1)} %copy-done.2, s32[1,128]{1,0:T(1,128)S(1)} %bitcast.12, f32[1,64]{1,0:T(1,128)S(1)} %get-tuple-element.37.gain_ref, bf16[2,64,128]{2,1,0:T(8,128)(2,1)S(1)} %bitcast.10, ...), custom_call_target="tpu_custom_call" | custom-call | flops 1048576 | bytes 1048576 | tf_op jit(solution)/shard_map/pallas_call | solution.py:380
  7.9 1.6 %collective-permute-start.3 = (bf16[768,128]{1,0:T(8,128)(2,1)S(1)}, bf16[768,128]{1,0:T(8,128)(2,1)S(1)}, u32[]{:S(2)}, u32[]{:S(2)}) collective-permute-start(bf16[768,128]{1,0:T(8,128)(2,1)S(1)} %get-tuple-element.41), channel_id=1, source_target_pairs={{0,4},{1,5},{2,6},{3,7},{4,0},{5,1},{6,2},{7,3},{8,12},{9,13},{10,... | collective-permute-start | bytes 589832 | tf_op jit(solution)/shard_map/ppermute | solution.py:358
  9.5 1.5 %collective-permute-start.6 = (bf16[256,128]{1,0:T(8,128)(2,1)S(1)}, bf16[256,128]{1,0:T(8,128)(2,1)S(1)}, u32[]{:S(2)}, u32[]{:S(2)}) collective-permute-start(bf16[256,128]{1,0:T(8,128)(2,1)S(1)} %get-tuple-element.40.after_ref.y0_ref), channel_id=1, source_target_pairs={{0,2},{1,3},{2,0},{3,1},{4,6},{5,7},{6,4},{7,5},{8,10},{9,11},{10,... | collective-permute-start | bytes 196616 | tf_op jit(solution)/shard_map/ppermute | solution.py:358
  11.0 0.4 %collective-permute-start.1 = (bf16[256,128]{1,0:T(8,128)(2,1)S(1)}, bf16[256,128]{1,0:T(8,128)(2,1)S(1)}, u32[]{:S(2)}, u32[]{:S(2)}) collective-permute-start(bf16[256,128]{1,0:T(8,128)(2,1)S(1)} %get-tuple-element.40.after_ref.y0_ref), channel_id=1, source_target_pairs={{0,6},{1,7},{2,4},{3,5},{4,2},{5,3},{6,0},{7,1},{8,14},{9,15},{10,... | collective-permute-start | bytes 196616 | tf_op jit(solution)/shard_map/ppermute | solution.py:358
  11.5 1.2 %shard_map.149 = (bf16[1024,512]{1,0:T(8,128)(2,1)S(1)}, bf16[256,128]{1,0:T(8,128)(2,1)S(1)}, bf16[32,4096]{1,0:T(8,128)(2,1)S(1)}, bf16[32,1024]{1,0:T(8,128)(2,1)S(1)}) custom-call(bf16[32,64]{1,0:T(8,128)(2,1)S(1)} %bitcast.14, bf16[32,64]{1,0:T(8,128)(2,1)S(1)} %bitcast.15, bf16[1024,128]{1,0:T(8,128)(2,1)S(1)} %copy-done.4, ...), custom_call_target="tpu_custom_call" | custom-call | flops 1073741824 | bytes 1048576 | tf_op jit(solution)/shard_map/pallas_call | solution.py:385
  12.7 1.8 %collective-permute-done.6.refs_0_ = bf16[256,128]{1,0:T(8,128)(2,1)S(1)} collective-permute-done((bf16[256,128]{1,0:T(8,128)(2,1)S(1)}, bf16[256,128]{1,0:T(8,128)(2,1)S(1)}, u32[]{:S(2)}, u32[]{:S(2)}) %collective-permute-start.6) | collective-permute-done | bytes 65568 | tf_op jit(solution)/shard_map/ppermute | solution.py:358
  14.5 1.8 %collective-permute-done.1.y0_ref = bf16[256,128]{1,0:T(8,128)(2,1)S(1)} collective-permute-done((bf16[256,128]{1,0:T(8,128)(2,1)S(1)}, bf16[256,128]{1,0:T(8,128)(2,1)S(1)}, u32[]{:S(2)}, u32[]{:S(2)}) %collective-permute-start.1) | collective-permute-done | bytes 65568 | tf_op jit(solution)/shard_map/ppermute | solution.py:358
  16.3 0.5 %collective-permute-start.4 = (bf16[768,128]{1,0:T(8,128)(2,1)S(1)}, bf16[768,128]{1,0:T(8,128)(2,1)S(1)}, u32[]{:S(2)}, u32[]{:S(2)}) collective-permute-start(bf16[768,128]{1,0:T(8,128)(2,1)S(1)} %collective-permute-done.3.y2_ref.across_ref), channel_id=1, source_target_pairs={{0,1},{1,0},{2,3},{3,2},{4,5},{5,4},{6,7},{7,6},{8,9},{9,8},{10,11... | collective-permute-start | bytes 589832 | tf_op jit(solution)/shard_map/ppermute | solution.py:358
  16.8 2.0 %shard_map.151 = (f32[128,1024]{1,0:T(8,128)S(1)}, f32[64,128]{1,0:T(8,128)S(1)}, bf16[512,128]{1,0:T(8,128)(2,1)S(1)}, bf16[128,256]{1,0:T(8,128)(2,1)S(1)}) custom-call(bf16[256,128]{1,0:T(8,128)(2,1)S(1)} %get-tuple-element.40.after_ref.y0_ref, bf16[512,128]{1,0:T(8,128)(2,1)S(1)} %collective-permute-done.5.y1_ref.core_ref, ...), custom_call_target="tpu_custom_call" | custom-call | flops 2147483648 | bytes 1048576 | tf_op jit(solution)/shard_map/pallas_call | solution.py:399
  18.9 2.0 %shard_map.152 = (f32[8,128,128]{2,1,0:T(8,128)S(1)}, bf16[64,128]{1,0:T(8,128)(2,1)S(1)}, bf16[64,128]{1,0:T(8,128)(2,1)S(1)}, f32[32,64]{1,0:T(8,128)S(1)}, bf...) custom-call(bf16[256,128]{1,0:T(8,128)(2,1)S(1)} %collective-permute-done.1.y0_ref, ...), custom_call_target="tpu_custom_call" | custom-call | flops 2147483648 | bytes 1048576 | tf_op jit(solution)/shard_map/pallas_call | solution.py:404
  21.0 1.7 %shard_map.153.sums_ref = bf16[288,128]{1,0:T(8,128)(2,1)S(1)} custom-call(bf16[512,128]{1,0:T(8,128)(2,1)S(1)} %get-tuple-element.52.right0_ref, bf16[512,128]{1,0:T(8,128)(2,1)S(1)} %get-tuple-element.53.right1_ref, bf16[128,256]{1,0:T(8,128)(2,1)S(1)} %get-tuple-element.54.own0_ref, bf16[128,256]{1,0:T(8,128)(2,1)S(1)} %get-tuple-element.55.own1_ref, ...), custom_call_target="tpu_custom_call" | custom-call | flops 1073741824 | bytes 1048576 | tf_op jit(solution)/shard_map/pallas_call | solution.py:409
  22.7 2.8 %collective-permute-start.9 = (bf16[352,128]{1,0:T(8,128)(2,1)S(1)}, bf16[352,128]{1,0:T(8,128)(2,1)S(1)}, u32[]{:S(2)}, u32[]{:S(2)}) collective-permute-start(bf16[352,128]{1,0:T(8,128)(2,1)S(1)} %shard_map.154.after_ref.own_ref), channel_id=1, source_target_pairs={{0,8},{1,9},{2,10},{3,11},{4,12},{5,13},{6,14},{7,15},{8,0},{9,1},... | collective-permute-start | bytes 270344 | tf_op jit(solution)/shard_map/ppermute | solution.py:358
  25.5 0.8 %shard_map.155 = (bf16[8,128,128]{2,1,0:T(8,128)(2,1)}, f32[8,128]{1,0:T(8,128)S(1)}) custom-call(f32[8,128,128]{2,1,0:T(8,128)S(1)} %get-tuple-element.36.scale_ref, f32[8,128,128]{2,1,0:T(8,128)S(1)} %get-tuple-element.51.value_ref, bf16[352,128]{1,0:T(8,128)(2,1)S(1)} %shard_map.154.after_ref.own_ref), custom_call_target="tpu_custom_call" | custom-call | flops 1073741824 | bytes 1048576 | tf_op jit(solution)/shard_map/pallas_call | solution.py:413
  26.3 4.4 %collective-permute-done.9.other_ref = bf16[352,128]{1,0:T(8,128)(2,1)S(1)} collective-permute-done((bf16[352,128]{1,0:T(8,128)(2,1)S(1)}, bf16[352,128]{1,0:T(8,128)(2,1)S(1)}, u32[]{:S(2)}, u32[]{:S(2)}) %collective-permute-start.9) | collective-permute-done | bytes 90144 | tf_op jit(solution)/shard_map/ppermute | solution.py:358
  30.7 0.5 %collective-permute-start.12 = (bf16[352,128]{1,0:T(8,128)(2,1)S(1)}, bf16[352,128]{1,0:T(8,128)(2,1)S(1)}, u32[]{:S(2)}, u32[]{:S(2)}) collective-permute-start(bf16[352,128]{1,0:T(8,128)(2,1)S(1)} %shard_map.156.own_ref), channel_id=1, source_target_pairs={{0,6},{1,7},{2,4},{3,5},{4,2},{5,3},{6,0},{7,1},{8,14},{9,15},{10,... | collective-permute-start | bytes 270344 | tf_op jit(solution)/shard_map/ppermute | solution.py:358
  31.2 1.6 %collective-permute-start.11 = (bf16[352,128]{1,0:T(8,128)(2,1)S(1)}, bf16[352,128]{1,0:T(8,128)(2,1)S(1)}, u32[]{:S(2)}, u32[]{:S(2)}) collective-permute-start(bf16[352,128]{1,0:T(8,128)(2,1)S(1)} %shard_map.156.own_ref), channel_id=1, source_target_pairs={{0,4},{1,5},{2,6},{3,7},{4,0},{5,1},{6,2},{7,3},{8,12},{9,13},{10,... | collective-permute-start | bytes 270344 | tf_op jit(solution)/shard_map/ppermute | solution.py:358
  32.8 1.5 %collective-permute-start.10 = (bf16[352,128]{1,0:T(8,128)(2,1)S(1)}, bf16[352,128]{1,0:T(8,128)(2,1)S(1)}, u32[]{:S(2)}, u32[]{:S(2)}) collective-permute-start(bf16[352,128]{1,0:T(8,128)(2,1)S(1)} %shard_map.156.own_ref), channel_id=1, source_target_pairs={{0,2},{1,3},{2,0},{3,1},{4,6},{5,7},{6,4},{7,5},{8,10},{9,11},{10,... | collective-permute-start | bytes 270344 | tf_op jit(solution)/shard_map/ppermute | solution.py:358
  34.3 2.7 %collective-permute-done.12.both_ref = bf16[352,128]{1,0:T(8,128)(2,1)S(1)} collective-permute-done((bf16[352,128]{1,0:T(8,128)(2,1)S(1)}, bf16[352,128]{1,0:T(8,128)(2,1)S(1)}, u32[]{:S(2)}, u32[]{:S(2)}) %collective-permute-start.12) | collective-permute-done | bytes 90144 | tf_op jit(solution)/shard_map/ppermute | solution.py:358
  37.0 0.9 %collective-permute-done.10.beside_ref = bf16[352,128]{1,0:T(8,128)(2,1)S(1)} collective-permute-done((bf16[352,128]{1,0:T(8,128)(2,1)S(1)}, bf16[352,128]{1,0:T(8,128)(2,1)S(1)}, u32[]{:S(2)}, u32[]{:S(2)}) %collective-permute-start.10) | collective-permute-done | bytes 90144 | tf_op jit(solution)/shard_map/ppermute | solution.py:358
  38.1 1.4 %collective-permute-done.13.other_ref = bf16[608,128]{1,0:T(8,128)(2,1)S(1)} collective-permute-done((bf16[608,128]{1,0:T(8,128)(2,1)S(1)}, bf16[608,128]{1,0:T(8,128)(2,1)S(1)}, u32[]{:S(2)}, u32[]{:S(2)}) %collective-permute-start.13) | collective-permute-done | bytes 155680 | tf_op jit(solution)/shard_map/ppermute | solution.py:358
  39.5 1.4 %shard_map.158 = (f32[1024,128]{1,0:T(8,128)}, f32[128,128]{1,0:T(8,128)}, f32[32,64]{1,0:T(8,128)}, f32[32,64]{1,0:T(8,128)}) custom-call(bf16[608,128]{1,0:T(8,128)(2,1)S(1)} %shard_map.157.local_ref, bf16[608,128]{1,0:T(8,128)(2,1)S(1)} %collective-permute-done.13.other_ref), custom_call_target="tpu_custom_call" | custom-call | flops 1048576 | bytes 1048576 | tf_op jit(solution)/shard_map/pallas_call | solution.py:418
  (39 shorter events, 0.8 us)
Async XLA Ops:
  0.6 4.2 %copy-start.3 = (bf16[8,128,128]{2,1,0:T(8,128)(2,1)S(1)}, bf16[8,128,128]{2,1,0:T(8,128)(2,1)}, u32[]{:S(2)}) copy-start(bf16[8,128,128]{2,1,0:T(8,128)(2,1)} %cot_ref.1) | copy-start | bytes 786436
  0.6 4.2 %copy-start.5 = (bf16[8,128,128]{2,1,0:T(8,128)(2,1)S(1)}, bf16[8,128,128]{2,1,0:T(8,128)(2,1)}, u32[]{:S(2)}) copy-start(bf16[8,128,128]{2,1,0:T(8,128)(2,1)} %pair_ref.3) | copy-start | bytes 786436
  0.7 4.2 %copy-start.6 = (bf16[128,128]{1,0:T(8,128)(2,1)S(1)}, bf16[128,128]{1,0:T(8,128)(2,1)}, u32[]{:S(2)}) copy-start(bf16[128,128]{1,0:T(8,128)(2,1)} %gate_ref.1) | copy-start | bytes 98308
  0.7 6.6 %collective-permute-start = (bf16[2,64,128]{2,1,0:T(8,128)(2,1)}, bf16[2,64,128]{2,1,0:T(8,128)(2,1)S(1)}, u32[]{:S(2)}, u32[]{:S(2)}) collective-permute-start(bf16[2,64,128]{2,1,0:T(8,128)(2,1)} %bitcast.9), channel_id=1, source_target_pairs={{0,8},{1,9},{2,10},{3,11},{4,12},{5,13},{6,14},{7,15},{8,0},{9,1},... | collective-permute-start | bytes 98312 | tf_op jit(solution)/shard_map/ppermute | solution.py:358
  4.8 0.7 %copy-start.1 = (s32[128]{0:T(128)S(1)}, s32[128]{0:T(128)}, u32[]{:S(2)}) copy-start(s32[128]{0:T(128)} %res_s_ref.1) | copy-start | bytes 1540
  4.8 0.7 %copy-start.2 = (s32[32]{0:T(128)S(1)}, s32[32]{0:T(128)}, u32[]{:S(2)}) copy-start(s32[32]{0:T(128)} %seq_ref.1) | copy-start | bytes 388
  4.8 0.7 %copy-start.9 = (f32[64]{0:T(128)S(1)}, f32[64]{0:T(128)}, u32[]{:S(2)}) copy-start(f32[64]{0:T(128)} %param.16) | copy-start | bytes 772
  5.5 1.8 %copy-start = (bf16[2,128,64]{1,2,0:T(8,128)(2,1)S(1)}, bf16[2,128,64]{1,2,0:T(8,128)(2,1)}, u32[]{:S(2)}) copy-start(bf16[2,128,64]{1,2,0:T(8,128)(2,1)} %param.11) | copy-start | bytes 98308
  5.5 6.0 %copy-start.8 = (bf16[64,32]{0,1:T(8,128)(2,1)S(1)}, bf16[64,32]{0,1:T(8,128)(2,1)}, u32[]{:S(2)}) copy-start(bf16[64,32]{0,1:T(8,128)(2,1)} %param.17) | copy-start | bytes 12292
  6.8 4.7 %copy-start.4 = (bf16[1024,128]{1,0:T(8,128)(2,1)S(1)}, bf16[1024,128]{1,0:T(8,128)(2,1)}, u32[]{:S(2)}) copy-start(bf16[1024,128]{1,0:T(8,128)(2,1)} %out_w_ref.1) | copy-start | bytes 786436
  7.9 3.6 %copy-start.7 = (bf16[64,32]{0,1:T(8,128)(2,1)S(1)}, bf16[64,32]{0,1:T(8,128)(2,1)}, u32[]{:S(2)}) copy-start(bf16[64,32]{0,1:T(8,128)(2,1)} %param.18) | copy-start | bytes 12292
  7.9 8.4 %collective-permute-start.3 = (bf16[768,128]{1,0:T(8,128)(2,1)S(1)}, bf16[768,128]{1,0:T(8,128)(2,1)S(1)}, u32[]{:S(2)}, u32[]{:S(2)}) collective-permute-start(bf16[768,128]{1,0:T(8,128)(2,1)S(1)} %get-tuple-element.41), channel_id=1, source_target_pairs={{0,4},{1,5},{2,6},{3,7},{4,0},{5,1},{6,2},{7,3},{8,12},{9,13},{10,... | collective-permute-start | bytes 589832 | tf_op jit(solution)/shard_map/ppermute | solution.py:358
  9.5 5.0 %collective-permute-start.6 = (bf16[256,128]{1,0:T(8,128)(2,1)S(1)}, bf16[256,128]{1,0:T(8,128)(2,1)S(1)}, u32[]{:S(2)}, u32[]{:S(2)}) collective-permute-start(bf16[256,128]{1,0:T(8,128)(2,1)S(1)} %get-tuple-element.40.after_ref.y0_ref), channel_id=1, source_target_pairs={{0,2},{1,3},{2,0},{3,1},{4,6},{5,7},{6,4},{7,5},{8,10},{9,11},{10,... | collective-permute-start | bytes 196616 | tf_op jit(solution)/shard_map/ppermute | solution.py:358
  11.0 5.3 %collective-permute-start.1 = (bf16[256,128]{1,0:T(8,128)(2,1)S(1)}, bf16[256,128]{1,0:T(8,128)(2,1)S(1)}, u32[]{:S(2)}, u32[]{:S(2)}) collective-permute-start(bf16[256,128]{1,0:T(8,128)(2,1)S(1)} %get-tuple-element.40.after_ref.y0_ref), channel_id=1, source_target_pairs={{0,6},{1,7},{2,4},{3,5},{4,2},{5,3},{6,0},{7,1},{8,14},{9,15},{10,... | collective-permute-start | bytes 196616 | tf_op jit(solution)/shard_map/ppermute | solution.py:358
  11.5 5.3 %collective-permute-start.5 = (bf16[512,128]{1,0:T(8,128)(2,1)S(1)}, bf16[512,128]{1,0:T(8,128)(2,1)S(1)}, u32[]{:S(2)}, u32[]{:S(2)}) collective-permute-start(bf16[512,128]{1,0:T(8,128)(2,1)S(1)} %get-tuple-element.46), channel_id=1, source_target_pairs={{0,1},{1,0},{2,3},{3,2},{4,5},{5,4},{6,7},{7,6},{8,9},{9,8},{10,11... | collective-permute-start | bytes 393224 | tf_op jit(solution)/shard_map/ppermute | solution.py:358
  14.5 2.3 %collective-permute-start.7 = (bf16[256,128]{1,0:T(8,128)(2,1)S(1)}, bf16[256,128]{1,0:T(8,128)(2,1)S(1)}, u32[]{:S(2)}, u32[]{:S(2)}) collective-permute-start(bf16[256,128]{1,0:T(8,128)(2,1)S(1)} %shard_map.150.y2_ref), channel_id=1, source_target_pairs={{0,1},{1,0},{2,3},{3,2},{4,5},{5,4},{6,7},{7,6},{8,9},{9,8},{10,11... | collective-permute-start | bytes 196616 | tf_op jit(solution)/shard_map/ppermute | solution.py:358
  16.3 2.6 %collective-permute-start.2 = (bf16[256,128]{1,0:T(8,128)(2,1)S(1)}, bf16[256,128]{1,0:T(8,128)(2,1)S(1)}, u32[]{:S(2)}, u32[]{:S(2)}) collective-permute-start(bf16[256,128]{1,0:T(8,128)(2,1)S(1)} %collective-permute-done.1.y0_ref), channel_id=1, source_target_pairs={{0,1},{1,0},{2,3},{3,2},{4,5},{5,4},{6,7},{7,6},{8,9},{9,8},{10,11... | collective-permute-start | bytes 196616 | tf_op jit(solution)/shard_map/ppermute | solution.py:358
  16.3 2.6 %collective-permute-start.4 = (bf16[768,128]{1,0:T(8,128)(2,1)S(1)}, bf16[768,128]{1,0:T(8,128)(2,1)S(1)}, u32[]{:S(2)}, u32[]{:S(2)}) collective-permute-start(bf16[768,128]{1,0:T(8,128)(2,1)S(1)} %collective-permute-done.3.y2_ref.across_ref), channel_id=1, source_target_pairs={{0,1},{1,0},{2,3},{3,2},{4,5},{5,4},{6,7},{7,6},{8,9},{9,8},{10,11... | collective-permute-start | bytes 589832 | tf_op jit(solution)/shard_map/ppermute | solution.py:358
  20.9 1.8 %collective-permute-start.8 = (bf16[64,128]{1,0:T(8,128)(2,1)S(1)}, bf16[64,128]{1,0:T(8,128)(2,1)S(1)}, u32[]{:S(2)}, u32[]{:S(2)}) collective-permute-start(bf16[64,128]{1,0:T(8,128)(2,1)S(1)} %get-tuple-element.60), channel_id=1, source_target_pairs={{0,1},{1,0},{2,3},{3,2},{4,5},{5,4},{6,7},{7,6},{8,9},{9,8},{10,11... | collective-permute-start | bytes 49160 | tf_op jit(solution)/shard_map/ppermute | solution.py:358
  22.7 8.0 %collective-permute-start.9 = (bf16[352,128]{1,0:T(8,128)(2,1)S(1)}, bf16[352,128]{1,0:T(8,128)(2,1)S(1)}, u32[]{:S(2)}, u32[]{:S(2)}) collective-permute-start(bf16[352,128]{1,0:T(8,128)(2,1)S(1)} %shard_map.154.after_ref.own_ref), channel_id=1, source_target_pairs={{0,8},{1,9},{2,10},{3,11},{4,12},{5,13},{6,14},{7,15},{8,0},{9,1},... | collective-permute-start | bytes 270344 | tf_op jit(solution)/shard_map/ppermute | solution.py:358
  30.7 6.3 %collective-permute-start.12 = (bf16[352,128]{1,0:T(8,128)(2,1)S(1)}, bf16[352,128]{1,0:T(8,128)(2,1)S(1)}, u32[]{:S(2)}, u32[]{:S(2)}) collective-permute-start(bf16[352,128]{1,0:T(8,128)(2,1)S(1)} %shard_map.156.own_ref), channel_id=1, source_target_pairs={{0,6},{1,7},{2,4},{3,5},{4,2},{5,3},{6,0},{7,1},{8,14},{9,15},{10,... | collective-permute-start | bytes 270344 | tf_op jit(solution)/shard_map/ppermute | solution.py:358
  31.2 5.8 %collective-permute-start.11 = (bf16[352,128]{1,0:T(8,128)(2,1)S(1)}, bf16[352,128]{1,0:T(8,128)(2,1)S(1)}, u32[]{:S(2)}, u32[]{:S(2)}) collective-permute-start(bf16[352,128]{1,0:T(8,128)(2,1)S(1)} %shard_map.156.own_ref), channel_id=1, source_target_pairs={{0,4},{1,5},{2,6},{3,7},{4,0},{5,1},{6,2},{7,3},{8,12},{9,13},{10,... | collective-permute-start | bytes 270344 | tf_op jit(solution)/shard_map/ppermute | solution.py:358
  32.8 5.2 %collective-permute-start.10 = (bf16[352,128]{1,0:T(8,128)(2,1)S(1)}, bf16[352,128]{1,0:T(8,128)(2,1)S(1)}, u32[]{:S(2)}, u32[]{:S(2)}) collective-permute-start(bf16[352,128]{1,0:T(8,128)(2,1)S(1)} %shard_map.156.own_ref), channel_id=1, source_target_pairs={{0,2},{1,3},{2,0},{3,1},{4,6},{5,7},{6,4},{7,5},{8,10},{9,11},{10,... | collective-permute-start | bytes 270344 | tf_op jit(solution)/shard_map/ppermute | solution.py:358
  38.0 1.4 %collective-permute-start.13 = (bf16[608,128]{1,0:T(8,128)(2,1)S(1)}, bf16[608,128]{1,0:T(8,128)(2,1)S(1)}, u32[]{:S(2)}, u32[]{:S(2)}) collective-permute-start(bf16[608,128]{1,0:T(8,128)(2,1)S(1)} %shard_map.157.local_ref), channel_id=1, source_target_pairs={{0,1},{1,0},{2,3},{3,2},{4,5},{5,4},{6,7},{7,6},{8,9},{9,8},{10,11... | collective-permute-start | bytes 466952 | tf_op jit(solution)/shard_map/ppermute | solution.py:358
  (1 other events, 0.7 us)
